TPU v7x, 128 devices: a whole 4x4x4 slice. The times are simulated.
128 devices in a mesh: pix: 8 (over x, z_hi), chan: 16 (over z_lo, y, core).
Axes of the slice: x: 4, y: 4, z: 4 (z_hi: 2, z_lo: 2; z = z_hi * 2 + z_lo), core: 2. Of those that a mesh axis runs over, the one named last changes fastest.
Arguments:
- data_cube: float32 [256, 128, 512], P('chan', 'pix'), may hold values from -2000 to 2000
- blanked: int32 [128, 512], P('pix'), may hold values 0 or 1
Outputs:
- snr_cubes: float32 [4, 256, 128, 512], P(None, 'chan', 'pix')
All inputs are finite; a program needn't handle non-finite values. No bound on the sum of `blanked` on one device may be relied on, other than what follows from the above.
Results may differ from a plain program's by a relative error of at most 0.0003.
Values sent between devices are 32-bit elements; how exact they have to be, the bound alone decides.
No kernel may reach another device: no remote copies, remote signals or barrier semaphores. Data moves between devices by JAX's collectives and lax.ppermute only.
A program may use at most 64 MiB of HBM per device.

v0:
```python
import math

import jax
import jax.numpy as jnp
from jax import lax
from jax.experimental import pallas as pl
from jax.experimental.pallas import tpu as pltpu
from jax.sharding import PartitionSpec as P

SIGMA = 3.0 / (2.0 * math.sqrt(2.0 * math.log(2.0)))
VOLUME = 14415.0
WIDTHS = (1, 3, 7, 15)
HALO = 14
LANES = 128
ANY = pl.BlockSpec(memory_space=pl.ANY)
VMEM = pl.BlockSpec(memory_space=pltpu.VMEM)


def kernel_taps():
    weights = [math.exp(-0.5 * (offset / SIGMA) ** 2) for offset in range(-3, 4)]
    total = sum(weights)
    return [weight / total for weight in weights]


def call(body, outs, scratch=(), vmem=16, micros=1.0, **specs):
    return pl.pallas_call(
        body,
        out_shape=outs,
        scratch_shapes=list(scratch),
        compiler_params=pltpu.CompilerParams(vmem_limit_bytes=vmem * 1024 * 1024),
        cost_estimate=pl.CostEstimate(
            flops=0, bytes_accessed=int(micros * 3.0e6), transcendentals=0
        ),
        **specs,
    )


def f32(*shape):
    return jax.ShapeDtypeStruct(shape, jnp.float32)


def odd_of(axis):
    return lax.axis_index(axis) % 2


def clean_cols_kernel(data, blanked, cells, edge, edge2):
    taps = kernel_taps()
    chans, rows, cols = data.shape
    even = odd_of("pix") == 0
    kept = (1 - blanked[...]).astype(jnp.float32)
    lane = lax.broadcasted_iota(jnp.int32, (rows, cols), 1)
    for c in range(chans):
        x = data[c] * kept
        acc = taps[3] * x
        for t in (1, 2, 3):
            left = jnp.where(lane >= t, pltpu.roll(x, t, 1), 0.0)
            right = jnp.where(lane < cols - t, pltpu.roll(x, cols - t, 1), 0.0)
            acc = acc + taps[3 + t] * (left + right)
        cells[c] = acc
    for r in range(3):
        top = cells[:, r, :]
        bottom = cells[:, rows - 3 + r, :]
        edge[r] = jnp.where(even, top, bottom)
        edge2[r] = jnp.where(even, bottom, top)


def smooth_rows(field, c, base, rows):
    taps = kernel_taps()
    acc = taps[3] * field[c, pl.ds(base, rows), :]
    for t in (1, 2, 3):
        acc = acc + taps[3 + t] * (
            field[c, pl.ds(base - t, rows), :] + field[c, pl.ds(base + t, rows), :]
        )
    return acc


def send_halos(full, link, core):
    chans = full.shape[0]
    odd = odd_of("chan")
    link[...] = full[pl.ds((chans - HALO) * odd, HALO)]
    core[...] = full[pl.ds((chans - HALO) * (1 - odd), HALO)]


def pair_rows_kernel(cells, near, edge_far, edge_near, full, link, core, field):
    chans, rows, cols = cells.shape
    odd = odd_of("pix")
    even = odd == 0
    field[:, pl.ds(pl.multiple_of(8 + rows * odd, 8), rows), :] = cells[...]
    field[:, pl.ds(pl.multiple_of(8 + rows * (1 - odd), 8), rows), :] = near[...]
    for r in range(3):
        field[:, 5 + r, :] = jnp.where(even, edge_far[r], edge_near[r])
        field[:, 40 + r, :] = jnp.where(even, edge_near[r], edge_far[r])

    def channel(c, carry):
        for part in range(2):
            full[c, pl.ds(rows * part, rows), :] = smooth_rows(field, c, 8 + rows * part, rows)
        return carry

    lax.fori_loop(0, chans, channel, 0)
    send_halos(full, link, core)


def far_rows_kernel(far, edge, beyond, full, link, core, field):
    chans, rows, cols = far.shape
    at, count = lax.axis_index("pix"), lax.axis_size("pix")
    even = odd_of("pix") == 0
    present = jnp.logical_and(at > 0, at < count - 1).astype(jnp.float32)
    field[:, 8:24, :] = far[...]
    for r in range(3):
        field[:, 5 + r, :] = jnp.where(even, beyond[r], edge[r])
        field[:, 24 + r, :] = jnp.where(even, edge[r], beyond[r])

    def channel(c, carry):
        full[c] = smooth_rows(field, c, 8, rows) * present
        return carry

    lax.fori_loop(0, chans, channel, 0)
    send_halos(full, link, core)


def gather_channels(link, core, field):
    odd = odd_of("chan")
    field[pl.ds(30 * odd, HALO)] = link[...]
    field[pl.ds(30 * (1 - odd), HALO)] = core[...]


def channel_sums(field, own, row, tile, energy, boxes, kept_at):
    chans, tall = own.shape[:2]
    at, count = lax.axis_index("chan"), lax.axis_size("chan")
    has_below = (at > 0).astype(jnp.float32)
    has_above = (at < count - 1).astype(jnp.float32)
    here = (pl.ds(pl.multiple_of(row, 8), 8), pl.ds(tile * LANES, LANES))

    def s(j):
        if HALO <= j < HALO + chans:
            return own[(j - HALO,) + here]
        return field[(j,) + here]

    def put(w, c, value):
        energy[w, tile, pl.ds(pl.multiple_of(c * tall + row, 8), 8), :] = value

    def get(w, c):
        return energy[w, tile, pl.ds(pl.multiple_of(c * tall + row, 8), 8), :]

    for step, first in ((-1, 28), (1, 15)):
        one, three, seven = {}, {}, {}
        runs = [None] * 4
        for n in range(29):
            j = first + step * n
            one[j] = s(j)
            a = j - step
            if n >= 2:
                three[a] = one[a - 1] + one[a] + one[a + 1]
            b = j - 3 * step
            if n >= 6:
                seven[b] = three[b - 2] + three[b + 2] + one[b]
            if n < 14:
                continue
            j -= 7 * step
            fifteen = seven[j - 4] + seven[j + 4] + one[j]
            k = j - 7
            for w, box in enumerate((one[j], three[j], seven[j], fifteen)):
                if kept_at is not None and 7 <= k < 23:
                    rows_at = pl.ds(pl.multiple_of(kept_at, 8), 8)
                    boxes[w, k - 7, rows_at, here[1]] = box
                square = box * box
                if k < 7:
                    square = square * has_below
                if k >= 23:
                    square = square * has_above
                runs[w] = square if runs[w] is None else runs[w] + square
                if step < 0:
                    put(w, k, runs[w])
                elif k < 29:
                    put(w, k - 14, get(w, k - 14) + runs[w])
                else:
                    put(w, k - 14, runs[w])


def two_terms(sums, w):
    value = jnp.concatenate([sums[w, tile] for tile in range(sums.shape[1])], axis=1)
    first = value.astype(jnp.bfloat16)
    second = (value - first.astype(jnp.float32)).astype(jnp.bfloat16)
    return jnp.concatenate([first, second], axis=1)


def column_windows(sums, w, band):
    both = jnp.concatenate([band, band], axis=0)
    return jnp.dot(two_terms(sums, w), both, preferred_element_type=jnp.float32)


def pair_noise_kernel(own, link, core, after, boxes, window, band, field, energy, sums):
    chans, tall, cols = own.shape
    rows = tall // 2
    odd = odd_of("pix")
    gather_channels(link, core, field)
    for tile in range(cols // LANES):

        def strips(i, carry):
            channel_sums(field, own, 8 * i + rows * odd, tile, energy, boxes, 8 * i)
            channel_sums(field, own, 8 * i + rows * (1 - odd), tile, energy, None, None)
            return carry

        lax.fori_loop(0, 2, strips, 0)

    def row_windows(step, carry):
        w, half = step // 2, step % 2
        for tile in range(cols // LANES):

            def e(i):
                return energy[w, tile, pl.ds(half * 8 * tall + i, 8, stride=tall), :]

            run = e(rows * odd)
            for i in range(1, rows):
                run = run + e(rows * odd + i)
            for d in range(rows):
                if d > 0:
                    run = run + e(jnp.where(odd == 0, 15 + d, 16 - d))
                row = jnp.where(odd == 0, d, 15 - d)
                sums[w, tile, pl.ds(half * 8 * rows + row, 8, stride=rows), :] = run
        return carry

    lax.fori_loop(0, 8, row_windows, 0)
    apart = lax.broadcasted_iota(jnp.int32, (cols, cols), 0) - lax.broadcasted_iota(
        jnp.int32, (cols, cols), 1
    )
    band[...] = (jnp.abs(apart) <= 15).astype(jnp.float32).astype(jnp.bfloat16)
    for w in range(4):
        window[w] = column_windows(sums, w, band[...])


def snr_kernel(
    own, link, core, window, band, boxes, blanked, out, field, energy, sums, ready, sems
):
    chans, rows, cols = own.shape
    odd = odd_of("pix")
    gather_channels(link, core, field)
    for tile in range(cols // LANES):

        def strips(i, carry):
            channel_sums(field, own, 8 * i, tile, energy, None, None)
            return carry

        lax.fori_loop(0, 2, strips, 0)

    def row_windows(step, carry):
        w, half = step // 2, step % 2
        for tile in range(cols // LANES):
            run = jnp.zeros((8, LANES), jnp.float32)
            for d in range(rows):
                if d > 0:
                    i = jnp.where(odd == 0, 16 - d, d - 1)
                    run = run + energy[w, tile, pl.ds(half * 8 * rows + i, 8, stride=rows), :]
                row = jnp.where(odd == 0, 15 - d, d)
                sums[w, tile, pl.ds(half * 8 * rows + row, 8, stride=rows), :] = run
        return carry

    lax.fori_loop(0, 8, row_windows, 0)
    kept = (1 - blanked[...]).astype(jnp.float32)
    copies = []
    for w, width in enumerate(WIDTHS):
        total = window[w] + column_windows(sums, w, band[...])
        scale = lax.rsqrt(total * (1.0 / (VOLUME * width * width)) + 1e-5) * (1.0 / width)
        ready[w] = boxes[w] * scale.reshape(chans, rows, cols) * kept[None]
        copies.append(pltpu.make_async_copy(ready.at[w], out.at[w], sems.at[w]))
        copies[-1].start()
    for copy in copies:
        copy.wait()


def per_device(data_cube, blanked):
    chans, rows, cols = data_cube.shape
    pix = lax.axis_size("pix")
    tiles = cols // LANES

    def move(value, axis, pairs):
        count = lax.axis_size(axis)
        return lax.ppermute(value, axis, [(a, b) for a, b in pairs if 0 <= b < count])

    def swap(value, axis, first):
        count = lax.axis_size(axis)
        pairs = [(i, i + 1 if (i - first) % 2 == 0 else i - 1) for i in range(count)]
        return move(value, axis, pairs)

    toward = [(i, i + 2 if i % 2 == 0 else i - 2) for i in range(pix)]
    back = [(i, i - 2 if i % 2 == 0 else i + 2) for i in range(pix)]
    cells, edge, edge2 = call(
        clean_cols_kernel, [f32(chans, rows, cols), f32(3, chans, cols), f32(3, chans, cols)]
    )(data_cube, blanked)
    near = swap(cells, "pix", 0)
    edge_near = move(edge, "pix", back)
    edge_far = swap(edge, "pix", 1)
    beyond = move(edge2, "pix", toward)
    near = call(
        lambda value, *rest: None,
        f32(*near.shape),
        in_specs=[ANY] * 4,
        out_specs=ANY,
        input_output_aliases={0: 0},
    )(near, edge_near, edge_far, beyond)
    far = move(near, "pix", toward)

    pair, pair_link, pair_core = call(
        pair_rows_kernel,
        [f32(chans, 32, cols), f32(HALO, 32, cols), f32(HALO, 32, cols)],
        [pltpu.VMEM((chans, 48, cols), jnp.float32)],
    )(cells, near, edge_far, edge_near)
    pair_link = swap(pair_link, "chan", 1)
    pair_core = swap(pair_core, "chan", 0)

    outer, outer_link, outer_core = call(
        far_rows_kernel,
        [f32(chans, 16, cols), f32(HALO, 16, cols), f32(HALO, 16, cols)],
        [pltpu.VMEM((chans, 32, cols), jnp.float32)],
    )(far, edge, beyond)
    outer_link = swap(outer_link, "chan", 1)
    outer_core = swap(outer_core, "chan", 0)

    boxes, window, band = call(
        pair_noise_kernel,
        [
            f32(4, chans, rows, cols),
            f32(4, chans * rows, cols),
            jax.ShapeDtypeStruct((cols, cols), jnp.bfloat16),
        ],
        [
            pltpu.VMEM((44, 32, cols), jnp.float32),
            pltpu.VMEM((4, tiles, chans * 32, LANES), jnp.float32),
            pltpu.VMEM((4, tiles, chans * rows, LANES), jnp.float32),
        ],
        vmem=24,
        micros=4.0,
        in_specs=[VMEM, VMEM, VMEM, ANY],
    )(pair, pair_link, pair_core, outer)
    return call(
        snr_kernel,
        f32(4, chans, rows, cols),
        [
            pltpu.VMEM((44, 16, cols), jnp.float32),
            pltpu.VMEM((4, tiles, chans * rows, LANES), jnp.float32),
            pltpu.VMEM((4, tiles, chans * rows, LANES), jnp.float32),
            pltpu.VMEM((4, chans, rows, cols), jnp.float32),
            pltpu.SemaphoreType.DMA((4,)),
        ],
        vmem=24,
        micros=4.0,
        out_specs=ANY,
    )(outer, outer_link, outer_core, window, band, boxes, blanked)


def solution(mesh):
    return jax.shard_map(
        per_device,
        mesh=mesh,
        in_specs=(P("chan", "pix", None), P("pix", None)),
        out_specs=P(None, "chan", "pix", None),
        check_vma=False,
    )
```

profile of v0, /device:TPU:34, one launch (start us, length us, event | category | flops | bytes accessed | tf_op | source)
XLA Modules:
  0.0 52.5 jit_solution(15762174216650870426)
XLA Ops:
  0.0 0.0 copy-start
  0.0 1.0 %copy-done = f32[16,16,512]{2,1,0:T(8,128)S(1)} copy-done((f32[16,16,512]{2,1,0:T(8,128)S(1)}, f32[16,16,512]{2,1,0:T(8,128)}, u32[]{:S(2)}) %copy-start) | copy-done | bytes 524312
  1.0 0.0 copy-start.1
  1.0 0.8 %copy-done.1 = s32[16,512]{1,0:T(8,128)S(1)} copy-done((s32[16,512]{1,0:T(8,128)S(1)}, s32[16,512]{1,0:T(8,128)}, u32[]{:S(2)}) %copy-start.1) | copy-done | bytes 32792
  1.8 0.9 %shard_map.28 = (f32[16,16,512]{2,1,0:T(8,128)S(1)}, f32[3,16,512]{2,1,0:T(8,128)S(1)}, f32[3,16,512]{2,1,0:T(8,128)S(1)}) custom-call(f32[16,16,512]{2,1,0:T(8,128)S(1)} %copy-done, s32[16,512]{1,0:T(8,128)S(1)} %copy-done.1), custom_call_target="tpu_custom_call" | custom-call | bytes 3000000 | tf_op jit(solution)/shard_map/pallas_call | solution.py:287
  2.7 3.1 %collective-permute-start = (f32[16,16,512]{2,1,0:T(8,128)S(1)}, f32[16,16,512]{2,1,0:T(8,128)S(1)}, u32[]{:S(2)}, u32[]{:S(2)}) collective-permute-start(f32[16,16,512]{2,1,0:T(8,128)S(1)} %get-tuple-element.17.cells), channel_id=1, source_target_pairs={{0,16},{16,0},{32,48},{48,32},{64,80},{80,64},{96,112},{112,96},{1... | collective-permute-start | bytes 1572872 | tf_op jit(solution)/shard_map/ppermute | solution.py:278
  5.8 3.4 %collective-permute-start.3 = (f32[3,16,512]{2,1,0:T(8,128)S(1)}, f32[3,16,512]{2,1,0:T(8,128)S(1)}, u32[]{:S(2)}, u32[]{:S(2)}) collective-permute-start(f32[3,16,512]{2,1,0:T(8,128)S(1)} %get-tuple-element.19), channel_id=1, source_target_pairs={{0,32},{32,64},{48,16},{64,96},{80,48},{112,80},{1,33},{33,65},{49... | collective-permute-start | bytes 294920 | tf_op jit(solution)/shard_map/ppermute | solution.py:278
  9.2 1.9 %collective-permute-start.2 = (f32[3,16,512]{2,1,0:T(8,128)S(1)}, f32[3,16,512]{2,1,0:T(8,128)S(1)}, u32[]{:S(2)}, u32[]{:S(2)}) collective-permute-start(f32[3,16,512]{2,1,0:T(8,128)S(1)} %get-tuple-element.18.edge), channel_id=1, source_target_pairs={{16,32},{32,16},{48,64},{64,48},{80,96},{96,80},{17,33},{33,17},{4... | collective-permute-start | bytes 294920 | tf_op jit(solution)/shard_map/ppermute | solution.py:278
  11.1 1.9 %collective-permute-start.1 = (f32[3,16,512]{2,1,0:T(8,128)S(1)}, f32[3,16,512]{2,1,0:T(8,128)S(1)}, u32[]{:S(2)}, u32[]{:S(2)}) collective-permute-start(f32[3,16,512]{2,1,0:T(8,128)S(1)} %get-tuple-element.18.edge), channel_id=1, source_target_pairs={{16,48},{32,0},{48,80},{64,32},{80,112},{96,64},{17,49},{33,1},{49... | collective-permute-start | bytes 294920 | tf_op jit(solution)/shard_map/ppermute | solution.py:278
  13.0 0.0 collective-permute-done.3.rest_2_.beyond
  13.0 5.1 %collective-permute-done.2.rest_1_.edge_far = f32[3,16,512]{2,1,0:T(8,128)S(1)} collective-permute-done((f32[3,16,512]{2,1,0:T(8,128)S(1)}, f32[3,16,512]{2,1,0:T(8,128)S(1)}, u32[]{:S(2)}, u32[]{:S(2)}) %collective-permute-start.2) | collective-permute-done | bytes 98336 | tf_op jit(solution)/shard_map/ppermute | solution.py:278
  18.2 0.0 collective-permute-done.1.rest_0_.edge_near
  18.2 1.9 %collective-permute-done.value = f32[16,16,512]{2,1,0:T(8,128)S(1)} collective-permute-done((f32[16,16,512]{2,1,0:T(8,128)S(1)}, f32[16,16,512]{2,1,0:T(8,128)S(1)}, u32[]{:S(2)}, u32[]{:S(2)}) %collective-permute-start) | collective-permute-done | bytes 524320 | tf_op jit(solution)/shard_map/ppermute | solution.py:278
  20.1 3.4 %collective-permute-start.4 = (f32[16,16,512]{2,1,0:T(8,128)S(1)}, f32[16,16,512]{2,1,0:T(8,128)S(1)}, u32[]{:S(2)}, u32[]{:S(2)}) collective-permute-start(f32[16,16,512]{2,1,0:T(8,128)S(1)} %shard_map.29.near), channel_id=1, source_target_pairs={{0,32},{32,64},{48,16},{64,96},{80,48},{112,80},{1,33},{33,65},{49... | collective-permute-start | bytes 1572872 | tf_op jit(solution)/shard_map/ppermute | solution.py:278
  23.5 1.4 %shard_map.31 = (f32[16,32,512]{2,1,0:T(8,128)S(1)}, f32[14,32,512]{2,1,0:T(8,128)S(1)}, f32[14,32,512]{2,1,0:T(8,128)S(1)}) custom-call(f32[16,16,512]{2,1,0:T(8,128)S(1)} %get-tuple-element.17.cells, f32[16,16,512]{2,1,0:T(8,128)S(1)} %shard_map.29.near, f32[3,16,512]{2,1,0:T(8,128)S(1)} %collective-permute-done.2.rest_1_.edge_far, ...), custom_call_target="tpu_custom_call" | custom-call | bytes 3000000 | tf_op jit(solution)/shard_map/pallas_call | solution.py:303
  24.8 0.0 copy-start.2
  24.8 3.7 %collective-permute-start.7 = (f32[14,32,512]{2,1,0:T(8,128)S(1)}, f32[14,32,512]{2,1,0:T(8,128)S(1)}, u32[]{:S(2)}, u32[]{:S(2)}) collective-permute-start(f32[14,32,512]{2,1,0:T(8,128)S(1)} %get-tuple-element.24), channel_id=1, source_target_pairs={{1,2},{2,1},{3,4},{4,3},{5,6},{6,5},{7,8},{8,7},{9,10},{10,9},{11,... | collective-permute-start | bytes 2752520 | tf_op jit(solution)/shard_map/ppermute | solution.py:278
  28.6 0.1 collective-permute-start.8
  28.6 6.1 %collective-permute-done.4.far = f32[16,16,512]{2,1,0:T(8,128)S(1)} collective-permute-done((f32[16,16,512]{2,1,0:T(8,128)S(1)}, f32[16,16,512]{2,1,0:T(8,128)S(1)}, u32[]{:S(2)}, u32[]{:S(2)}) %collective-permute-start.4) | collective-permute-done | bytes 524320 | tf_op jit(solution)/shard_map/ppermute | solution.py:278
  34.7 0.8 %shard_map.30 = (f32[16,16,512]{2,1,0:T(8,128)S(1)}, f32[14,16,512]{2,1,0:T(8,128)S(1)}, f32[14,16,512]{2,1,0:T(8,128)S(1)}) custom-call(f32[16,16,512]{2,1,0:T(8,128)S(1)} %collective-permute-done.4.far, f32[3,16,512]{2,1,0:T(8,128)S(1)} %get-tuple-element.18.edge, f32[3,16,512]{2,1,0:T(8,128)S(1)} %collective-permute-done.3.rest_2_.beyond), custom_call_target="tpu_custom_call" | custom-call | bytes 3000000 | tf_op jit(solution)/shard_map/pallas_call | solution.py:311
  35.6 3.4 %collective-permute-start.5 = (f32[14,16,512]{2,1,0:T(8,128)S(1)}, f32[14,16,512]{2,1,0:T(8,128)S(1)}, u32[]{:S(2)}, u32[]{:S(2)}) collective-permute-start(f32[14,16,512]{2,1,0:T(8,128)S(1)} %get-tuple-element.21), channel_id=1, source_target_pairs={{1,2},{2,1},{3,4},{4,3},{5,6},{6,5},{7,8},{8,7},{9,10},{10,9},{11,... | collective-permute-start | bytes 1376264 | tf_op jit(solution)/shard_map/ppermute | solution.py:278
  38.9 0.3 collective-permute-start.6
  39.2 2.4 %collective-permute-done.7.link = f32[14,32,512]{2,1,0:T(8,128)S(1)} collective-permute-done((f32[14,32,512]{2,1,0:T(8,128)S(1)}, f32[14,32,512]{2,1,0:T(8,128)S(1)}, u32[]{:S(2)}, u32[]{:S(2)}) %collective-permute-start.7) | collective-permute-done | bytes 917536 | tf_op jit(solution)/shard_map/ppermute | solution.py:278
  41.7 0.0 collective-permute-done.8.core
  41.7 6.2 %shard_map.32 = (f32[4,16,16,512]{3,2,1,0:T(8,128)S(1)}, f32[4,256,512]{2,1,0:T(8,128)S(1)}, bf16[512,512]{1,0:T(8,128)(2,1)S(1)}) custom-call(f32[16,32,512]{2,1,0:T(8,128)S(1)} %get-tuple-element.23.own, f32[14,32,512]{2,1,0:T(8,128)S(1)} %collective-permute-done.7.link, f32[14,32,512]{2,1,0:T(8,128)S(1)} %collective-permute-done.8.core, ...), custom_call_target="tpu_custom_call" | custom-call | bytes 12000000 | tf_op jit(solution)/shard_map/pallas_call | solution.py:319
  47.8 0.0 collective-permute-done.5.link
  47.8 0.0 collective-permute-done.6.core
  47.8 0.0 copy-done.2
  47.9 4.6 %shard_map.33 = f32[4,16,16,512]{3,2,1,0:T(8,128)} custom-call(f32[16,16,512]{2,1,0:T(8,128)S(1)} %get-tuple-element.20.after.own, f32[14,16,512]{2,1,0:T(8,128)S(1)} %collective-permute-done.5.link, f32[14,16,512]{2,1,0:T(8,128)S(1)} %collective-permute-done.6.core, f32[4,256,512]{2,1,0:T(8,128)S(1)} %get-tuple-element.26.window, ...), custom_call_target="tpu_custom_call" | custom-call | bytes 12000000 | tf_op jit(solution)/shard_map/pallas_call | solution.py:335
  (1 shorter events, 0.0 us)
Async XLA Ops:
  0.0 1.0 %copy-start = (f32[16,16,512]{2,1,0:T(8,128)S(1)}, f32[16,16,512]{2,1,0:T(8,128)}, u32[]{:S(2)}) copy-start(f32[16,16,512]{2,1,0:T(8,128)} %data.1) | copy-start | bytes 1572868
  1.0 0.8 %copy-start.1 = (s32[16,512]{1,0:T(8,128)S(1)}, s32[16,512]{1,0:T(8,128)}, u32[]{:S(2)}) copy-start(s32[16,512]{1,0:T(8,128)} %blanked.3) | copy-start | bytes 98308
  2.7 17.4 %collective-permute-start = (f32[16,16,512]{2,1,0:T(8,128)S(1)}, f32[16,16,512]{2,1,0:T(8,128)S(1)}, u32[]{:S(2)}, u32[]{:S(2)}) collective-permute-start(f32[16,16,512]{2,1,0:T(8,128)S(1)} %get-tuple-element.17.cells), channel_id=1, source_target_pairs={{0,16},{16,0},{32,48},{48,32},{64,80},{80,64},{96,112},{112,96},{1... | collective-permute-start | bytes 1572872 | tf_op jit(solution)/shard_map/ppermute | solution.py:278
  5.8 7.3 %collective-permute-start.3 = (f32[3,16,512]{2,1,0:T(8,128)S(1)}, f32[3,16,512]{2,1,0:T(8,128)S(1)}, u32[]{:S(2)}, u32[]{:S(2)}) collective-permute-start(f32[3,16,512]{2,1,0:T(8,128)S(1)} %get-tuple-element.19), channel_id=1, source_target_pairs={{0,32},{32,64},{48,16},{64,96},{80,48},{112,80},{1,33},{33,65},{49... | collective-permute-start | bytes 294920 | tf_op jit(solution)/shard_map/ppermute | solution.py:278
  9.2 9.0 %collective-permute-start.2 = (f32[3,16,512]{2,1,0:T(8,128)S(1)}, f32[3,16,512]{2,1,0:T(8,128)S(1)}, u32[]{:S(2)}, u32[]{:S(2)}) collective-permute-start(f32[3,16,512]{2,1,0:T(8,128)S(1)} %get-tuple-element.18.edge), channel_id=1, source_target_pairs={{16,32},{32,16},{48,64},{64,48},{80,96},{96,80},{17,33},{33,17},{4... | collective-permute-start | bytes 294920 | tf_op jit(solution)/shard_map/ppermute | solution.py:278
  11.1 7.1 %collective-permute-start.1 = (f32[3,16,512]{2,1,0:T(8,128)S(1)}, f32[3,16,512]{2,1,0:T(8,128)S(1)}, u32[]{:S(2)}, u32[]{:S(2)}) collective-permute-start(f32[3,16,512]{2,1,0:T(8,128)S(1)} %get-tuple-element.18.edge), channel_id=1, source_target_pairs={{16,48},{32,0},{48,80},{64,32},{80,112},{96,64},{17,49},{33,1},{49... | collective-permute-start | bytes 294920 | tf_op jit(solution)/shard_map/ppermute | solution.py:278
  20.1 14.7 %collective-permute-start.4 = (f32[16,16,512]{2,1,0:T(8,128)S(1)}, f32[16,16,512]{2,1,0:T(8,128)S(1)}, u32[]{:S(2)}, u32[]{:S(2)}) collective-permute-start(f32[16,16,512]{2,1,0:T(8,128)S(1)} %shard_map.29.near), channel_id=1, source_target_pairs={{0,32},{32,64},{48,16},{64,96},{80,48},{112,80},{1,33},{33,65},{49... | collective-permute-start | bytes 1572872 | tf_op jit(solution)/shard_map/ppermute | solution.py:278
  24.8 23.0 %copy-start.2 = (s32[16,512]{1,0:T(8,128)S(1)}, s32[16,512]{1,0:T(8,128)}, u32[]{:S(2)}) copy-start(s32[16,512]{1,0:T(8,128)} %blanked.3) | copy-start | bytes 98308
  24.8 16.8 %collective-permute-start.7 = (f32[14,32,512]{2,1,0:T(8,128)S(1)}, f32[14,32,512]{2,1,0:T(8,128)S(1)}, u32[]{:S(2)}, u32[]{:S(2)}) collective-permute-start(f32[14,32,512]{2,1,0:T(8,128)S(1)} %get-tuple-element.24), channel_id=1, source_target_pairs={{1,2},{2,1},{3,4},{4,3},{5,6},{6,5},{7,8},{8,7},{9,10},{10,9},{11,... | collective-permute-start | bytes 2752520 | tf_op jit(solution)/shard_map/ppermute | solution.py:278
  28.6 13.1 %collective-permute-start.8 = (f32[14,32,512]{2,1,0:T(8,128)S(1)}, f32[14,32,512]{2,1,0:T(8,128)S(1)}, u32[]{:S(2)}, u32[]{:S(2)}) collective-permute-start(f32[14,32,512]{2,1,0:T(8,128)S(1)} %get-tuple-element.25), channel_id=1, source_target_pairs={{0,1},{1,0},{2,3},{3,2},{4,5},{5,4},{6,7},{7,6},{8,9},{9,8},{10,11... | collective-permute-start | bytes 2752520 | tf_op jit(solution)/shard_map/ppermute | solution.py:278
  35.6 12.3 %collective-permute-start.5 = (f32[14,16,512]{2,1,0:T(8,128)S(1)}, f32[14,16,512]{2,1,0:T(8,128)S(1)}, u32[]{:S(2)}, u32[]{:S(2)}) collective-permute-start(f32[14,16,512]{2,1,0:T(8,128)S(1)} %get-tuple-element.21), channel_id=1, source_target_pairs={{1,2},{2,1},{3,4},{4,3},{5,6},{6,5},{7,8},{8,7},{9,10},{10,9},{11,... | collective-permute-start | bytes 1376264 | tf_op jit(solution)/shard_map/ppermute | solution.py:278
  38.9 8.9 %collective-permute-start.6 = (f32[14,16,512]{2,1,0:T(8,128)S(1)}, f32[14,16,512]{2,1,0:T(8,128)S(1)}, u32[]{:S(2)}, u32[]{:S(2)}) collective-permute-start(f32[14,16,512]{2,1,0:T(8,128)S(1)} %get-tuple-element.22), channel_id=1, source_target_pairs={{0,1},{1,0},{2,3},{3,2},{4,5},{5,4},{6,7},{7,6},{8,9},{9,8},{10,11... | collective-permute-start | bytes 1376264 | tf_op jit(solution)/shard_map/ppermute | solution.py:278
where the time goes:
time: 52.9 us; the launch traced here: 52.5 us
  starting transfers between devices  21.1 us (40%)
  waiting for transfers between devices  15.6 us (29%)
  Pallas kernels  13.8 us (26%)
  local copies, waits for them, and re-layouts  1.8 us (3%)
    ppermute x9, starting transfers between devices, move(): lax.ppermute(value, axis, [(a, b) for a, b in pairs if 0 <= b < count])  21.1 us
    ppermute x9, waiting for transfers between devices, move(): lax.ppermute(value, axis, [(a, b) for a, b in pairs if 0 <= b < count])  15.6 us
    pallas_call x1, Pallas kernels, per_device(): call(pair_noise_kernel, [f32(4, chans, rows, cols), f32(4, chans * rows,...  6.16 us
    pallas_call x1, Pallas kernels, per_device(): call(snr_kernel, f32(4, chans, rows, cols), [pltpu.VMEM((44, 16, cols), j...  4.62 us
    unnamed x6, local copies, waits for them, and re-layouts  1.8 us
    pallas_call x1, Pallas kernels, per_device(): call(pair_rows_kernel, [f32(chans, 32, cols), f32(HALO, 32, cols), f32(HA...  1.35 us
  transfers between devices with their start and end apart: 9, of which 4 were waited for; matrix products, arithmetic and copies ran while one was open for 0% of the time, Pallas kernels for 16%

commit v1 on v0

--- a/solution.py
+++ b/solution.py
@@ -43,13 +43,23 @@
     return lax.axis_index(axis) % 2
 
 
-def clean_cols_kernel(data, blanked, cells, edge, edge2):
+def clean_cols_kernel(data_hbm, blanked_hbm, cells, edge, edge2, data, blanked, sems):
     taps = kernel_taps()
     chans, rows, cols = data.shape
+    group = chans // 4
+    copies = [pltpu.make_async_copy(blanked_hbm, blanked, sems.at[4])]
+    for g in range(4):
+        part = pl.ds(g * group, group)
+        copies.append(pltpu.make_async_copy(data_hbm.at[part], data.at[part], sems.at[g]))
+    for copy in copies:
+        copy.start()
     even = odd_of("pix") == 0
+    copies[0].wait()
     kept = (1 - blanked[...]).astype(jnp.float32)
     lane = lax.broadcasted_iota(jnp.int32, (rows, cols), 1)
     for c in range(chans):
+        if c % group == 0:
+            copies[1 + c // group].wait()
         x = data[c] * kept
         acc = taps[3] * x
         for t in (1, 2, 3):
@@ -177,19 +187,7 @@
                     put(w, k - 14, runs[w])
 
 
-def two_terms(sums, w):
-    value = jnp.concatenate([sums[w, tile] for tile in range(sums.shape[1])], axis=1)
-    first = value.astype(jnp.bfloat16)
-    second = (value - first.astype(jnp.float32)).astype(jnp.bfloat16)
-    return jnp.concatenate([first, second], axis=1)
-
-
-def column_windows(sums, w, band):
-    both = jnp.concatenate([band, band], axis=0)
-    return jnp.dot(two_terms(sums, w), both, preferred_element_type=jnp.float32)
-
-
-def pair_noise_kernel(own, link, core, after, boxes, window, band, field, energy, sums):
+def pair_noise_kernel(own, link, core, after, boxes, sums, band, field, energy):
     chans, tall, cols = own.shape
     rows = tall // 2
     odd = odd_of("pix")
@@ -221,16 +219,14 @@
         return carry
 
     lax.fori_loop(0, 8, row_windows, 0)
-    apart = lax.broadcasted_iota(jnp.int32, (cols, cols), 0) - lax.broadcasted_iota(
-        jnp.int32, (cols, cols), 1
-    )
-    band[...] = (jnp.abs(apart) <= 15).astype(jnp.float32).astype(jnp.bfloat16)
-    for w in range(4):
-        window[w] = column_windows(sums, w, band[...])
+    for h in range(2):
+        i = lax.broadcasted_iota(jnp.int32, band.shape[1:], 0) + h * LANES
+        j = lax.broadcasted_iota(jnp.int32, band.shape[1:], 1) + h * 2 * LANES
+        band[h] = (jnp.abs(i - j) <= 15).astype(jnp.float32).astype(jnp.bfloat16)
 
 
 def snr_kernel(
-    own, link, core, window, band, boxes, blanked, out, field, energy, sums, ready, sems
+    own, link, core, part, band, boxes, blanked, out, field, energy, sums, ready, sems
 ):
     chans, rows, cols = own.shape
     odd = odd_of("pix")
@@ -246,24 +242,38 @@
     def row_windows(step, carry):
         w, half = step // 2, step % 2
         for tile in range(cols // LANES):
-            run = jnp.zeros((8, LANES), jnp.float32)
+            run = None
             for d in range(rows):
                 if d > 0:
                     i = jnp.where(odd == 0, 16 - d, d - 1)
-                    run = run + energy[w, tile, pl.ds(half * 8 * rows + i, 8, stride=rows), :]
+                    e = energy[w, tile, pl.ds(half * 8 * rows + i, 8, stride=rows), :]
+                    run = e if run is None else run + e
                 row = jnp.where(odd == 0, 15 - d, d)
-                sums[w, tile, pl.ds(half * 8 * rows + row, 8, stride=rows), :] = run
+                at = (w, tile, pl.ds(half * 8 * rows + row, 8, stride=rows), slice(None))
+                sums[at] = part[at] if run is None else part[at] + run
         return carry
 
     lax.fori_loop(0, 8, row_windows, 0)
-    kept = (1 - blanked[...]).astype(jnp.float32)
+    firsts, seconds = [], []
+    for tile in range(cols // LANES):
+        value = sums[:, tile].reshape(4 * chans * rows, LANES)
+        firsts.append(value.astype(jnp.bfloat16))
+        seconds.append((value - firsts[-1].astype(jnp.float32)).astype(jnp.bfloat16))
     copies = []
-    for w, width in enumerate(WIDTHS):
-        total = window[w] + column_windows(sums, w, band[...])
-        scale = lax.rsqrt(total * (1.0 / (VOLUME * width * width)) + 1e-5) * (1.0 / width)
-        ready[w] = boxes[w] * scale.reshape(chans, rows, cols) * kept[None]
-        copies.append(pltpu.make_async_copy(ready.at[w], out.at[w], sems.at[w]))
-        copies[-1].start()
+    for h in range(2):
+        both = jnp.concatenate(firsts[h : h + 3] + seconds[h : h + 3], axis=1)
+        ones = jnp.concatenate([band[h], band[h]], axis=0)
+        total = jnp.dot(both, ones, preferred_element_type=jnp.float32)
+        lanes = slice(h * 2 * LANES, (h + 1) * 2 * LANES)
+        kept = (1 - blanked[:, lanes]).astype(jnp.float32)
+        for w, width in enumerate(WIDTHS):
+            scale = total[w * chans * rows : (w + 1) * chans * rows]
+            scale = lax.rsqrt(scale * (1.0 / (VOLUME * width * width)) + 1e-5) * (1.0 / width)
+            scale = scale.reshape(chans, rows, 2 * LANES)
+            ready[w, :, :, lanes] = boxes[w, :, :, lanes] * scale * kept[None]
+            there = out.at[w, :, :, lanes]
+            copies.append(pltpu.make_async_copy(ready.at[w, :, :, lanes], there, sems.at[h, w]))
+            copies[-1].start()
     for copy in copies:
         copy.wait()
 
@@ -285,7 +295,15 @@
     toward = [(i, i + 2 if i % 2 == 0 else i - 2) for i in range(pix)]
     back = [(i, i - 2 if i % 2 == 0 else i + 2) for i in range(pix)]
     cells, edge, edge2 = call(
-        clean_cols_kernel, [f32(chans, rows, cols), f32(3, chans, cols), f32(3, chans, cols)]
+        clean_cols_kernel,
+        [f32(chans, rows, cols), f32(3, chans, cols), f32(3, chans, cols)],
+        [
+            pltpu.VMEM((chans, rows, cols), jnp.float32),
+            pltpu.VMEM((rows, cols), jnp.int32),
+            pltpu.SemaphoreType.DMA((5,)),
+        ],
+        vmem=53,
+        in_specs=[ANY, ANY],
     )(data_cube, blanked)
     near = swap(cells, "pix", 0)
     edge_near = move(edge, "pix", back)
@@ -316,17 +334,16 @@
     outer_link = swap(outer_link, "chan", 1)
     outer_core = swap(outer_core, "chan", 0)
 
-    boxes, window, band = call(
+    boxes, part, band = call(
         pair_noise_kernel,
         [
             f32(4, chans, rows, cols),
-            f32(4, chans * rows, cols),
-            jax.ShapeDtypeStruct((cols, cols), jnp.bfloat16),
+            f32(4, tiles, chans * rows, LANES),
+            jax.ShapeDtypeStruct((2, 3 * LANES, 2 * LANES), jnp.bfloat16),
         ],
         [
             pltpu.VMEM((44, 32, cols), jnp.float32),
             pltpu.VMEM((4, tiles, chans * 32, LANES), jnp.float32),
-            pltpu.VMEM((4, tiles, chans * rows, LANES), jnp.float32),
         ],
         vmem=24,
         micros=4.0,
@@ -340,12 +357,12 @@
             pltpu.VMEM((4, tiles, chans * rows, LANES), jnp.float32),
             pltpu.VMEM((4, tiles, chans * rows, LANES), jnp.float32),
             pltpu.VMEM((4, chans, rows, cols), jnp.float32),
-            pltpu.SemaphoreType.DMA((4,)),
+            pltpu.SemaphoreType.DMA((2, 4)),
         ],
         vmem=24,
         micros=4.0,
         out_specs=ANY,
-    )(outer, outer_link, outer_core, window, band, boxes, blanked)
+    )(outer, outer_link, outer_core, part, band, boxes, blanked)
 
 
 def solution(mesh):

time: 52.9 us -> 53.5 us (1.011)
  local copies, waits for them, and re-layouts: 1.8 us -> 0.76 us
  Pallas kernels: 13.8 us -> 14.8 us
  waiting for transfers between devices: 15.6 us -> 16.3 us
    pallas_call x1, Pallas kernels: 0.9 us -> 2.1 us  [per_device(): call(clean_cols_kernel, [f32(chans, rows, cols), f32(3, chans, cols), f32...]
    pallas_call x1, Pallas kernels: 6.16 us -> 5.03 us  [per_device(): call(pair_noise_kernel, [f32(4, chans, rows, cols), f32(4, tiles, chans *...]
    unnamed x6 -> x2, local copies, waits for them, and re-layouts: 1.8 us -> 0.76 us
    pallas_call x1, Pallas kernels: 4.62 us -> 5.53 us  [per_device(): call(snr_kernel, f32(4, chans, rows, cols), [pltpu.VMEM((44, 16, cols), j...]
    ppermute x9, waiting for transfers between devices: 15.6 us -> 16.3 us  [move(): lax.ppermute(value, axis, [(a, b) for a, b in pairs if 0 <= b < count])]
  transfers between devices with their start and end apart: 9 -> 9, of which waited for: 4 -> 5; matrix products, arithmetic and copies ran while one was open for 0% -> 0% of each run, Pallas kernels for 16% -> 14%
where the time goes in v1:
time: 53.5 us; the launch traced here: 53.2 us
  starting transfers between devices  21.1 us (39%)
  waiting for transfers between devices  16.3 us (30%)
  Pallas kernels  14.8 us (28%)
  local copies, waits for them, and re-layouts  0.76 us (1%)
    ppermute x9, starting transfers between devices, move(): lax.ppermute(value, axis, [(a, b) for a, b in pairs if 0 <= b < count])  21.1 us
    ppermute x9, waiting for transfers between devices, move(): lax.ppermute(value, axis, [(a, b) for a, b in pairs if 0 <= b < count])  16.3 us
    pallas_call x1, Pallas kernels, per_device(): call(snr_kernel, f32(4, chans, rows, cols), [pltpu.VMEM((44, 16, cols), j...  5.53 us
    pallas_call x1, Pallas kernels, per_device(): call(pair_noise_kernel, [f32(4, chans, rows, cols), f32(4, tiles, chans *...  5.03 us
    pallas_call x1, Pallas kernels, per_device(): call(clean_cols_kernel, [f32(chans, rows, cols), f32(3, chans, cols), f32...  2.1 us
    pallas_call x1, Pallas kernels, per_device(): call(pair_rows_kernel, [f32(chans, 32, cols), f32(HALO, 32, cols), f32(HA...  1.35 us
  transfers between devices with their start and end apart: 9, of which 5 were waited for; matrix products, arithmetic and copies ran while one was open for 0% of the time, Pallas kernels for 14%

profile of v1, /device:TPU:34, one launch (start us, length us, event | category | flops | bytes accessed | tf_op | source)
XLA Modules:
  0.0 53.2 jit_solution(15082681838980261097)
XLA Ops:
  0.0 0.0 copy-start
  0.0 0.8 %copy-done = s32[16,512]{1,0:T(8,128)S(1)} copy-done((s32[16,512]{1,0:T(8,128)S(1)}, s32[16,512]{1,0:T(8,128)}, u32[]{:S(2)}) %copy-start) | copy-done | bytes 32792
  0.8 2.1 %shard_map.28 = (f32[16,16,512]{2,1,0:T(8,128)S(1)}, f32[3,16,512]{2,1,0:T(8,128)S(1)}, f32[3,16,512]{2,1,0:T(8,128)S(1)}) custom-call(f32[16,16,512]{2,1,0:T(8,128)} %data_hbm.1, s32[16,512]{1,0:T(8,128)S(1)} %copy-done), custom_call_target="tpu_custom_call" | custom-call | bytes 3000000 | tf_op jit(solution)/shard_map/pallas_call | solution.py:297
  2.9 3.1 %collective-permute-start = (f32[16,16,512]{2,1,0:T(8,128)S(1)}, f32[16,16,512]{2,1,0:T(8,128)S(1)}, u32[]{:S(2)}, u32[]{:S(2)}) collective-permute-start(f32[16,16,512]{2,1,0:T(8,128)S(1)} %get-tuple-element.17.cells), channel_id=1, source_target_pairs={{0,16},{16,0},{32,48},{48,32},{64,80},{80,64},{96,112},{112,96},{1... | collective-permute-start | bytes 1572872 | tf_op jit(solution)/shard_map/ppermute | solution.py:288
  5.9 3.4 %collective-permute-start.3 = (f32[3,16,512]{2,1,0:T(8,128)S(1)}, f32[3,16,512]{2,1,0:T(8,128)S(1)}, u32[]{:S(2)}, u32[]{:S(2)}) collective-permute-start(f32[3,16,512]{2,1,0:T(8,128)S(1)} %get-tuple-element.19), channel_id=1, source_target_pairs={{0,32},{32,64},{48,16},{64,96},{80,48},{112,80},{1,33},{33,65},{49... | collective-permute-start | bytes 294920 | tf_op jit(solution)/shard_map/ppermute | solution.py:288
  9.3 1.9 %collective-permute-start.2 = (f32[3,16,512]{2,1,0:T(8,128)S(1)}, f32[3,16,512]{2,1,0:T(8,128)S(1)}, u32[]{:S(2)}, u32[]{:S(2)}) collective-permute-start(f32[3,16,512]{2,1,0:T(8,128)S(1)} %get-tuple-element.18.edge), channel_id=1, source_target_pairs={{16,32},{32,16},{48,64},{64,48},{80,96},{96,80},{17,33},{33,17},{4... | collective-permute-start | bytes 294920 | tf_op jit(solution)/shard_map/ppermute | solution.py:288
  11.2 1.9 %collective-permute-start.1 = (f32[3,16,512]{2,1,0:T(8,128)S(1)}, f32[3,16,512]{2,1,0:T(8,128)S(1)}, u32[]{:S(2)}, u32[]{:S(2)}) collective-permute-start(f32[3,16,512]{2,1,0:T(8,128)S(1)} %get-tuple-element.18.edge), channel_id=1, source_target_pairs={{16,48},{32,0},{48,80},{64,32},{80,112},{96,64},{17,49},{33,1},{49... | collective-permute-start | bytes 294920 | tf_op jit(solution)/shard_map/ppermute | solution.py:288
  13.2 0.0 collective-permute-done.3.rest_2_.beyond
  13.2 5.1 %collective-permute-done.2.rest_1_.edge_far = f32[3,16,512]{2,1,0:T(8,128)S(1)} collective-permute-done((f32[3,16,512]{2,1,0:T(8,128)S(1)}, f32[3,16,512]{2,1,0:T(8,128)S(1)}, u32[]{:S(2)}, u32[]{:S(2)}) %collective-permute-start.2) | collective-permute-done | bytes 98336 | tf_op jit(solution)/shard_map/ppermute | solution.py:288
  18.3 0.0 collective-permute-done.1.rest_0_.edge_near
  18.3 1.9 %collective-permute-done.value = f32[16,16,512]{2,1,0:T(8,128)S(1)} collective-permute-done((f32[16,16,512]{2,1,0:T(8,128)S(1)}, f32[16,16,512]{2,1,0:T(8,128)S(1)}, u32[]{:S(2)}, u32[]{:S(2)}) %collective-permute-start) | collective-permute-done | bytes 524320 | tf_op jit(solution)/shard_map/ppermute | solution.py:288
  20.2 3.4 %collective-permute-start.4 = (f32[16,16,512]{2,1,0:T(8,128)S(1)}, f32[16,16,512]{2,1,0:T(8,128)S(1)}, u32[]{:S(2)}, u32[]{:S(2)}) collective-permute-start(f32[16,16,512]{2,1,0:T(8,128)S(1)} %shard_map.29.near), channel_id=1, source_target_pairs={{0,32},{32,64},{48,16},{64,96},{80,48},{112,80},{1,33},{33,65},{49... | collective-permute-start | bytes 1572872 | tf_op jit(solution)/shard_map/ppermute | solution.py:288
  23.6 1.4 %shard_map.31 = (f32[16,32,512]{2,1,0:T(8,128)S(1)}, f32[14,32,512]{2,1,0:T(8,128)S(1)}, f32[14,32,512]{2,1,0:T(8,128)S(1)}) custom-call(f32[16,16,512]{2,1,0:T(8,128)S(1)} %get-tuple-element.17.cells, f32[16,16,512]{2,1,0:T(8,128)S(1)} %shard_map.29.near, f32[3,16,512]{2,1,0:T(8,128)S(1)} %collective-permute-done.2.rest_1_.edge_far, ...), custom_call_target="tpu_custom_call" | custom-call | bytes 3000000 | tf_op jit(solution)/shard_map/pallas_call | solution.py:321
  25.0 3.7 %collective-permute-start.7 = (f32[14,32,512]{2,1,0:T(8,128)S(1)}, f32[14,32,512]{2,1,0:T(8,128)S(1)}, u32[]{:S(2)}, u32[]{:S(2)}) collective-permute-start(f32[14,32,512]{2,1,0:T(8,128)S(1)} %get-tuple-element.24), channel_id=1, source_target_pairs={{1,2},{2,1},{3,4},{4,3},{5,6},{6,5},{7,8},{8,7},{9,10},{10,9},{11,... | collective-permute-start | bytes 2752520 | tf_op jit(solution)/shard_map/ppermute | solution.py:288
  28.7 0.1 collective-permute-start.8
  28.8 6.1 %collective-permute-done.4.far = f32[16,16,512]{2,1,0:T(8,128)S(1)} collective-permute-done((f32[16,16,512]{2,1,0:T(8,128)S(1)}, f32[16,16,512]{2,1,0:T(8,128)S(1)}, u32[]{:S(2)}, u32[]{:S(2)}) %collective-permute-start.4) | collective-permute-done | bytes 524320 | tf_op jit(solution)/shard_map/ppermute | solution.py:288
  34.9 0.8 %shard_map.30 = (f32[16,16,512]{2,1,0:T(8,128)S(1)}, f32[14,16,512]{2,1,0:T(8,128)S(1)}, f32[14,16,512]{2,1,0:T(8,128)S(1)}) custom-call(f32[16,16,512]{2,1,0:T(8,128)S(1)} %collective-permute-done.4.far, f32[3,16,512]{2,1,0:T(8,128)S(1)} %get-tuple-element.18.edge, f32[3,16,512]{2,1,0:T(8,128)S(1)} %collective-permute-done.3.rest_2_.beyond), custom_call_target="tpu_custom_call" | custom-call | bytes 3000000 | tf_op jit(solution)/shard_map/pallas_call | solution.py:329
  35.7 3.4 %collective-permute-start.5 = (f32[14,16,512]{2,1,0:T(8,128)S(1)}, f32[14,16,512]{2,1,0:T(8,128)S(1)}, u32[]{:S(2)}, u32[]{:S(2)}) collective-permute-start(f32[14,16,512]{2,1,0:T(8,128)S(1)} %get-tuple-element.21), channel_id=1, source_target_pairs={{1,2},{2,1},{3,4},{4,3},{5,6},{6,5},{7,8},{8,7},{9,10},{10,9},{11,... | collective-permute-start | bytes 1376264 | tf_op jit(solution)/shard_map/ppermute | solution.py:288
  39.1 0.3 collective-permute-start.6
  39.4 2.4 %collective-permute-done.7.link = f32[14,32,512]{2,1,0:T(8,128)S(1)} collective-permute-done((f32[14,32,512]{2,1,0:T(8,128)S(1)}, f32[14,32,512]{2,1,0:T(8,128)S(1)}, u32[]{:S(2)}, u32[]{:S(2)}) %collective-permute-start.7) | collective-permute-done | bytes 917536 | tf_op jit(solution)/shard_map/ppermute | solution.py:288
  41.8 0.0 collective-permute-done.8.core
  41.8 5.0 %shard_map.32 = (f32[4,16,16,512]{3,2,1,0:T(8,128)S(1)}, f32[4,4,256,128]{3,2,1,0:T(8,128)S(1)}, bf16[2,384,256]{2,1,0:T(8,128)(2,1)S(1)}) custom-call(f32[16,32,512]{2,1,0:T(8,128)S(1)} %get-tuple-element.23.own, f32[14,32,512]{2,1,0:T(8,128)S(1)} %collective-permute-done.7.link, f32[14,32,512]{2,1,0:T(8,128)S(1)} %collective-permute-done.8.core, ...), custom_call_target="tpu_custom_call" | custom-call | bytes 12000000 | tf_op jit(solution)/shard_map/pallas_call | solution.py:337
  46.8 0.8 %collective-permute-done.5.link = f32[14,16,512]{2,1,0:T(8,128)S(1)} collective-permute-done((f32[14,16,512]{2,1,0:T(8,128)S(1)}, f32[14,16,512]{2,1,0:T(8,128)S(1)}, u32[]{:S(2)}, u32[]{:S(2)}) %collective-permute-start.5) | collective-permute-done | bytes 458784 | tf_op jit(solution)/shard_map/ppermute | solution.py:288
  47.6 0.0 collective-permute-done.6.core
  47.6 5.5 %shard_map.33 = f32[4,16,16,512]{3,2,1,0:T(8,128)} custom-call(f32[16,16,512]{2,1,0:T(8,128)S(1)} %get-tuple-element.20.after.own, f32[14,16,512]{2,1,0:T(8,128)S(1)} %collective-permute-done.5.link, f32[14,16,512]{2,1,0:T(8,128)S(1)} %collective-permute-done.6.core, f32[4,4,256,128]{3,2,1,0:T(8,128)S(1)} %get-tuple-element.26.part, ...), custom_call_target="tpu_custom_call" | custom-call | bytes 12000000 | tf_op jit(solution)/shard_map/pallas_call | solution.py:352
  (1 shorter events, 0.0 us)
Async XLA Ops:
  0.0 0.8 %copy-start = (s32[16,512]{1,0:T(8,128)S(1)}, s32[16,512]{1,0:T(8,128)}, u32[]{:S(2)}) copy-start(s32[16,512]{1,0:T(8,128)} %blanked.1) | copy-start | bytes 98308
  2.9 17.4 %collective-permute-start = (f32[16,16,512]{2,1,0:T(8,128)S(1)}, f32[16,16,512]{2,1,0:T(8,128)S(1)}, u32[]{:S(2)}, u32[]{:S(2)}) collective-permute-start(f32[16,16,512]{2,1,0:T(8,128)S(1)} %get-tuple-element.17.cells), channel_id=1, source_target_pairs={{0,16},{16,0},{32,48},{48,32},{64,80},{80,64},{96,112},{112,96},{1... | collective-permute-start | bytes 1572872 | tf_op jit(solution)/shard_map/ppermute | solution.py:288
  5.9 7.3 %collective-permute-start.3 = (f32[3,16,512]{2,1,0:T(8,128)S(1)}, f32[3,16,512]{2,1,0:T(8,128)S(1)}, u32[]{:S(2)}, u32[]{:S(2)}) collective-permute-start(f32[3,16,512]{2,1,0:T(8,128)S(1)} %get-tuple-element.19), channel_id=1, source_target_pairs={{0,32},{32,64},{48,16},{64,96},{80,48},{112,80},{1,33},{33,65},{49... | collective-permute-start | bytes 294920 | tf_op jit(solution)/shard_map/ppermute | solution.py:288
  9.3 9.0 %collective-permute-start.2 = (f32[3,16,512]{2,1,0:T(8,128)S(1)}, f32[3,16,512]{2,1,0:T(8,128)S(1)}, u32[]{:S(2)}, u32[]{:S(2)}) collective-permute-start(f32[3,16,512]{2,1,0:T(8,128)S(1)} %get-tuple-element.18.edge), channel_id=1, source_target_pairs={{16,32},{32,16},{48,64},{64,48},{80,96},{96,80},{17,33},{33,17},{4... | collective-permute-start | bytes 294920 | tf_op jit(solution)/shard_map/ppermute | solution.py:288
  11.2 7.1 %collective-permute-start.1 = (f32[3,16,512]{2,1,0:T(8,128)S(1)}, f32[3,16,512]{2,1,0:T(8,128)S(1)}, u32[]{:S(2)}, u32[]{:S(2)}) collective-permute-start(f32[3,16,512]{2,1,0:T(8,128)S(1)} %get-tuple-element.18.edge), channel_id=1, source_target_pairs={{16,48},{32,0},{48,80},{64,32},{80,112},{96,64},{17,49},{33,1},{49... | collective-permute-start | bytes 294920 | tf_op jit(solution)/shard_map/ppermute | solution.py:288
  20.2 14.7 %collective-permute-start.4 = (f32[16,16,512]{2,1,0:T(8,128)S(1)}, f32[16,16,512]{2,1,0:T(8,128)S(1)}, u32[]{:S(2)}, u32[]{:S(2)}) collective-permute-start(f32[16,16,512]{2,1,0:T(8,128)S(1)} %shard_map.29.near), channel_id=1, source_target_pairs={{0,32},{32,64},{48,16},{64,96},{80,48},{112,80},{1,33},{33,65},{49... | collective-permute-start | bytes 1572872 | tf_op jit(solution)/shard_map/ppermute | solution.py:288
  25.0 16.8 %collective-permute-start.7 = (f32[14,32,512]{2,1,0:T(8,128)S(1)}, f32[14,32,512]{2,1,0:T(8,128)S(1)}, u32[]{:S(2)}, u32[]{:S(2)}) collective-permute-start(f32[14,32,512]{2,1,0:T(8,128)S(1)} %get-tuple-element.24), channel_id=1, source_target_pairs={{1,2},{2,1},{3,4},{4,3},{5,6},{6,5},{7,8},{8,7},{9,10},{10,9},{11,... | collective-permute-start | bytes 2752520 | tf_op jit(solution)/shard_map/ppermute | solution.py:288
  28.7 13.1 %collective-permute-start.8 = (f32[14,32,512]{2,1,0:T(8,128)S(1)}, f32[14,32,512]{2,1,0:T(8,128)S(1)}, u32[]{:S(2)}, u32[]{:S(2)}) collective-permute-start(f32[14,32,512]{2,1,0:T(8,128)S(1)} %get-tuple-element.25), channel_id=1, source_target_pairs={{0,1},{1,0},{2,3},{3,2},{4,5},{5,4},{6,7},{7,6},{8,9},{9,8},{10,11... | collective-permute-start | bytes 2752520 | tf_op jit(solution)/shard_map/ppermute | solution.py:288
  35.7 11.9 %collective-permute-start.5 = (f32[14,16,512]{2,1,0:T(8,128)S(1)}, f32[14,16,512]{2,1,0:T(8,128)S(1)}, u32[]{:S(2)}, u32[]{:S(2)}) collective-permute-start(f32[14,16,512]{2,1,0:T(8,128)S(1)} %get-tuple-element.21), channel_id=1, source_target_pairs={{1,2},{2,1},{3,4},{4,3},{5,6},{6,5},{7,8},{8,7},{9,10},{10,9},{11,... | collective-permute-start | bytes 1376264 | tf_op jit(solution)/shard_map/ppermute | solution.py:288
  39.1 8.5 %collective-permute-start.6 = (f32[14,16,512]{2,1,0:T(8,128)S(1)}, f32[14,16,512]{2,1,0:T(8,128)S(1)}, u32[]{:S(2)}, u32[]{:S(2)}) collective-permute-start(f32[14,16,512]{2,1,0:T(8,128)S(1)} %get-tuple-element.22), channel_id=1, source_target_pairs={{0,1},{1,0},{2,3},{3,2},{4,5},{5,4},{6,7},{7,6},{8,9},{9,8},{10,11... | collective-permute-start | bytes 1376264 | tf_op jit(solution)/shard_map/ppermute | solution.py:288

commit v2 on v0

--- a/solution.py
+++ b/solution.py
@@ -184,12 +184,19 @@
     return jnp.concatenate([first, second], axis=1)
 
 
-def column_windows(sums, w, band):
-    both = jnp.concatenate([band, band], axis=0)
-    return jnp.dot(two_terms(sums, w), both, preferred_element_type=jnp.float32)
-
-
-def pair_noise_kernel(own, link, core, after, boxes, window, band, field, energy, sums):
+def for_parity(odd, body):
+    def loop(even):
+        def step(w, carry):
+            body(w, even)
+            return carry
+
+        lax.fori_loop(0, 4, step, 0)
+
+    pl.when(odd == 0)(lambda: loop(True))
+    pl.when(odd == 1)(lambda: loop(False))
+
+
+def pair_noise_kernel(own, link, core, after, boxes, sums, band, field, energy):
     chans, tall, cols = own.shape
     rows = tall // 2
     odd = odd_of("pix")
@@ -203,34 +210,32 @@
 
         lax.fori_loop(0, 2, strips, 0)
 
-    def row_windows(step, carry):
-        w, half = step // 2, step % 2
-        for tile in range(cols // LANES):
-
-            def e(i):
-                return energy[w, tile, pl.ds(half * 8 * tall + i, 8, stride=tall), :]
-
-            run = e(rows * odd)
-            for i in range(1, rows):
-                run = run + e(rows * odd + i)
-            for d in range(rows):
-                if d > 0:
-                    run = run + e(jnp.where(odd == 0, 15 + d, 16 - d))
-                row = jnp.where(odd == 0, d, 15 - d)
-                sums[w, tile, pl.ds(half * 8 * rows + row, 8, stride=rows), :] = run
-        return carry
-
-    lax.fori_loop(0, 8, row_windows, 0)
+    def row_windows(w, even):
+        for half in range(2):
+            for tile in range(cols // LANES):
+
+                def e(i):
+                    return energy[w, tile, pl.ds(half * 8 * tall + i, 8, stride=tall), :]
+
+                first = 0 if even else rows
+                run = e(first)
+                for i in range(1, rows):
+                    run = run + e(first + i)
+                for d in range(rows):
+                    if d > 0:
+                        run = run + e(15 + d if even else 16 - d)
+                    row = d if even else 15 - d
+                    sums[w, tile, pl.ds(half * 8 * rows + row, 8, stride=rows), :] = run
+
+    for_parity(odd, row_windows)
     apart = lax.broadcasted_iota(jnp.int32, (cols, cols), 0) - lax.broadcasted_iota(
         jnp.int32, (cols, cols), 1
     )
     band[...] = (jnp.abs(apart) <= 15).astype(jnp.float32).astype(jnp.bfloat16)
-    for w in range(4):
-        window[w] = column_windows(sums, w, band[...])
 
 
 def snr_kernel(
-    own, link, core, window, band, boxes, blanked, out, field, energy, sums, ready, sems
+    own, link, core, part, band, boxes, blanked, out, field, energy, sums, ready, sems
 ):
     chans, rows, cols = own.shape
     odd = odd_of("pix")
@@ -243,23 +248,25 @@
 
         lax.fori_loop(0, 2, strips, 0)
 
-    def row_windows(step, carry):
-        w, half = step // 2, step % 2
-        for tile in range(cols // LANES):
-            run = jnp.zeros((8, LANES), jnp.float32)
-            for d in range(rows):
-                if d > 0:
-                    i = jnp.where(odd == 0, 16 - d, d - 1)
-                    run = run + energy[w, tile, pl.ds(half * 8 * rows + i, 8, stride=rows), :]
-                row = jnp.where(odd == 0, 15 - d, d)
-                sums[w, tile, pl.ds(half * 8 * rows + row, 8, stride=rows), :] = run
-        return carry
-
-    lax.fori_loop(0, 8, row_windows, 0)
+    def row_windows(w, even):
+        for half in range(2):
+            for tile in range(cols // LANES):
+                run = None
+                for d in range(rows):
+                    if d > 0:
+                        i = 16 - d if even else d - 1
+                        e = energy[w, tile, pl.ds(half * 8 * rows + i, 8, stride=rows), :]
+                        run = e if run is None else run + e
+                    row = 15 - d if even else d
+                    at = (w, tile, pl.ds(half * 8 * rows + row, 8, stride=rows), slice(None))
+                    sums[at] = part[at] if run is None else part[at] + run
+
+    for_parity(odd, row_windows)
     kept = (1 - blanked[...]).astype(jnp.float32)
+    both = jnp.concatenate([band[...], band[...]], axis=0)
     copies = []
     for w, width in enumerate(WIDTHS):
-        total = window[w] + column_windows(sums, w, band[...])
+        total = jnp.dot(two_terms(sums, w), both, preferred_element_type=jnp.float32)
         scale = lax.rsqrt(total * (1.0 / (VOLUME * width * width)) + 1e-5) * (1.0 / width)
         ready[w] = boxes[w] * scale.reshape(chans, rows, cols) * kept[None]
         copies.append(pltpu.make_async_copy(ready.at[w], out.at[w], sems.at[w]))
@@ -316,17 +323,16 @@
     outer_link = swap(outer_link, "chan", 1)
     outer_core = swap(outer_core, "chan", 0)
 
-    boxes, window, band = call(
+    boxes, part, band = call(
         pair_noise_kernel,
         [
             f32(4, chans, rows, cols),
-            f32(4, chans * rows, cols),
+            f32(4, tiles, chans * rows, LANES),
             jax.ShapeDtypeStruct((cols, cols), jnp.bfloat16),
         ],
         [
             pltpu.VMEM((44, 32, cols), jnp.float32),
             pltpu.VMEM((4, tiles, chans * 32, LANES), jnp.float32),
-            pltpu.VMEM((4, tiles, chans * rows, LANES), jnp.float32),
         ],
         vmem=24,
         micros=4.0,
@@ -345,7 +351,7 @@
         vmem=24,
         micros=4.0,
         out_specs=ANY,
-    )(outer, outer_link, outer_core, window, band, boxes, blanked)
+    )(outer, outer_link, outer_core, part, band, boxes, blanked)
 
 
 def solution(mesh):

time: 52.9 us -> 52.6 us (level)
  Pallas kernels: 13.8 us -> 12.2 us
  waiting for transfers between devices: 15.6 us -> 17 us
    pallas_call x1, Pallas kernels: 6.16 us -> 4.38 us  [per_device(): call(pair_noise_kernel, [f32(4, chans, rows, cols), f32(4, tiles, chans *...]
    ppermute x9, waiting for transfers between devices: 15.6 us -> 17 us  [move(): lax.ppermute(value, axis, [(a, b) for a, b in pairs if 0 <= b < count])]
  transfers between devices with their start and end apart: 9 -> 9, of which waited for: 4 -> 5; matrix products, arithmetic and copies ran while one was open for 0% -> 0% of each run, Pallas kernels for 16% -> 13%
where the time goes in v2:
time: 52.6 us; the launch traced here: 52.2 us
  starting transfers between devices  21.1 us (40%)
  waiting for transfers between devices  17 us (32%)
  Pallas kernels  12.2 us (23%)
  local copies, waits for them, and re-layouts  1.8 us (3%)
    ppermute x9, starting transfers between devices, move(): lax.ppermute(value, axis, [(a, b) for a, b in pairs if 0 <= b < count])  21.1 us
    ppermute x9, waiting for transfers between devices, move(): lax.ppermute(value, axis, [(a, b) for a, b in pairs if 0 <= b < count])  17 us
    pallas_call x1, Pallas kernels, per_device(): call(snr_kernel, f32(4, chans, rows, cols), [pltpu.VMEM((44, 16, cols), j...  4.71 us
    pallas_call x1, Pallas kernels, per_device(): call(pair_noise_kernel, [f32(4, chans, rows, cols), f32(4, tiles, chans *...  4.38 us
    unnamed x6, local copies, waits for them, and re-layouts  1.8 us
    pallas_call x1, Pallas kernels, per_device(): call(pair_rows_kernel, [f32(chans, 32, cols), f32(HALO, 32, cols), f32(HA...  1.35 us
  transfers between devices with their start and end apart: 9, of which 5 were waited for; matrix products, arithmetic and copies ran while one was open for 0% of the time, Pallas kernels for 13%

profile of v2, /device:TPU:34, one launch (start us, length us, event | category | flops | bytes accessed | tf_op | source)
XLA Modules:
  0.0 52.2 jit_solution(13798901426182570727)
XLA Ops:
  0.0 0.0 copy-start
  0.0 1.0 %copy-done = f32[16,16,512]{2,1,0:T(8,128)S(1)} copy-done((f32[16,16,512]{2,1,0:T(8,128)S(1)}, f32[16,16,512]{2,1,0:T(8,128)}, u32[]{:S(2)}) %copy-start) | copy-done | bytes 524312
  1.0 0.0 copy-start.1
  1.0 0.8 %copy-done.1 = s32[16,512]{1,0:T(8,128)S(1)} copy-done((s32[16,512]{1,0:T(8,128)S(1)}, s32[16,512]{1,0:T(8,128)}, u32[]{:S(2)}) %copy-start.1) | copy-done | bytes 32792
  1.8 0.9 %shard_map.28 = (f32[16,16,512]{2,1,0:T(8,128)S(1)}, f32[3,16,512]{2,1,0:T(8,128)S(1)}, f32[3,16,512]{2,1,0:T(8,128)S(1)}) custom-call(f32[16,16,512]{2,1,0:T(8,128)S(1)} %copy-done, s32[16,512]{1,0:T(8,128)S(1)} %copy-done.1), custom_call_target="tpu_custom_call" | custom-call | bytes 3000000 | tf_op jit(solution)/shard_map/pallas_call | solution.py:294
  2.7 3.1 %collective-permute-start = (f32[16,16,512]{2,1,0:T(8,128)S(1)}, f32[16,16,512]{2,1,0:T(8,128)S(1)}, u32[]{:S(2)}, u32[]{:S(2)}) collective-permute-start(f32[16,16,512]{2,1,0:T(8,128)S(1)} %get-tuple-element.17.cells), channel_id=1, source_target_pairs={{0,16},{16,0},{32,48},{48,32},{64,80},{80,64},{96,112},{112,96},{1... | collective-permute-start | bytes 1572872 | tf_op jit(solution)/shard_map/ppermute | solution.py:285
  5.8 3.4 %collective-permute-start.3 = (f32[3,16,512]{2,1,0:T(8,128)S(1)}, f32[3,16,512]{2,1,0:T(8,128)S(1)}, u32[]{:S(2)}, u32[]{:S(2)}) collective-permute-start(f32[3,16,512]{2,1,0:T(8,128)S(1)} %get-tuple-element.19), channel_id=1, source_target_pairs={{0,32},{32,64},{48,16},{64,96},{80,48},{112,80},{1,33},{33,65},{49... | collective-permute-start | bytes 294920 | tf_op jit(solution)/shard_map/ppermute | solution.py:285
  9.2 1.9 %collective-permute-start.2 = (f32[3,16,512]{2,1,0:T(8,128)S(1)}, f32[3,16,512]{2,1,0:T(8,128)S(1)}, u32[]{:S(2)}, u32[]{:S(2)}) collective-permute-start(f32[3,16,512]{2,1,0:T(8,128)S(1)} %get-tuple-element.18.edge), channel_id=1, source_target_pairs={{16,32},{32,16},{48,64},{64,48},{80,96},{96,80},{17,33},{33,17},{4... | collective-permute-start | bytes 294920 | tf_op jit(solution)/shard_map/ppermute | solution.py:285
  11.1 1.9 %collective-permute-start.1 = (f32[3,16,512]{2,1,0:T(8,128)S(1)}, f32[3,16,512]{2,1,0:T(8,128)S(1)}, u32[]{:S(2)}, u32[]{:S(2)}) collective-permute-start(f32[3,16,512]{2,1,0:T(8,128)S(1)} %get-tuple-element.18.edge), channel_id=1, source_target_pairs={{16,48},{32,0},{48,80},{64,32},{80,112},{96,64},{17,49},{33,1},{49... | collective-permute-start | bytes 294920 | tf_op jit(solution)/shard_map/ppermute | solution.py:285
  13.0 0.0 collective-permute-done.3.rest_2_.beyond
  13.0 5.1 %collective-permute-done.2.rest_1_.edge_far = f32[3,16,512]{2,1,0:T(8,128)S(1)} collective-permute-done((f32[3,16,512]{2,1,0:T(8,128)S(1)}, f32[3,16,512]{2,1,0:T(8,128)S(1)}, u32[]{:S(2)}, u32[]{:S(2)}) %collective-permute-start.2) | collective-permute-done | bytes 98336 | tf_op jit(solution)/shard_map/ppermute | solution.py:285
  18.2 0.0 collective-permute-done.1.rest_0_.edge_near
  18.2 1.9 %collective-permute-done.value = f32[16,16,512]{2,1,0:T(8,128)S(1)} collective-permute-done((f32[16,16,512]{2,1,0:T(8,128)S(1)}, f32[16,16,512]{2,1,0:T(8,128)S(1)}, u32[]{:S(2)}, u32[]{:S(2)}) %collective-permute-start) | collective-permute-done | bytes 524320 | tf_op jit(solution)/shard_map/ppermute | solution.py:285
  20.1 3.4 %collective-permute-start.4 = (f32[16,16,512]{2,1,0:T(8,128)S(1)}, f32[16,16,512]{2,1,0:T(8,128)S(1)}, u32[]{:S(2)}, u32[]{:S(2)}) collective-permute-start(f32[16,16,512]{2,1,0:T(8,128)S(1)} %shard_map.29.near), channel_id=1, source_target_pairs={{0,32},{32,64},{48,16},{64,96},{80,48},{112,80},{1,33},{33,65},{49... | collective-permute-start | bytes 1572872 | tf_op jit(solution)/shard_map/ppermute | solution.py:285
  23.5 1.4 %shard_map.31 = (f32[16,32,512]{2,1,0:T(8,128)S(1)}, f32[14,32,512]{2,1,0:T(8,128)S(1)}, f32[14,32,512]{2,1,0:T(8,128)S(1)}) custom-call(f32[16,16,512]{2,1,0:T(8,128)S(1)} %get-tuple-element.17.cells, f32[16,16,512]{2,1,0:T(8,128)S(1)} %shard_map.29.near, f32[3,16,512]{2,1,0:T(8,128)S(1)} %collective-permute-done.2.rest_1_.edge_far, ...), custom_call_target="tpu_custom_call" | custom-call | bytes 3000000 | tf_op jit(solution)/shard_map/pallas_call | solution.py:310
  24.8 0.0 copy-start.2
  24.8 3.7 %collective-permute-start.7 = (f32[14,32,512]{2,1,0:T(8,128)S(1)}, f32[14,32,512]{2,1,0:T(8,128)S(1)}, u32[]{:S(2)}, u32[]{:S(2)}) collective-permute-start(f32[14,32,512]{2,1,0:T(8,128)S(1)} %get-tuple-element.24), channel_id=1, source_target_pairs={{1,2},{2,1},{3,4},{4,3},{5,6},{6,5},{7,8},{8,7},{9,10},{10,9},{11,... | collective-permute-start | bytes 2752520 | tf_op jit(solution)/shard_map/ppermute | solution.py:285
  28.6 0.1 collective-permute-start.8
  28.6 6.1 %collective-permute-done.4.far = f32[16,16,512]{2,1,0:T(8,128)S(1)} collective-permute-done((f32[16,16,512]{2,1,0:T(8,128)S(1)}, f32[16,16,512]{2,1,0:T(8,128)S(1)}, u32[]{:S(2)}, u32[]{:S(2)}) %collective-permute-start.4) | collective-permute-done | bytes 524320 | tf_op jit(solution)/shard_map/ppermute | solution.py:285
  34.7 0.8 %shard_map.30 = (f32[16,16,512]{2,1,0:T(8,128)S(1)}, f32[14,16,512]{2,1,0:T(8,128)S(1)}, f32[14,16,512]{2,1,0:T(8,128)S(1)}) custom-call(f32[16,16,512]{2,1,0:T(8,128)S(1)} %collective-permute-done.4.far, f32[3,16,512]{2,1,0:T(8,128)S(1)} %get-tuple-element.18.edge, f32[3,16,512]{2,1,0:T(8,128)S(1)} %collective-permute-done.3.rest_2_.beyond), custom_call_target="tpu_custom_call" | custom-call | bytes 3000000 | tf_op jit(solution)/shard_map/pallas_call | solution.py:318
  35.6 3.4 %collective-permute-start.5 = (f32[14,16,512]{2,1,0:T(8,128)S(1)}, f32[14,16,512]{2,1,0:T(8,128)S(1)}, u32[]{:S(2)}, u32[]{:S(2)}) collective-permute-start(f32[14,16,512]{2,1,0:T(8,128)S(1)} %get-tuple-element.21), channel_id=1, source_target_pairs={{1,2},{2,1},{3,4},{4,3},{5,6},{6,5},{7,8},{8,7},{9,10},{10,9},{11,... | collective-permute-start | bytes 1376264 | tf_op jit(solution)/shard_map/ppermute | solution.py:285
  38.9 0.3 collective-permute-start.6
  39.2 2.4 %collective-permute-done.7.link = f32[14,32,512]{2,1,0:T(8,128)S(1)} collective-permute-done((f32[14,32,512]{2,1,0:T(8,128)S(1)}, f32[14,32,512]{2,1,0:T(8,128)S(1)}, u32[]{:S(2)}, u32[]{:S(2)}) %collective-permute-start.7) | collective-permute-done | bytes 917536 | tf_op jit(solution)/shard_map/ppermute | solution.py:285
  41.7 0.0 collective-permute-done.8.core
  41.7 4.4 %shard_map.32 = (f32[4,16,16,512]{3,2,1,0:T(8,128)S(1)}, f32[4,4,256,128]{3,2,1,0:T(8,128)S(1)}, bf16[512,512]{1,0:T(8,128)(2,1)S(1)}) custom-call(f32[16,32,512]{2,1,0:T(8,128)S(1)} %get-tuple-element.23.own, f32[14,32,512]{2,1,0:T(8,128)S(1)} %collective-permute-done.7.link, f32[14,32,512]{2,1,0:T(8,128)S(1)} %collective-permute-done.8.core, ...), custom_call_target="tpu_custom_call" | custom-call | bytes 12000000 | tf_op jit(solution)/shard_map/pallas_call | solution.py:326
  46.0 1.4 %collective-permute-done.5.link = f32[14,16,512]{2,1,0:T(8,128)S(1)} collective-permute-done((f32[14,16,512]{2,1,0:T(8,128)S(1)}, f32[14,16,512]{2,1,0:T(8,128)S(1)}, u32[]{:S(2)}, u32[]{:S(2)}) %collective-permute-start.5) | collective-permute-done | bytes 458784 | tf_op jit(solution)/shard_map/ppermute | solution.py:285
  47.5 0.0 collective-permute-done.6.core
  47.5 0.0 copy-done.2
  47.5 4.7 %shard_map.33 = f32[4,16,16,512]{3,2,1,0:T(8,128)} custom-call(f32[16,16,512]{2,1,0:T(8,128)S(1)} %get-tuple-element.20.after.own, f32[14,16,512]{2,1,0:T(8,128)S(1)} %collective-permute-done.5.link, f32[14,16,512]{2,1,0:T(8,128)S(1)} %collective-permute-done.6.core, f32[4,4,256,128]{3,2,1,0:T(8,128)S(1)} %get-tuple-element.26.part, ...), custom_call_target="tpu_custom_call" | custom-call | bytes 12000000 | tf_op jit(solution)/shard_map/pallas_call | solution.py:341
  (1 shorter events, 0.0 us)
Async XLA Ops:
  0.0 1.0 %copy-start = (f32[16,16,512]{2,1,0:T(8,128)S(1)}, f32[16,16,512]{2,1,0:T(8,128)}, u32[]{:S(2)}) copy-start(f32[16,16,512]{2,1,0:T(8,128)} %data.1) | copy-start | bytes 1572868
  1.0 0.8 %copy-start.1 = (s32[16,512]{1,0:T(8,128)S(1)}, s32[16,512]{1,0:T(8,128)}, u32[]{:S(2)}) copy-start(s32[16,512]{1,0:T(8,128)} %blanked.3) | copy-start | bytes 98308
  2.7 17.4 %collective-permute-start = (f32[16,16,512]{2,1,0:T(8,128)S(1)}, f32[16,16,512]{2,1,0:T(8,128)S(1)}, u32[]{:S(2)}, u32[]{:S(2)}) collective-permute-start(f32[16,16,512]{2,1,0:T(8,128)S(1)} %get-tuple-element.17.cells), channel_id=1, source_target_pairs={{0,16},{16,0},{32,48},{48,32},{64,80},{80,64},{96,112},{112,96},{1... | collective-permute-start | bytes 1572872 | tf_op jit(solution)/shard_map/ppermute | solution.py:285
  5.8 7.3 %collective-permute-start.3 = (f32[3,16,512]{2,1,0:T(8,128)S(1)}, f32[3,16,512]{2,1,0:T(8,128)S(1)}, u32[]{:S(2)}, u32[]{:S(2)}) collective-permute-start(f32[3,16,512]{2,1,0:T(8,128)S(1)} %get-tuple-element.19), channel_id=1, source_target_pairs={{0,32},{32,64},{48,16},{64,96},{80,48},{112,80},{1,33},{33,65},{49... | collective-permute-start | bytes 294920 | tf_op jit(solution)/shard_map/ppermute | solution.py:285
  9.2 9.0 %collective-permute-start.2 = (f32[3,16,512]{2,1,0:T(8,128)S(1)}, f32[3,16,512]{2,1,0:T(8,128)S(1)}, u32[]{:S(2)}, u32[]{:S(2)}) collective-permute-start(f32[3,16,512]{2,1,0:T(8,128)S(1)} %get-tuple-element.18.edge), channel_id=1, source_target_pairs={{16,32},{32,16},{48,64},{64,48},{80,96},{96,80},{17,33},{33,17},{4... | collective-permute-start | bytes 294920 | tf_op jit(solution)/shard_map/ppermute | solution.py:285
  11.1 7.1 %collective-permute-start.1 = (f32[3,16,512]{2,1,0:T(8,128)S(1)}, f32[3,16,512]{2,1,0:T(8,128)S(1)}, u32[]{:S(2)}, u32[]{:S(2)}) collective-permute-start(f32[3,16,512]{2,1,0:T(8,128)S(1)} %get-tuple-element.18.edge), channel_id=1, source_target_pairs={{16,48},{32,0},{48,80},{64,32},{80,112},{96,64},{17,49},{33,1},{49... | collective-permute-start | bytes 294920 | tf_op jit(solution)/shard_map/ppermute | solution.py:285
  20.1 14.7 %collective-permute-start.4 = (f32[16,16,512]{2,1,0:T(8,128)S(1)}, f32[16,16,512]{2,1,0:T(8,128)S(1)}, u32[]{:S(2)}, u32[]{:S(2)}) collective-permute-start(f32[16,16,512]{2,1,0:T(8,128)S(1)} %shard_map.29.near), channel_id=1, source_target_pairs={{0,32},{32,64},{48,16},{64,96},{80,48},{112,80},{1,33},{33,65},{49... | collective-permute-start | bytes 1572872 | tf_op jit(solution)/shard_map/ppermute | solution.py:285
  24.8 22.6 %copy-start.2 = (s32[16,512]{1,0:T(8,128)S(1)}, s32[16,512]{1,0:T(8,128)}, u32[]{:S(2)}) copy-start(s32[16,512]{1,0:T(8,128)} %blanked.3) | copy-start | bytes 98308
  24.8 16.8 %collective-permute-start.7 = (f32[14,32,512]{2,1,0:T(8,128)S(1)}, f32[14,32,512]{2,1,0:T(8,128)S(1)}, u32[]{:S(2)}, u32[]{:S(2)}) collective-permute-start(f32[14,32,512]{2,1,0:T(8,128)S(1)} %get-tuple-element.24), channel_id=1, source_target_pairs={{1,2},{2,1},{3,4},{4,3},{5,6},{6,5},{7,8},{8,7},{9,10},{10,9},{11,... | collective-permute-start | bytes 2752520 | tf_op jit(solution)/shard_map/ppermute | solution.py:285
  28.6 13.1 %collective-permute-start.8 = (f32[14,32,512]{2,1,0:T(8,128)S(1)}, f32[14,32,512]{2,1,0:T(8,128)S(1)}, u32[]{:S(2)}, u32[]{:S(2)}) collective-permute-start(f32[14,32,512]{2,1,0:T(8,128)S(1)} %get-tuple-element.25), channel_id=1, source_target_pairs={{0,1},{1,0},{2,3},{3,2},{4,5},{5,4},{6,7},{7,6},{8,9},{9,8},{10,11... | collective-permute-start | bytes 2752520 | tf_op jit(solution)/shard_map/ppermute | solution.py:285
  35.6 11.9 %collective-permute-start.5 = (f32[14,16,512]{2,1,0:T(8,128)S(1)}, f32[14,16,512]{2,1,0:T(8,128)S(1)}, u32[]{:S(2)}, u32[]{:S(2)}) collective-permute-start(f32[14,16,512]{2,1,0:T(8,128)S(1)} %get-tuple-element.21), channel_id=1, source_target_pairs={{1,2},{2,1},{3,4},{4,3},{5,6},{6,5},{7,8},{8,7},{9,10},{10,9},{11,... | collective-permute-start | bytes 1376264 | tf_op jit(solution)/shard_map/ppermute | solution.py:285
  38.9 8.5 %collective-permute-start.6 = (f32[14,16,512]{2,1,0:T(8,128)S(1)}, f32[14,16,512]{2,1,0:T(8,128)S(1)}, u32[]{:S(2)}, u32[]{:S(2)}) collective-permute-start(f32[14,16,512]{2,1,0:T(8,128)S(1)} %get-tuple-element.22), channel_id=1, source_target_pairs={{0,1},{1,0},{2,3},{3,2},{4,5},{5,4},{6,7},{7,6},{8,9},{9,8},{10,11... | collective-permute-start | bytes 1376264 | tf_op jit(solution)/shard_map/ppermute | solution.py:285

commit v3 on v2

--- a/solution.py
+++ b/solution.py
@@ -29,7 +29,7 @@
         scratch_shapes=list(scratch),
         compiler_params=pltpu.CompilerParams(vmem_limit_bytes=vmem * 1024 * 1024),
         cost_estimate=pl.CostEstimate(
-            flops=0, bytes_accessed=int(micros * 3.0e6), transcendentals=0
+            flops=int(micros * 1e9), bytes_accessed=int(micros * 3.0e6), transcendentals=0
         ),
         **specs,
     )
@@ -43,7 +43,7 @@
     return lax.axis_index(axis) % 2
 
 
-def clean_cols_kernel(data, blanked, cells, edge, edge2):
+def clean_cols_kernel(data, blanked, cells1, cells2, edge, edge2):
     taps = kernel_taps()
     chans, rows, cols = data.shape
     even = odd_of("pix") == 0
@@ -56,12 +56,12 @@
             left = jnp.where(lane >= t, pltpu.roll(x, t, 1), 0.0)
             right = jnp.where(lane < cols - t, pltpu.roll(x, cols - t, 1), 0.0)
             acc = acc + taps[3 + t] * (left + right)
-        cells[c] = acc
-    for r in range(3):
-        top = cells[:, r, :]
-        bottom = cells[:, rows - 3 + r, :]
-        edge[r] = jnp.where(even, top, bottom)
-        edge2[r] = jnp.where(even, bottom, top)
+        half = cells1.shape[2]
+        cells1[c] = acc[:, :half]
+        cells2[c] = acc[:, half:]
+        top, bottom = acc[0:3], acc[rows - 3 :]
+        edge[:, c, :] = jnp.where(even, top, bottom)
+        edge2[:, c, :] = jnp.where(even, bottom, top)
 
 
 def smooth_rows(field, c, base, rows):
@@ -81,12 +81,18 @@
     core[...] = full[pl.ds((chans - HALO) * (1 - odd), HALO)]
 
 
-def pair_rows_kernel(cells, near, edge_far, edge_near, full, link, core, field):
-    chans, rows, cols = cells.shape
+def pair_rows_kernel(
+    cells1, cells2, near1, near2, edge_far, edge_near, full, link, core, field
+):
+    chans, rows, half = cells1.shape
     odd = odd_of("pix")
     even = odd == 0
-    field[:, pl.ds(pl.multiple_of(8 + rows * odd, 8), rows), :] = cells[...]
-    field[:, pl.ds(pl.multiple_of(8 + rows * (1 - odd), 8), rows), :] = near[...]
+    own_at = pl.ds(pl.multiple_of(8 + rows * odd, 8), rows)
+    near_at = pl.ds(pl.multiple_of(8 + rows * (1 - odd), 8), rows)
+    field[:, own_at, :half] = cells1[...]
+    field[:, own_at, half:] = cells2[...]
+    field[:, near_at, :half] = near1[...]
+    field[:, near_at, half:] = near2[...]
     for r in range(3):
         field[:, 5 + r, :] = jnp.where(even, edge_far[r], edge_near[r])
         field[:, 40 + r, :] = jnp.where(even, edge_near[r], edge_far[r])
@@ -100,12 +106,13 @@
     send_halos(full, link, core)
 
 
-def far_rows_kernel(far, edge, beyond, full, link, core, field):
-    chans, rows, cols = far.shape
+def far_rows_kernel(far1, far2, edge, beyond, full, link, core, field):
+    chans, rows, half = far1.shape
     at, count = lax.axis_index("pix"), lax.axis_size("pix")
     even = odd_of("pix") == 0
     present = jnp.logical_and(at > 0, at < count - 1).astype(jnp.float32)
-    field[:, 8:24, :] = far[...]
+    field[:, 8:24, :half] = far1[...]
+    field[:, 8:24, half:] = far2[...]
     for r in range(3):
         field[:, 5 + r, :] = jnp.where(even, beyond[r], edge[r])
         field[:, 24 + r, :] = jnp.where(even, edge[r], beyond[r])
@@ -291,27 +298,32 @@
 
     toward = [(i, i + 2 if i % 2 == 0 else i - 2) for i in range(pix)]
     back = [(i, i - 2 if i % 2 == 0 else i + 2) for i in range(pix)]
-    cells, edge, edge2 = call(
-        clean_cols_kernel, [f32(chans, rows, cols), f32(3, chans, cols), f32(3, chans, cols)]
+    half = 256
+    cells1, cells2, edge, edge2 = call(
+        clean_cols_kernel,
+        [f32(chans, rows, half), f32(chans, rows, cols - half)] + [f32(3, chans, cols)] * 2,
     )(data_cube, blanked)
-    near = swap(cells, "pix", 0)
+    near1 = swap(cells1, "pix", 0)
+    near2 = swap(cells2, "pix", 0)
     edge_near = move(edge, "pix", back)
     edge_far = swap(edge, "pix", 1)
     beyond = move(edge2, "pix", toward)
-    near = call(
+    near1 = call(
         lambda value, *rest: None,
-        f32(*near.shape),
+        f32(*near1.shape),
         in_specs=[ANY] * 4,
         out_specs=ANY,
         input_output_aliases={0: 0},
-    )(near, edge_near, edge_far, beyond)
-    far = move(near, "pix", toward)
+    )(near1, edge_near, edge_far, beyond)
+    far1 = move(near1, "pix", toward)
+    far2 = move(near2, "pix", toward)
 
     pair, pair_link, pair_core = call(
         pair_rows_kernel,
         [f32(chans, 32, cols), f32(HALO, 32, cols), f32(HALO, 32, cols)],
         [pltpu.VMEM((chans, 48, cols), jnp.float32)],
-    )(cells, near, edge_far, edge_near)
+        micros=0.01,
+    )(cells1, cells2, near1, near2, edge_far, edge_near)
     pair_link = swap(pair_link, "chan", 1)
     pair_core = swap(pair_core, "chan", 0)
 
@@ -319,7 +331,8 @@
         far_rows_kernel,
         [f32(chans, 16, cols), f32(HALO, 16, cols), f32(HALO, 16, cols)],
         [pltpu.VMEM((chans, 32, cols), jnp.float32)],
-    )(far, edge, beyond)
+        micros=30.0,
+    )(far1, far2, edge, beyond)
     outer_link = swap(outer_link, "chan", 1)
     outer_core = swap(outer_core, "chan", 0)
 
@@ -335,7 +348,7 @@
             pltpu.VMEM((4, tiles, chans * 32, LANES), jnp.float32),
         ],
         vmem=24,
-        micros=4.0,
+        micros=0.01,
         in_specs=[VMEM, VMEM, VMEM, ANY],
     )(pair, pair_link, pair_core, outer)
     return call(

time: 52.6 us -> 55.2 us (1.049)
  the two profiles are of different devices: /device:TPU:34 before, /device:TPU:32 now
where the time goes in v3:
time: 55.2 us; the launch traced here: 54.8 us
  starting transfers between devices  24.6 us (45%)
  waiting for transfers between devices  16.1 us (29%)
  Pallas kernels  12.2 us (22%)
  local copies, waits for them, and re-layouts  1.8 us (3%)
    ppermute x11, starting transfers between devices, move(): lax.ppermute(value, axis, [(a, b) for a, b in pairs if 0 <= b < count])  24.6 us
    ppermute x11, waiting for transfers between devices, move(): lax.ppermute(value, axis, [(a, b) for a, b in pairs if 0 <= b < count])  16.1 us
    pallas_call x1, Pallas kernels, per_device(): call(snr_kernel, f32(4, chans, rows, cols), [pltpu.VMEM((44, 16, cols), j...  4.73 us
    pallas_call x1, Pallas kernels, per_device(): call(pair_noise_kernel, [f32(4, chans, rows, cols), f32(4, tiles, chans *...  4.38 us
    unnamed x6, local copies, waits for them, and re-layouts  1.8 us
    pallas_call x1, Pallas kernels, per_device(): call(pair_rows_kernel, [f32(chans, 32, cols), f32(HALO, 32, cols), f32(HA...  1.35 us
  transfers between devices with their start and end apart: 11, of which 5 were waited for; matrix products, arithmetic and copies ran while one was open for 0% of the time, Pallas kernels for 12%

profile of v3, /device:TPU:32, one launch (start us, length us, event | category | flops | bytes accessed | tf_op | source)
XLA Modules:
  0.0 54.8 jit_solution(12403153500223801203)
XLA Ops:
  0.0 0.0 copy-start
  0.0 1.0 %copy-done = f32[16,16,512]{2,1,0:T(8,128)S(1)} copy-done((f32[16,16,512]{2,1,0:T(8,128)S(1)}, f32[16,16,512]{2,1,0:T(8,128)}, u32[]{:S(2)}) %copy-start) | copy-done | bytes 524312
  1.0 0.0 copy-start.1
  1.0 0.8 %copy-done.1 = s32[16,512]{1,0:T(8,128)S(1)} copy-done((s32[16,512]{1,0:T(8,128)S(1)}, s32[16,512]{1,0:T(8,128)}, u32[]{:S(2)}) %copy-start.1) | copy-done | bytes 32792
  1.8 0.9 %shard_map.28 = (f32[16,16,256]{2,1,0:T(8,128)S(1)}, f32[16,16,256]{2,1,0:T(8,128)S(1)}, f32[3,16,512]{2,1,0:T(8,128)S(1)}, f32[3,16,512]{2,1,0:T(8,128)S(1)}) custom-call(f32[16,16,512]{2,1,0:T(8,128)S(1)} %copy-done, s32[16,512]{1,0:T(8,128)S(1)} %copy-done.1), custom_call_target="tpu_custom_call" | custom-call | flops 1000000000 | bytes 3000000 | tf_op jit(solution)/shard_map/pallas_call | solution.py:302
  2.7 3.1 %collective-permute-start = (f32[16,16,256]{2,1,0:T(8,128)S(1)}, f32[16,16,256]{2,1,0:T(8,128)S(1)}, u32[]{:S(2)}, u32[]{:S(2)}) collective-permute-start(f32[16,16,256]{2,1,0:T(8,128)S(1)} %get-tuple-element.18.cells1), channel_id=1, source_target_pairs={{0,16},{16,0},{32,48},{48,32},{64,80},{80,64},{96,112},{112,96},{1... | collective-permute-start | bytes 786440 | tf_op jit(solution)/shard_map/ppermute | solution.py:292
  5.8 0.6 %collective-permute-start.5 = (f32[16,16,256]{2,1,0:T(8,128)S(1)}, f32[16,16,256]{2,1,0:T(8,128)S(1)}, u32[]{:S(2)}, u32[]{:S(2)}) collective-permute-start(f32[16,16,256]{2,1,0:T(8,128)S(1)} %get-tuple-element.21.cells2), channel_id=1, source_target_pairs={{0,16},{16,0},{32,48},{48,32},{64,80},{80,64},{96,112},{112,96},{1... | collective-permute-start | bytes 786440 | tf_op jit(solution)/shard_map/ppermute | solution.py:292
  6.3 3.4 %collective-permute-start.3 = (f32[3,16,512]{2,1,0:T(8,128)S(1)}, f32[3,16,512]{2,1,0:T(8,128)S(1)}, u32[]{:S(2)}, u32[]{:S(2)}) collective-permute-start(f32[3,16,512]{2,1,0:T(8,128)S(1)} %get-tuple-element.20), channel_id=1, source_target_pairs={{0,32},{32,64},{48,16},{64,96},{80,48},{112,80},{1,33},{33,65},{49... | collective-permute-start | bytes 294920 | tf_op jit(solution)/shard_map/ppermute | solution.py:292
  9.7 0.7 %collective-permute-start.2 = (f32[3,16,512]{2,1,0:T(8,128)S(1)}, f32[3,16,512]{2,1,0:T(8,128)S(1)}, u32[]{:S(2)}, u32[]{:S(2)}) collective-permute-start(f32[3,16,512]{2,1,0:T(8,128)S(1)} %get-tuple-element.19.edge), channel_id=1, source_target_pairs={{16,32},{32,16},{48,64},{64,48},{80,96},{96,80},{17,33},{33,17},{4... | collective-permute-start | bytes 294920 | tf_op jit(solution)/shard_map/ppermute | solution.py:292
  10.4 1.3 %collective-permute-start.1 = (f32[3,16,512]{2,1,0:T(8,128)S(1)}, f32[3,16,512]{2,1,0:T(8,128)S(1)}, u32[]{:S(2)}, u32[]{:S(2)}) collective-permute-start(f32[3,16,512]{2,1,0:T(8,128)S(1)} %get-tuple-element.19.edge), channel_id=1, source_target_pairs={{16,48},{32,0},{48,80},{64,32},{80,112},{96,64},{17,49},{33,1},{49... | collective-permute-start | bytes 294920 | tf_op jit(solution)/shard_map/ppermute | solution.py:292
  11.7 0.2 collective-permute-done.3.rest_2_.beyond
  11.9 0.0 collective-permute-done.2.rest_1_.edge_far
  11.9 6.7 %collective-permute-done.1.rest_0_.edge_near = f32[3,16,512]{2,1,0:T(8,128)S(1)} collective-permute-done((f32[3,16,512]{2,1,0:T(8,128)S(1)}, f32[3,16,512]{2,1,0:T(8,128)S(1)}, u32[]{:S(2)}, u32[]{:S(2)}) %collective-permute-start.1) | collective-permute-done | bytes 98336 | tf_op jit(solution)/shard_map/ppermute | solution.py:292
  18.6 0.0 collective-permute-done.value
  18.6 4.5 %collective-permute-start.4 = (f32[16,16,256]{2,1,0:T(8,128)S(1)}, f32[16,16,256]{2,1,0:T(8,128)S(1)}, u32[]{:S(2)}, u32[]{:S(2)}) collective-permute-start(f32[16,16,256]{2,1,0:T(8,128)S(1)} %shard_map.29.near1), channel_id=1, source_target_pairs={{0,32},{32,64},{48,16},{64,96},{80,48},{112,80},{1,33},{33,65},{49... | collective-permute-start | bytes 786440 | tf_op jit(solution)/shard_map/ppermute | solution.py:292
  23.1 0.0 collective-permute-done.5.near2
  23.2 3.8 %collective-permute-start.6 = (f32[16,16,256]{2,1,0:T(8,128)S(1)}, f32[16,16,256]{2,1,0:T(8,128)S(1)}, u32[]{:S(2)}, u32[]{:S(2)}) collective-permute-start(f32[16,16,256]{2,1,0:T(8,128)S(1)} %collective-permute-done.5.near2), channel_id=1, source_target_pairs={{0,32},{32,64},{48,16},{64,96},{80,48},{112,80},{1,33},{33,65},{49... | collective-permute-start | bytes 786440 | tf_op jit(solution)/shard_map/ppermute | solution.py:292
  27.0 1.4 %shard_map.31 = (f32[16,32,512]{2,1,0:T(8,128)S(1)}, f32[14,32,512]{2,1,0:T(8,128)S(1)}, f32[14,32,512]{2,1,0:T(8,128)S(1)}) custom-call(f32[16,16,256]{2,1,0:T(8,128)S(1)} %get-tuple-element.18.cells1, f32[16,16,256]{2,1,0:T(8,128)S(1)} %get-tuple-element.21.cells2, f32[16,16,256]{2,1,0:T(8,128)S(1)} %shard_map.29.near1, ...), custom_call_target="tpu_custom_call" | custom-call | flops 10000000 | bytes 30000 | tf_op jit(solution)/shard_map/pallas_call | solution.py:321
  28.3 3.1 %collective-permute-start.9 = (f32[14,32,512]{2,1,0:T(8,128)S(1)}, f32[14,32,512]{2,1,0:T(8,128)S(1)}, u32[]{:S(2)}, u32[]{:S(2)}) collective-permute-start(f32[14,32,512]{2,1,0:T(8,128)S(1)} %get-tuple-element.26), channel_id=1, source_target_pairs={{1,2},{2,1},{3,4},{4,3},{5,6},{6,5},{7,8},{8,7},{9,10},{10,9},{11,... | collective-permute-start | bytes 2752520 | tf_op jit(solution)/shard_map/ppermute | solution.py:292
  31.4 0.6 %collective-permute-start.10 = (f32[14,32,512]{2,1,0:T(8,128)S(1)}, f32[14,32,512]{2,1,0:T(8,128)S(1)}, u32[]{:S(2)}, u32[]{:S(2)}) collective-permute-start(f32[14,32,512]{2,1,0:T(8,128)S(1)} %get-tuple-element.27), channel_id=1, source_target_pairs={{0,1},{1,0},{2,3},{3,2},{4,5},{5,4},{6,7},{7,6},{8,9},{9,8},{10,11... | collective-permute-start | bytes 2752520 | tf_op jit(solution)/shard_map/ppermute | solution.py:292
  32.0 0.0 collective-permute-done.4.far1
  32.0 1.5 %collective-permute-done.6.far2 = f32[16,16,256]{2,1,0:T(8,128)S(1)} collective-permute-done((f32[16,16,256]{2,1,0:T(8,128)S(1)}, f32[16,16,256]{2,1,0:T(8,128)S(1)}, u32[]{:S(2)}, u32[]{:S(2)}) %collective-permute-start.6) | collective-permute-done | bytes 262176 | tf_op jit(solution)/shard_map/ppermute | solution.py:292
  33.5 0.8 %shard_map.30 = (f32[16,16,512]{2,1,0:T(8,128)S(1)}, f32[14,16,512]{2,1,0:T(8,128)S(1)}, f32[14,16,512]{2,1,0:T(8,128)S(1)}) custom-call(f32[16,16,256]{2,1,0:T(8,128)S(1)} %collective-permute-done.4.far1, f32[16,16,256]{2,1,0:T(8,128)S(1)} %collective-permute-done.6.far2, f32[3,16,512]{2,1,0:T(8,128)S(1)} %get-tuple-element.19.edge, ...), custom_call_target="tpu_custom_call" | custom-call | flops 30000001024 | bytes 90000000 | tf_op jit(solution)/shard_map/pallas_call | solution.py:330
  34.3 0.0 copy-start.2
  34.3 3.1 %collective-permute-start.7 = (f32[14,16,512]{2,1,0:T(8,128)S(1)}, f32[14,16,512]{2,1,0:T(8,128)S(1)}, u32[]{:S(2)}, u32[]{:S(2)}) collective-permute-start(f32[14,16,512]{2,1,0:T(8,128)S(1)} %get-tuple-element.23), channel_id=1, source_target_pairs={{1,2},{2,1},{3,4},{4,3},{5,6},{6,5},{7,8},{8,7},{9,10},{10,9},{11,... | collective-permute-start | bytes 1376264 | tf_op jit(solution)/shard_map/ppermute | solution.py:292
  37.4 0.6 %collective-permute-start.8 = (f32[14,16,512]{2,1,0:T(8,128)S(1)}, f32[14,16,512]{2,1,0:T(8,128)S(1)}, u32[]{:S(2)}, u32[]{:S(2)}) collective-permute-start(f32[14,16,512]{2,1,0:T(8,128)S(1)} %get-tuple-element.24), channel_id=1, source_target_pairs={{0,1},{1,0},{2,3},{3,2},{4,5},{5,4},{6,7},{7,6},{8,9},{9,8},{10,11... | collective-permute-start | bytes 1376264 | tf_op jit(solution)/shard_map/ppermute | solution.py:292
  38.0 7.1 %collective-permute-done.9.link = f32[14,32,512]{2,1,0:T(8,128)S(1)} collective-permute-done((f32[14,32,512]{2,1,0:T(8,128)S(1)}, f32[14,32,512]{2,1,0:T(8,128)S(1)}, u32[]{:S(2)}, u32[]{:S(2)}) %collective-permute-start.9) | collective-permute-done | bytes 917536 | tf_op jit(solution)/shard_map/ppermute | solution.py:292
  45.1 0.0 collective-permute-done.10.core
  45.1 4.4 %shard_map.32 = (f32[4,16,16,512]{3,2,1,0:T(8,128)S(1)}, f32[4,4,256,128]{3,2,1,0:T(8,128)S(1)}, bf16[512,512]{1,0:T(8,128)(2,1)S(1)}) custom-call(f32[16,32,512]{2,1,0:T(8,128)S(1)} %get-tuple-element.25.own, f32[14,32,512]{2,1,0:T(8,128)S(1)} %collective-permute-done.9.link, f32[14,32,512]{2,1,0:T(8,128)S(1)} %collective-permute-done.10.core, ...), custom_call_target="tpu_custom_call" | custom-call | flops 10000000 | bytes 30000 | tf_op jit(solution)/shard_map/pallas_call | solution.py:339
  49.5 0.5 collective-permute-done.7.link
  50.1 0.0 collective-permute-done.8.core
  50.1 0.0 copy-done.2
  50.1 4.7 %shard_map.33 = f32[4,16,16,512]{3,2,1,0:T(8,128)} custom-call(f32[16,16,512]{2,1,0:T(8,128)S(1)} %get-tuple-element.22.after.own, f32[14,16,512]{2,1,0:T(8,128)S(1)} %collective-permute-done.7.link, f32[14,16,512]{2,1,0:T(8,128)S(1)} %collective-permute-done.8.core, f32[4,4,256,128]{3,2,1,0:T(8,128)S(1)} %get-tuple-element.28.part, ...), custom_call_target="tpu_custom_call" | custom-call | flops 4000000000 | bytes 12000000 | tf_op jit(solution)/shard_map/pallas_call | solution.py:354
  (1 shorter events, 0.0 us)
Async XLA Ops:
  0.0 1.0 %copy-start = (f32[16,16,512]{2,1,0:T(8,128)S(1)}, f32[16,16,512]{2,1,0:T(8,128)}, u32[]{:S(2)}) copy-start(f32[16,16,512]{2,1,0:T(8,128)} %data.1) | copy-start | bytes 1572868
  1.0 0.8 %copy-start.1 = (s32[16,512]{1,0:T(8,128)S(1)}, s32[16,512]{1,0:T(8,128)}, u32[]{:S(2)}) copy-start(s32[16,512]{1,0:T(8,128)} %blanked.3) | copy-start | bytes 98308
  2.7 15.9 %collective-permute-start = (f32[16,16,256]{2,1,0:T(8,128)S(1)}, f32[16,16,256]{2,1,0:T(8,128)S(1)}, u32[]{:S(2)}, u32[]{:S(2)}) collective-permute-start(f32[16,16,256]{2,1,0:T(8,128)S(1)} %get-tuple-element.18.cells1), channel_id=1, source_target_pairs={{0,16},{16,0},{32,48},{48,32},{64,80},{80,64},{96,112},{112,96},{1... | collective-permute-start | bytes 786440 | tf_op jit(solution)/shard_map/ppermute | solution.py:292
  5.8 17.4 %collective-permute-start.5 = (f32[16,16,256]{2,1,0:T(8,128)S(1)}, f32[16,16,256]{2,1,0:T(8,128)S(1)}, u32[]{:S(2)}, u32[]{:S(2)}) collective-permute-start(f32[16,16,256]{2,1,0:T(8,128)S(1)} %get-tuple-element.21.cells2), channel_id=1, source_target_pairs={{0,16},{16,0},{32,48},{48,32},{64,80},{80,64},{96,112},{112,96},{1... | collective-permute-start | bytes 786440 | tf_op jit(solution)/shard_map/ppermute | solution.py:292
  6.3 5.6 %collective-permute-start.3 = (f32[3,16,512]{2,1,0:T(8,128)S(1)}, f32[3,16,512]{2,1,0:T(8,128)S(1)}, u32[]{:S(2)}, u32[]{:S(2)}) collective-permute-start(f32[3,16,512]{2,1,0:T(8,128)S(1)} %get-tuple-element.20), channel_id=1, source_target_pairs={{0,32},{32,64},{48,16},{64,96},{80,48},{112,80},{1,33},{33,65},{49... | collective-permute-start | bytes 294920 | tf_op jit(solution)/shard_map/ppermute | solution.py:292
  9.7 2.2 %collective-permute-start.2 = (f32[3,16,512]{2,1,0:T(8,128)S(1)}, f32[3,16,512]{2,1,0:T(8,128)S(1)}, u32[]{:S(2)}, u32[]{:S(2)}) collective-permute-start(f32[3,16,512]{2,1,0:T(8,128)S(1)} %get-tuple-element.19.edge), channel_id=1, source_target_pairs={{16,32},{32,16},{48,64},{64,48},{80,96},{96,80},{17,33},{33,17},{4... | collective-permute-start | bytes 294920 | tf_op jit(solution)/shard_map/ppermute | solution.py:292
  10.4 8.2 %collective-permute-start.1 = (f32[3,16,512]{2,1,0:T(8,128)S(1)}, f32[3,16,512]{2,1,0:T(8,128)S(1)}, u32[]{:S(2)}, u32[]{:S(2)}) collective-permute-start(f32[3,16,512]{2,1,0:T(8,128)S(1)} %get-tuple-element.19.edge), channel_id=1, source_target_pairs={{16,48},{32,0},{48,80},{64,32},{80,112},{96,64},{17,49},{33,1},{49... | collective-permute-start | bytes 294920 | tf_op jit(solution)/shard_map/ppermute | solution.py:292
  18.6 13.4 %collective-permute-start.4 = (f32[16,16,256]{2,1,0:T(8,128)S(1)}, f32[16,16,256]{2,1,0:T(8,128)S(1)}, u32[]{:S(2)}, u32[]{:S(2)}) collective-permute-start(f32[16,16,256]{2,1,0:T(8,128)S(1)} %shard_map.29.near1), channel_id=1, source_target_pairs={{0,32},{32,64},{48,16},{64,96},{80,48},{112,80},{1,33},{33,65},{49... | collective-permute-start | bytes 786440 | tf_op jit(solution)/shard_map/ppermute | solution.py:292
  23.2 10.3 %collective-permute-start.6 = (f32[16,16,256]{2,1,0:T(8,128)S(1)}, f32[16,16,256]{2,1,0:T(8,128)S(1)}, u32[]{:S(2)}, u32[]{:S(2)}) collective-permute-start(f32[16,16,256]{2,1,0:T(8,128)S(1)} %collective-permute-done.5.near2), channel_id=1, source_target_pairs={{0,32},{32,64},{48,16},{64,96},{80,48},{112,80},{1,33},{33,65},{49... | collective-permute-start | bytes 786440 | tf_op jit(solution)/shard_map/ppermute | solution.py:292
  28.3 16.8 %collective-permute-start.9 = (f32[14,32,512]{2,1,0:T(8,128)S(1)}, f32[14,32,512]{2,1,0:T(8,128)S(1)}, u32[]{:S(2)}, u32[]{:S(2)}) collective-permute-start(f32[14,32,512]{2,1,0:T(8,128)S(1)} %get-tuple-element.26), channel_id=1, source_target_pairs={{1,2},{2,1},{3,4},{4,3},{5,6},{6,5},{7,8},{8,7},{9,10},{10,9},{11,... | collective-permute-start | bytes 2752520 | tf_op jit(solution)/shard_map/ppermute | solution.py:292
  31.4 13.7 %collective-permute-start.10 = (f32[14,32,512]{2,1,0:T(8,128)S(1)}, f32[14,32,512]{2,1,0:T(8,128)S(1)}, u32[]{:S(2)}, u32[]{:S(2)}) collective-permute-start(f32[14,32,512]{2,1,0:T(8,128)S(1)} %get-tuple-element.27), channel_id=1, source_target_pairs={{0,1},{1,0},{2,3},{3,2},{4,5},{5,4},{6,7},{7,6},{8,9},{9,8},{10,11... | collective-permute-start | bytes 2752520 | tf_op jit(solution)/shard_map/ppermute | solution.py:292
  34.3 15.8 %copy-start.2 = (s32[16,512]{1,0:T(8,128)S(1)}, s32[16,512]{1,0:T(8,128)}, u32[]{:S(2)}) copy-start(s32[16,512]{1,0:T(8,128)} %blanked.3) | copy-start | bytes 98308
  34.3 15.8 %collective-permute-start.7 = (f32[14,16,512]{2,1,0:T(8,128)S(1)}, f32[14,16,512]{2,1,0:T(8,128)S(1)}, u32[]{:S(2)}, u32[]{:S(2)}) collective-permute-start(f32[14,16,512]{2,1,0:T(8,128)S(1)} %get-tuple-element.23), channel_id=1, source_target_pairs={{1,2},{2,1},{3,4},{4,3},{5,6},{6,5},{7,8},{8,7},{9,10},{10,9},{11,... | collective-permute-start | bytes 1376264 | tf_op jit(solution)/shard_map/ppermute | solution.py:292
  37.4 12.7 %collective-permute-start.8 = (f32[14,16,512]{2,1,0:T(8,128)S(1)}, f32[14,16,512]{2,1,0:T(8,128)S(1)}, u32[]{:S(2)}, u32[]{:S(2)}) collective-permute-start(f32[14,16,512]{2,1,0:T(8,128)S(1)} %get-tuple-element.24), channel_id=1, source_target_pairs={{0,1},{1,0},{2,3},{3,2},{4,5},{5,4},{6,7},{7,6},{8,9},{9,8},{10,11... | collective-permute-start | bytes 1376264 | tf_op jit(solution)/shard_map/ppermute | solution.py:292

commit v4 on v2

--- a/solution.py
+++ b/solution.py
@@ -118,67 +118,93 @@
     send_halos(full, link, core)
 
 
-def gather_channels(link, core, field):
+def channel_pass(own, halo, down, row, tile, energy, before, boxes, kept_at):
+    chans = own.shape[0]
+    stride = energy.shape[2] // chans
+    at, count = lax.axis_index("chan"), lax.axis_size("chan")
+    there = (at > 0 if down else at < count - 1).astype(jnp.float32)
+    lanes = pl.ds(pl.multiple_of(tile * LANES, LANES), LANES)
+    here = (pl.ds(pl.multiple_of(row, 8), 8), lanes)
+
+    def s(j):
+        if down and j < HALO:
+            return halo[(j,) + here]
+        if not down and j >= HALO + chans:
+            return halo[(j - HALO - chans,) + here]
+        return own[(j - HALO,) + here]
+
+    step, first = (-1, 28) if down else (1, 15)
+    one, three, seven = {}, {}, {}
+    runs = [None] * 4
+    for n in range(29):
+        j = first + step * n
+        one[j] = s(j)
+        a = j - step
+        if n >= 2:
+            three[a] = one[a - 1] + one[a] + one[a + 1]
+        b = j - 3 * step
+        if n >= 6:
+            seven[b] = three[b - 2] + three[b + 2] + one[b]
+        if n < 14:
+            continue
+        j -= 7 * step
+        fifteen = seven[j - 4] + seven[j + 4] + one[j]
+        k = j - 7
+        c = k if down else k - 14
+        for w, box in enumerate((one[j], three[j], seven[j], fifteen)):
+            if kept_at is not None and 7 <= k < 23:
+                at_rows = pl.ds(pl.multiple_of(kept_at, 8), 8)
+                boxes[w, k - 7 if down else k - 15, at_rows, lanes] = box
+            square = box * box
+            if k < 7 or k >= 23:
+                square = square * there
+            runs[w] = square if runs[w] is None else runs[w] + square
+            at_c = (w, tile, pl.ds(pl.multiple_of(c * stride + row, 8), 8), slice(None))
+            if before is not None and 1 <= c <= 14:
+                energy[at_c] = before[at_c] + runs[w]
+            else:
+                energy[at_c] = runs[w]
+    if before is not None:
+        c = 15 if down else 0
+        for w in range(4):
+            at_c = (w, tile, pl.ds(pl.multiple_of(c * stride + row, 8), 8), slice(None))
+            energy[at_c] = before[at_c]
+
+
+def strips(own, halo, core_side, energy, before, boxes):
+    chans, tall, cols = own.shape
     odd = odd_of("chan")
-    field[pl.ds(30 * odd, HALO)] = link[...]
-    field[pl.ds(30 * (1 - odd), HALO)] = core[...]
-
-
-def channel_sums(field, own, row, tile, energy, boxes, kept_at):
-    chans, tall = own.shape[:2]
-    at, count = lax.axis_index("chan"), lax.axis_size("chan")
-    has_below = (at > 0).astype(jnp.float32)
-    has_above = (at < count - 1).astype(jnp.float32)
-    here = (pl.ds(pl.multiple_of(row, 8), 8), pl.ds(tile * LANES, LANES))
-
-    def s(j):
-        if HALO <= j < HALO + chans:
-            return own[(j - HALO,) + here]
-        return field[(j,) + here]
-
-    def put(w, c, value):
-        energy[w, tile, pl.ds(pl.multiple_of(c * tall + row, 8), 8), :] = value
-
-    def get(w, c):
-        return energy[w, tile, pl.ds(pl.multiple_of(c * tall + row, 8), 8), :]
-
-    for step, first in ((-1, 28), (1, 15)):
-        one, three, seven = {}, {}, {}
-        runs = [None] * 4
-        for n in range(29):
-            j = first + step * n
-            one[j] = s(j)
-            a = j - step
-            if n >= 2:
-                three[a] = one[a - 1] + one[a] + one[a + 1]
-            b = j - 3 * step
-            if n >= 6:
-                seven[b] = three[b - 2] + three[b + 2] + one[b]
-            if n < 14:
-                continue
-            j -= 7 * step
-            fifteen = seven[j - 4] + seven[j + 4] + one[j]
-            k = j - 7
-            for w, box in enumerate((one[j], three[j], seven[j], fifteen)):
-                if kept_at is not None and 7 <= k < 23:
-                    rows_at = pl.ds(pl.multiple_of(kept_at, 8), 8)
-                    boxes[w, k - 7, rows_at, here[1]] = box
-                square = box * box
-                if k < 7:
-                    square = square * has_below
-                if k >= 23:
-                    square = square * has_above
-                runs[w] = square if runs[w] is None else runs[w] + square
-                if step < 0:
-                    put(w, k, runs[w])
-                elif k < 29:
-                    put(w, k - 14, get(w, k - 14) + runs[w])
-                else:
-                    put(w, k - 14, runs[w])
+    tiles = cols // LANES
+    own_row = 16 * odd_of("pix")
+
+    def run(down):
+        def both(n, carry):
+            tile, i = n // 2, n % 2
+            if tall == 32:
+                channel_pass(own, halo, down, own_row + 8 * i, tile, energy, before, boxes, 8 * i)
+                channel_pass(own, halo, down, 16 - own_row + 8 * i, tile, energy, before, None, None)
+            else:
+                channel_pass(own, halo, down, 8 * i, tile, energy, before, None, None)
+            return carry
+
+        lax.fori_loop(0, 2 * tiles, both, 0)
+
+    pl.when(odd == 0)(lambda: run(not core_side))
+    pl.when(odd == 1)(lambda: run(core_side))
+
+
+def pair_core_kernel(own, core, after, energy, boxes):
+    strips(own, core, True, energy, None, boxes)
+
+
+def far_core_kernel(own, core, after, energy):
+    strips(own, core, True, energy, None, None)
 
 
 def two_terms(sums, w):
-    value = jnp.concatenate([sums[w, tile] for tile in range(sums.shape[1])], axis=1)
+    tiles, height = sums.shape[1:3]
+    value = jnp.concatenate([sums[w, tile] for tile in range(tiles)], axis=1)
+    value = value.reshape(16, height // 16, tiles * LANES)[:, :16].reshape(256, tiles * LANES)
     first = value.astype(jnp.bfloat16)
     second = (value - first.astype(jnp.float32)).astype(jnp.bfloat16)
     return jnp.concatenate([first, second], axis=1)
@@ -196,26 +222,24 @@
     pl.when(odd == 1)(lambda: loop(False))
 
 
-def pair_noise_kernel(own, link, core, after, boxes, sums, band, field, energy):
+def pair_noise_kernel(own, link, before, core_boxes, after, boxes, sums, band, link_boxes, energy):
     chans, tall, cols = own.shape
     rows = tall // 2
     odd = odd_of("pix")
-    gather_channels(link, core, field)
-    for tile in range(cols // LANES):
-
-        def strips(i, carry):
-            channel_sums(field, own, 8 * i + rows * odd, tile, energy, boxes, 8 * i)
-            channel_sums(field, own, 8 * i + rows * (1 - odd), tile, energy, None, None)
-            return carry
-
-        lax.fori_loop(0, 2, strips, 0)
+    strips(own, link, False, energy, before, link_boxes)
+    low = pl.ds(8 * odd_of("chan"), 8)
+    high = pl.ds(8 - 8 * odd_of("chan"), 8)
+    boxes[:, low] = link_boxes[...]
+    boxes[:, high] = core_boxes[...]
+
+    stride = energy.shape[2] // chans
 
     def row_windows(w, even):
         for half in range(2):
             for tile in range(cols // LANES):
 
                 def e(i):
-                    return energy[w, tile, pl.ds(half * 8 * tall + i, 8, stride=tall), :]
+                    return energy[w, tile, pl.ds(half * 8 * stride + i, 8, stride=stride), :]
 
                 first = 0 if even else rows
                 run = e(first)
@@ -224,8 +248,7 @@
                 for d in range(rows):
                     if d > 0:
                         run = run + e(15 + d if even else 16 - d)
-                    row = d if even else 15 - d
-                    sums[w, tile, pl.ds(half * 8 * rows + row, 8, stride=rows), :] = run
+                    sums[w, tile, half, d if even else 15 - d] = run
 
     for_parity(odd, row_windows)
     apart = lax.broadcasted_iota(jnp.int32, (cols, cols), 0) - lax.broadcasted_iota(
@@ -235,18 +258,13 @@
 
 
 def snr_kernel(
-    own, link, core, part, band, boxes, blanked, out, field, energy, sums, ready, sems
+    own, link, before, part, band, boxes, blanked, out, energy, sums, ready, sems
 ):
     chans, rows, cols = own.shape
     odd = odd_of("pix")
-    gather_channels(link, core, field)
-    for tile in range(cols // LANES):
-
-        def strips(i, carry):
-            channel_sums(field, own, 8 * i, tile, energy, None, None)
-            return carry
-
-        lax.fori_loop(0, 2, strips, 0)
+    strips(own, link, False, energy, before, None)
+
+    stride = energy.shape[2] // chans
 
     def row_windows(w, even):
         for half in range(2):
@@ -255,11 +273,12 @@
                 for d in range(rows):
                     if d > 0:
                         i = 16 - d if even else d - 1
-                        e = energy[w, tile, pl.ds(half * 8 * rows + i, 8, stride=rows), :]
+                        e = energy[w, tile, pl.ds(half * 8 * stride + i, 8, stride=stride), :]
                         run = e if run is None else run + e
                     row = 15 - d if even else d
-                    at = (w, tile, pl.ds(half * 8 * rows + row, 8, stride=rows), slice(None))
-                    sums[at] = part[at] if run is None else part[at] + run
+                    value = part[w, tile, half, row]
+                    at = pl.ds(half * 8 * stride + row, 8, stride=stride)
+                    sums[w, tile, at, :] = value if run is None else value + run
 
     for_parity(odd, row_windows)
     kept = (1 - blanked[...]).astype(jnp.float32)
@@ -323,35 +342,43 @@
     outer_link = swap(outer_link, "chan", 1)
     outer_core = swap(outer_core, "chan", 0)
 
+    pair_energy, core_boxes = call(
+        pair_core_kernel,
+        [f32(4, tiles, chans * 40, LANES), f32(4, chans // 2, rows, cols)],
+        micros=2.0,
+        in_specs=[VMEM, VMEM, ANY],
+    )(pair, pair_core, outer)
     boxes, part, band = call(
         pair_noise_kernel,
         [
             f32(4, chans, rows, cols),
-            f32(4, tiles, chans * rows, LANES),
+            f32(4, tiles, 2, rows, chans // 2, LANES),
             jax.ShapeDtypeStruct((cols, cols), jnp.bfloat16),
         ],
         [
-            pltpu.VMEM((44, 32, cols), jnp.float32),
-            pltpu.VMEM((4, tiles, chans * 32, LANES), jnp.float32),
+            pltpu.VMEM((4, chans // 2, rows, cols), jnp.float32),
+            pltpu.VMEM((4, tiles, chans * 40, LANES), jnp.float32),
         ],
-        vmem=24,
-        micros=4.0,
-        in_specs=[VMEM, VMEM, VMEM, ANY],
-    )(pair, pair_link, pair_core, outer)
+        micros=3.0,
+        in_specs=[VMEM, VMEM, VMEM, VMEM, ANY],
+    )(pair, pair_link, pair_energy, core_boxes, outer)
+    far_energy = call(
+        far_core_kernel,
+        f32(4, tiles, chans * 24, LANES),
+        in_specs=[VMEM, VMEM, ANY],
+    )(outer, outer_core, part)
     return call(
         snr_kernel,
         f32(4, chans, rows, cols),
         [
-            pltpu.VMEM((44, 16, cols), jnp.float32),
-            pltpu.VMEM((4, tiles, chans * rows, LANES), jnp.float32),
-            pltpu.VMEM((4, tiles, chans * rows, LANES), jnp.float32),
+            pltpu.VMEM((4, tiles, chans * 24, LANES), jnp.float32),
+            pltpu.VMEM((4, tiles, chans * 24, LANES), jnp.float32),
             pltpu.VMEM((4, chans, rows, cols), jnp.float32),
             pltpu.SemaphoreType.DMA((4,)),
         ],
-        vmem=24,
         micros=4.0,
         out_specs=ANY,
-    )(outer, outer_link, outer_core, part, band, boxes, blanked)
+    )(outer, outer_link, far_energy, part, band, boxes, blanked)
 
 
 def solution(mesh):

time: 52.6 us -> 53 us (level)
  the two profiles are of different devices: /device:TPU:34 before, /device:TPU:29 now
where the time goes in v4:
time: 53 us; the launch traced here: 52.6 us
  starting transfers between devices  22.1 us (42%)
  waiting for transfers between devices  18.7 us (35%)
  Pallas kernels  9.86 us (19%)
  local copies, waits for them, and re-layouts  1.8 us (3%)
    ppermute x9, starting transfers between devices, move(): lax.ppermute(value, axis, [(a, b) for a, b in pairs if 0 <= b < count])  22.1 us
    ppermute x9, waiting for transfers between devices, move(): lax.ppermute(value, axis, [(a, b) for a, b in pairs if 0 <= b < count])  18.7 us
    pallas_call x1, Pallas kernels, per_device(): call(snr_kernel, f32(4, chans, rows, cols), [pltpu.VMEM((4, tiles, chans...  3.43 us
    pallas_call x1, Pallas kernels, per_device(): call(pair_noise_kernel, [f32(4, chans, rows, cols), f32(4, tiles, 2, rows...  1.94 us
    unnamed x6, local copies, waits for them, and re-layouts  1.8 us
    pallas_call x1, Pallas kernels, per_device(): call(pair_rows_kernel, [f32(chans, 32, cols), f32(HALO, 32, cols), f32(HA...  1.35 us
  transfers between devices with their start and end apart: 9, of which 5 were waited for; matrix products, arithmetic and copies ran while one was open for 0% of the time, Pallas kernels for 11%

profile of v4, /device:TPU:29, one launch (start us, length us, event | category | flops | bytes accessed | tf_op | source)
XLA Modules:
  0.0 52.6 jit_solution(12604298369272329793)
XLA Ops:
  0.0 0.0 copy-start
  0.0 1.0 %copy-done = f32[16,16,512]{2,1,0:T(8,128)S(1)} copy-done((f32[16,16,512]{2,1,0:T(8,128)S(1)}, f32[16,16,512]{2,1,0:T(8,128)}, u32[]{:S(2)}) %copy-start) | copy-done | bytes 524312
  1.0 0.0 copy-start.1
  1.0 0.8 %copy-done.1 = s32[16,512]{1,0:T(8,128)S(1)} copy-done((s32[16,512]{1,0:T(8,128)S(1)}, s32[16,512]{1,0:T(8,128)}, u32[]{:S(2)}) %copy-start.1) | copy-done | bytes 32792
  1.8 0.9 %shard_map.28 = (f32[16,16,512]{2,1,0:T(8,128)S(1)}, f32[3,16,512]{2,1,0:T(8,128)S(1)}, f32[3,16,512]{2,1,0:T(8,128)S(1)}) custom-call(f32[16,16,512]{2,1,0:T(8,128)S(1)} %copy-done, s32[16,512]{1,0:T(8,128)S(1)} %copy-done.1), custom_call_target="tpu_custom_call" | custom-call | bytes 3000000 | tf_op jit(solution)/shard_map/pallas_call | solution.py:313
  2.7 3.7 %collective-permute-start = (f32[16,16,512]{2,1,0:T(8,128)S(1)}, f32[16,16,512]{2,1,0:T(8,128)S(1)}, u32[]{:S(2)}, u32[]{:S(2)}) collective-permute-start(f32[16,16,512]{2,1,0:T(8,128)S(1)} %get-tuple-element.19.cells), channel_id=1, source_target_pairs={{0,16},{16,0},{32,48},{48,32},{64,80},{80,64},{96,112},{112,96},{1... | collective-permute-start | bytes 1572872 | tf_op jit(solution)/shard_map/ppermute | solution.py:304
  6.4 2.8 %collective-permute-start.3 = (f32[3,16,512]{2,1,0:T(8,128)S(1)}, f32[3,16,512]{2,1,0:T(8,128)S(1)}, u32[]{:S(2)}, u32[]{:S(2)}) collective-permute-start(f32[3,16,512]{2,1,0:T(8,128)S(1)} %get-tuple-element.21), channel_id=1, source_target_pairs={{0,32},{32,64},{48,16},{64,96},{80,48},{112,80},{1,33},{33,65},{49... | collective-permute-start | bytes 294920 | tf_op jit(solution)/shard_map/ppermute | solution.py:304
  9.2 1.9 %collective-permute-start.2 = (f32[3,16,512]{2,1,0:T(8,128)S(1)}, f32[3,16,512]{2,1,0:T(8,128)S(1)}, u32[]{:S(2)}, u32[]{:S(2)}) collective-permute-start(f32[3,16,512]{2,1,0:T(8,128)S(1)} %get-tuple-element.20.edge), channel_id=1, source_target_pairs={{16,32},{32,16},{48,64},{64,48},{80,96},{96,80},{17,33},{33,17},{4... | collective-permute-start | bytes 294920 | tf_op jit(solution)/shard_map/ppermute | solution.py:304
  11.1 2.5 %collective-permute-start.1 = (f32[3,16,512]{2,1,0:T(8,128)S(1)}, f32[3,16,512]{2,1,0:T(8,128)S(1)}, u32[]{:S(2)}, u32[]{:S(2)}) collective-permute-start(f32[3,16,512]{2,1,0:T(8,128)S(1)} %get-tuple-element.20.edge), channel_id=1, source_target_pairs={{16,48},{32,0},{48,80},{64,32},{80,112},{96,64},{17,49},{33,1},{49... | collective-permute-start | bytes 294920 | tf_op jit(solution)/shard_map/ppermute | solution.py:304
  13.6 0.0 collective-permute-done.3.rest_2_.beyond
  13.6 3.5 %collective-permute-done.2.rest_1_.edge_far = f32[3,16,512]{2,1,0:T(8,128)S(1)} collective-permute-done((f32[3,16,512]{2,1,0:T(8,128)S(1)}, f32[3,16,512]{2,1,0:T(8,128)S(1)}, u32[]{:S(2)}, u32[]{:S(2)}) %collective-permute-start.2) | collective-permute-done | bytes 98336 | tf_op jit(solution)/shard_map/ppermute | solution.py:304
  17.1 0.0 collective-permute-done.1.rest_0_.edge_near
  17.1 3.1 %collective-permute-done.value = f32[16,16,512]{2,1,0:T(8,128)S(1)} collective-permute-done((f32[16,16,512]{2,1,0:T(8,128)S(1)}, f32[16,16,512]{2,1,0:T(8,128)S(1)}, u32[]{:S(2)}, u32[]{:S(2)}) %collective-permute-start) | collective-permute-done | bytes 524320 | tf_op jit(solution)/shard_map/ppermute | solution.py:304
  20.1 2.8 %collective-permute-start.4 = (f32[16,16,512]{2,1,0:T(8,128)S(1)}, f32[16,16,512]{2,1,0:T(8,128)S(1)}, u32[]{:S(2)}, u32[]{:S(2)}) collective-permute-start(f32[16,16,512]{2,1,0:T(8,128)S(1)} %shard_map.29.near), channel_id=1, source_target_pairs={{0,32},{32,64},{48,16},{64,96},{80,48},{112,80},{1,33},{33,65},{49... | collective-permute-start | bytes 1572872 | tf_op jit(solution)/shard_map/ppermute | solution.py:304
  23.0 1.4 %shard_map.31 = (f32[16,32,512]{2,1,0:T(8,128)S(1)}, f32[14,32,512]{2,1,0:T(8,128)S(1)}, f32[14,32,512]{2,1,0:T(8,128)S(1)}) custom-call(f32[16,16,512]{2,1,0:T(8,128)S(1)} %get-tuple-element.19.cells, f32[16,16,512]{2,1,0:T(8,128)S(1)} %shard_map.29.near, f32[3,16,512]{2,1,0:T(8,128)S(1)} %collective-permute-done.2.rest_1_.edge_far, ...), custom_call_target="tpu_custom_call" | custom-call | bytes 3000000 | tf_op jit(solution)/shard_map/pallas_call | solution.py:329
  24.3 1.6 %collective-permute-start.8 = (f32[14,32,512]{2,1,0:T(8,128)S(1)}, f32[14,32,512]{2,1,0:T(8,128)S(1)}, u32[]{:S(2)}, u32[]{:S(2)}) collective-permute-start(f32[14,32,512]{2,1,0:T(8,128)S(1)} %get-tuple-element.27), channel_id=1, source_target_pairs={{0,1},{1,0},{2,3},{3,2},{4,5},{5,4},{6,7},{7,6},{8,9},{9,8},{10,11... | collective-permute-start | bytes 2752520 | tf_op jit(solution)/shard_map/ppermute | solution.py:304
  25.9 2.5 %collective-permute-start.7 = (f32[14,32,512]{2,1,0:T(8,128)S(1)}, f32[14,32,512]{2,1,0:T(8,128)S(1)}, u32[]{:S(2)}, u32[]{:S(2)}) collective-permute-start(f32[14,32,512]{2,1,0:T(8,128)S(1)} %get-tuple-element.26), channel_id=1, source_target_pairs={{1,2},{2,1},{3,4},{4,3},{5,6},{6,5},{7,8},{8,7},{9,10},{10,9},{11,... | collective-permute-start | bytes 2752520 | tf_op jit(solution)/shard_map/ppermute | solution.py:304
  28.4 5.8 %collective-permute-done.4.far = f32[16,16,512]{2,1,0:T(8,128)S(1)} collective-permute-done((f32[16,16,512]{2,1,0:T(8,128)S(1)}, f32[16,16,512]{2,1,0:T(8,128)S(1)}, u32[]{:S(2)}, u32[]{:S(2)}) %collective-permute-start.4) | collective-permute-done | bytes 524320 | tf_op jit(solution)/shard_map/ppermute | solution.py:304
  34.2 0.8 %shard_map.30 = (f32[16,16,512]{2,1,0:T(8,128)S(1)}, f32[14,16,512]{2,1,0:T(8,128)S(1)}, f32[14,16,512]{2,1,0:T(8,128)S(1)}) custom-call(f32[16,16,512]{2,1,0:T(8,128)S(1)} %collective-permute-done.4.far, f32[3,16,512]{2,1,0:T(8,128)S(1)} %get-tuple-element.20.edge, f32[3,16,512]{2,1,0:T(8,128)S(1)} %collective-permute-done.3.rest_2_.beyond), custom_call_target="tpu_custom_call" | custom-call | bytes 3000000 | tf_op jit(solution)/shard_map/pallas_call | solution.py:337
  35.0 2.2 %collective-permute-start.6 = (f32[14,16,512]{2,1,0:T(8,128)S(1)}, f32[14,16,512]{2,1,0:T(8,128)S(1)}, u32[]{:S(2)}, u32[]{:S(2)}) collective-permute-start(f32[14,16,512]{2,1,0:T(8,128)S(1)} %get-tuple-element.24), channel_id=1, source_target_pairs={{0,1},{1,0},{2,3},{3,2},{4,5},{5,4},{6,7},{7,6},{8,9},{9,8},{10,11... | collective-permute-start | bytes 1376264 | tf_op jit(solution)/shard_map/ppermute | solution.py:304
  37.3 2.2 %collective-permute-start.5 = (f32[14,16,512]{2,1,0:T(8,128)S(1)}, f32[14,16,512]{2,1,0:T(8,128)S(1)}, u32[]{:S(2)}, u32[]{:S(2)}) collective-permute-start(f32[14,16,512]{2,1,0:T(8,128)S(1)} %get-tuple-element.23), channel_id=1, source_target_pairs={{1,2},{2,1},{3,4},{4,3},{5,6},{6,5},{7,8},{8,7},{9,10},{10,9},{11,... | collective-permute-start | bytes 1376264 | tf_op jit(solution)/shard_map/ppermute | solution.py:304
  39.4 0.0 collective-permute-done.8.core
  39.4 0.9 %shard_map.32 = (f32[4,4,640,128]{3,2,1,0:T(8,128)S(1)}, f32[4,8,16,512]{3,2,1,0:T(8,128)S(1)}) custom-call(f32[16,32,512]{2,1,0:T(8,128)S(1)} %get-tuple-element.25.own, f32[14,32,512]{2,1,0:T(8,128)S(1)} %collective-permute-done.8.core, f32[16,16,512]{2,1,0:T(8,128)S(1)} %get-tuple-element.22.after.own), custom_call_target="tpu_custom_call" | custom-call | bytes 6000000 | tf_op jit(solution)/shard_map/pallas_call | solution.py:345
  40.4 2.4 %collective-permute-done.7.link = f32[14,32,512]{2,1,0:T(8,128)S(1)} collective-permute-done((f32[14,32,512]{2,1,0:T(8,128)S(1)}, f32[14,32,512]{2,1,0:T(8,128)S(1)}, u32[]{:S(2)}, u32[]{:S(2)}) %collective-permute-start.7) | collective-permute-done | bytes 917536 | tf_op jit(solution)/shard_map/ppermute | solution.py:304
  42.7 1.9 %shard_map.33 = (f32[4,16,16,512]{3,2,1,0:T(8,128)S(1)}, f32[4,4,2,16,8,128]{5,4,3,2,1,0:T(8,128)S(1)}, bf16[512,512]{1,0:T(8,128)(2,1)S(1)}) custom-call(f32[16,32,512]{2,1,0:T(8,128)S(1)} %get-tuple-element.25.own, f32[14,32,512]{2,1,0:T(8,128)S(1)} %collective-permute-done.7.link, f32[4,4,640,128]{3,2,1,0:T(8,128)S(1)} %get-tuple-element.28.before, ...), custom_call_target="tpu_custom_call" | custom-call | bytes 9000000 | tf_op jit(solution)/shard_map/pallas_call | solution.py:351
  44.7 0.0 collective-permute-done.6.core
  44.7 0.0 copy-start.2
  44.7 0.5 shard_map.34.before
  45.2 4.0 %collective-permute-done.5.link = f32[14,16,512]{2,1,0:T(8,128)S(1)} collective-permute-done((f32[14,16,512]{2,1,0:T(8,128)S(1)}, f32[14,16,512]{2,1,0:T(8,128)S(1)}, u32[]{:S(2)}, u32[]{:S(2)}) %collective-permute-start.5) | collective-permute-done | bytes 458784 | tf_op jit(solution)/shard_map/ppermute | solution.py:304
  49.2 0.0 copy-done.2
  49.2 3.4 %shard_map.35 = f32[4,16,16,512]{3,2,1,0:T(8,128)} custom-call(f32[16,16,512]{2,1,0:T(8,128)S(1)} %get-tuple-element.22.after.own, f32[14,16,512]{2,1,0:T(8,128)S(1)} %collective-permute-done.5.link, f32[4,4,384,128]{3,2,1,0:T(8,128)S(1)} %shard_map.34.before, f32[4,4,2,16,8,128]{5,4,3,2,1,0:T(8,128)S(1)} %get-tuple-element.30.after.part, ...), custom_call_target="tpu_custom_call" | custom-call | bytes 12000000 | tf_op jit(solution)/shard_map/pallas_call | solution.py:370
  (1 shorter events, 0.0 us)
Async XLA Ops:
  0.0 1.0 %copy-start = (f32[16,16,512]{2,1,0:T(8,128)S(1)}, f32[16,16,512]{2,1,0:T(8,128)}, u32[]{:S(2)}) copy-start(f32[16,16,512]{2,1,0:T(8,128)} %data.1) | copy-start | bytes 1572868
  1.0 0.8 %copy-start.1 = (s32[16,512]{1,0:T(8,128)S(1)}, s32[16,512]{1,0:T(8,128)}, u32[]{:S(2)}) copy-start(s32[16,512]{1,0:T(8,128)} %blanked.3) | copy-start | bytes 98308
  2.7 17.4 %collective-permute-start = (f32[16,16,512]{2,1,0:T(8,128)S(1)}, f32[16,16,512]{2,1,0:T(8,128)S(1)}, u32[]{:S(2)}, u32[]{:S(2)}) collective-permute-start(f32[16,16,512]{2,1,0:T(8,128)S(1)} %get-tuple-element.19.cells), channel_id=1, source_target_pairs={{0,16},{16,0},{32,48},{48,32},{64,80},{80,64},{96,112},{112,96},{1... | collective-permute-start | bytes 1572872 | tf_op jit(solution)/shard_map/ppermute | solution.py:304
  6.4 7.2 %collective-permute-start.3 = (f32[3,16,512]{2,1,0:T(8,128)S(1)}, f32[3,16,512]{2,1,0:T(8,128)S(1)}, u32[]{:S(2)}, u32[]{:S(2)}) collective-permute-start(f32[3,16,512]{2,1,0:T(8,128)S(1)} %get-tuple-element.21), channel_id=1, source_target_pairs={{0,32},{32,64},{48,16},{64,96},{80,48},{112,80},{1,33},{33,65},{49... | collective-permute-start | bytes 294920 | tf_op jit(solution)/shard_map/ppermute | solution.py:304
  9.2 7.9 %collective-permute-start.2 = (f32[3,16,512]{2,1,0:T(8,128)S(1)}, f32[3,16,512]{2,1,0:T(8,128)S(1)}, u32[]{:S(2)}, u32[]{:S(2)}) collective-permute-start(f32[3,16,512]{2,1,0:T(8,128)S(1)} %get-tuple-element.20.edge), channel_id=1, source_target_pairs={{16,32},{32,16},{48,64},{64,48},{80,96},{96,80},{17,33},{33,17},{4... | collective-permute-start | bytes 294920 | tf_op jit(solution)/shard_map/ppermute | solution.py:304
  11.1 5.9 %collective-permute-start.1 = (f32[3,16,512]{2,1,0:T(8,128)S(1)}, f32[3,16,512]{2,1,0:T(8,128)S(1)}, u32[]{:S(2)}, u32[]{:S(2)}) collective-permute-start(f32[3,16,512]{2,1,0:T(8,128)S(1)} %get-tuple-element.20.edge), channel_id=1, source_target_pairs={{16,48},{32,0},{48,80},{64,32},{80,112},{96,64},{17,49},{33,1},{49... | collective-permute-start | bytes 294920 | tf_op jit(solution)/shard_map/ppermute | solution.py:304
  20.1 14.1 %collective-permute-start.4 = (f32[16,16,512]{2,1,0:T(8,128)S(1)}, f32[16,16,512]{2,1,0:T(8,128)S(1)}, u32[]{:S(2)}, u32[]{:S(2)}) collective-permute-start(f32[16,16,512]{2,1,0:T(8,128)S(1)} %shard_map.29.near), channel_id=1, source_target_pairs={{0,32},{32,64},{48,16},{64,96},{80,48},{112,80},{1,33},{33,65},{49... | collective-permute-start | bytes 1572872 | tf_op jit(solution)/shard_map/ppermute | solution.py:304
  24.3 15.1 %collective-permute-start.8 = (f32[14,32,512]{2,1,0:T(8,128)S(1)}, f32[14,32,512]{2,1,0:T(8,128)S(1)}, u32[]{:S(2)}, u32[]{:S(2)}) collective-permute-start(f32[14,32,512]{2,1,0:T(8,128)S(1)} %get-tuple-element.27), channel_id=1, source_target_pairs={{0,1},{1,0},{2,3},{3,2},{4,5},{5,4},{6,7},{7,6},{8,9},{9,8},{10,11... | collective-permute-start | bytes 2752520 | tf_op jit(solution)/shard_map/ppermute | solution.py:304
  25.9 16.8 %collective-permute-start.7 = (f32[14,32,512]{2,1,0:T(8,128)S(1)}, f32[14,32,512]{2,1,0:T(8,128)S(1)}, u32[]{:S(2)}, u32[]{:S(2)}) collective-permute-start(f32[14,32,512]{2,1,0:T(8,128)S(1)} %get-tuple-element.26), channel_id=1, source_target_pairs={{1,2},{2,1},{3,4},{4,3},{5,6},{6,5},{7,8},{8,7},{9,10},{10,9},{11,... | collective-permute-start | bytes 2752520 | tf_op jit(solution)/shard_map/ppermute | solution.py:304
  35.0 9.6 %collective-permute-start.6 = (f32[14,16,512]{2,1,0:T(8,128)S(1)}, f32[14,16,512]{2,1,0:T(8,128)S(1)}, u32[]{:S(2)}, u32[]{:S(2)}) collective-permute-start(f32[14,16,512]{2,1,0:T(8,128)S(1)} %get-tuple-element.24), channel_id=1, source_target_pairs={{0,1},{1,0},{2,3},{3,2},{4,5},{5,4},{6,7},{7,6},{8,9},{9,8},{10,11... | collective-permute-start | bytes 1376264 | tf_op jit(solution)/shard_map/ppermute | solution.py:304
  37.3 11.9 %collective-permute-start.5 = (f32[14,16,512]{2,1,0:T(8,128)S(1)}, f32[14,16,512]{2,1,0:T(8,128)S(1)}, u32[]{:S(2)}, u32[]{:S(2)}) collective-permute-start(f32[14,16,512]{2,1,0:T(8,128)S(1)} %get-tuple-element.23), channel_id=1, source_target_pairs={{1,2},{2,1},{3,4},{4,3},{5,6},{6,5},{7,8},{8,7},{9,10},{10,9},{11,... | collective-permute-start | bytes 1376264 | tf_op jit(solution)/shard_map/ppermute | solution.py:304
  44.7 4.5 %copy-start.2 = (s32[16,512]{1,0:T(8,128)S(1)}, s32[16,512]{1,0:T(8,128)}, u32[]{:S(2)}) copy-start(s32[16,512]{1,0:T(8,128)} %blanked.3) | copy-start | bytes 98308

commit v5 on v4

--- a/solution.py
+++ b/solution.py
@@ -29,7 +29,7 @@
         scratch_shapes=list(scratch),
         compiler_params=pltpu.CompilerParams(vmem_limit_bytes=vmem * 1024 * 1024),
         cost_estimate=pl.CostEstimate(
-            flops=0, bytes_accessed=int(micros * 3.0e6), transcendentals=0
+            flops=int(micros * 1e9), bytes_accessed=int(micros * 3.0e6), transcendentals=0
         ),
         **specs,
     )
@@ -330,6 +330,7 @@
         pair_rows_kernel,
         [f32(chans, 32, cols), f32(HALO, 32, cols), f32(HALO, 32, cols)],
         [pltpu.VMEM((chans, 48, cols), jnp.float32)],
+        micros=0.01,
     )(cells, near, edge_far, edge_near)
     pair_link = swap(pair_link, "chan", 1)
     pair_core = swap(pair_core, "chan", 0)
@@ -338,6 +339,7 @@
         far_rows_kernel,
         [f32(chans, 16, cols), f32(HALO, 16, cols), f32(HALO, 16, cols)],
         [pltpu.VMEM((chans, 32, cols), jnp.float32)],
+        micros=30.0,
     )(far, edge, beyond)
     outer_link = swap(outer_link, "chan", 1)
     outer_core = swap(outer_core, "chan", 0)

time: 53 us -> 51.3 us (0.968)
  the two profiles are of different devices: /device:TPU:29 before, /device:TPU:34 now
where the time goes in v5:
time: 51.3 us; the launch traced here: 50.9 us
  starting transfers between devices  21.1 us (41%)
  waiting for transfers between devices  18 us (35%)
  Pallas kernels  9.82 us (19%)
  local copies, waits for them, and re-layouts  1.8 us (4%)
    ppermute x9, starting transfers between devices, move(): lax.ppermute(value, axis, [(a, b) for a, b in pairs if 0 <= b < count])  21.1 us
    ppermute x9, waiting for transfers between devices, move(): lax.ppermute(value, axis, [(a, b) for a, b in pairs if 0 <= b < count])  18 us
    pallas_call x1, Pallas kernels, per_device(): call(snr_kernel, f32(4, chans, rows, cols), [pltpu.VMEM((4, tiles, chans...  3.43 us
    pallas_call x1, Pallas kernels, per_device(): call(pair_noise_kernel, [f32(4, chans, rows, cols), f32(4, tiles, 2, rows...  1.94 us
    unnamed x6, local copies, waits for them, and re-layouts  1.8 us
    pallas_call x1, Pallas kernels, per_device(): call(pair_rows_kernel, [f32(chans, 32, cols), f32(HALO, 32, cols), f32(HA...  1.35 us
  transfers between devices with their start and end apart: 9, of which 5 were waited for; matrix products, arithmetic and copies ran while one was open for 0% of the time, Pallas kernels for 11%

profile of v5, /device:TPU:34, one launch (start us, length us, event | category | flops | bytes accessed | tf_op | source)
XLA Modules:
  0.0 50.9 jit_solution(8168881559254455437)
XLA Ops:
  0.0 0.0 copy-start
  0.0 1.0 %copy-done = f32[16,16,512]{2,1,0:T(8,128)S(1)} copy-done((f32[16,16,512]{2,1,0:T(8,128)S(1)}, f32[16,16,512]{2,1,0:T(8,128)}, u32[]{:S(2)}) %copy-start) | copy-done | bytes 524312
  1.0 0.0 copy-start.1
  1.0 0.8 %copy-done.1 = s32[16,512]{1,0:T(8,128)S(1)} copy-done((s32[16,512]{1,0:T(8,128)S(1)}, s32[16,512]{1,0:T(8,128)}, u32[]{:S(2)}) %copy-start.1) | copy-done | bytes 32792
  1.8 0.9 %shard_map.28 = (f32[16,16,512]{2,1,0:T(8,128)S(1)}, f32[3,16,512]{2,1,0:T(8,128)S(1)}, f32[3,16,512]{2,1,0:T(8,128)S(1)}) custom-call(f32[16,16,512]{2,1,0:T(8,128)S(1)} %copy-done, s32[16,512]{1,0:T(8,128)S(1)} %copy-done.1), custom_call_target="tpu_custom_call" | custom-call | flops 1000000000 | bytes 3000000 | tf_op jit(solution)/shard_map/pallas_call | solution.py:313
  2.7 3.1 %collective-permute-start = (f32[16,16,512]{2,1,0:T(8,128)S(1)}, f32[16,16,512]{2,1,0:T(8,128)S(1)}, u32[]{:S(2)}, u32[]{:S(2)}) collective-permute-start(f32[16,16,512]{2,1,0:T(8,128)S(1)} %get-tuple-element.19.cells), channel_id=1, source_target_pairs={{0,16},{16,0},{32,48},{48,32},{64,80},{80,64},{96,112},{112,96},{1... | collective-permute-start | bytes 1572872 | tf_op jit(solution)/shard_map/ppermute | solution.py:304
  5.8 3.4 %collective-permute-start.3 = (f32[3,16,512]{2,1,0:T(8,128)S(1)}, f32[3,16,512]{2,1,0:T(8,128)S(1)}, u32[]{:S(2)}, u32[]{:S(2)}) collective-permute-start(f32[3,16,512]{2,1,0:T(8,128)S(1)} %get-tuple-element.21), channel_id=1, source_target_pairs={{0,32},{32,64},{48,16},{64,96},{80,48},{112,80},{1,33},{33,65},{49... | collective-permute-start | bytes 294920 | tf_op jit(solution)/shard_map/ppermute | solution.py:304
  9.2 1.9 %collective-permute-start.2 = (f32[3,16,512]{2,1,0:T(8,128)S(1)}, f32[3,16,512]{2,1,0:T(8,128)S(1)}, u32[]{:S(2)}, u32[]{:S(2)}) collective-permute-start(f32[3,16,512]{2,1,0:T(8,128)S(1)} %get-tuple-element.20.edge), channel_id=1, source_target_pairs={{16,32},{32,16},{48,64},{64,48},{80,96},{96,80},{17,33},{33,17},{4... | collective-permute-start | bytes 294920 | tf_op jit(solution)/shard_map/ppermute | solution.py:304
  11.1 1.9 %collective-permute-start.1 = (f32[3,16,512]{2,1,0:T(8,128)S(1)}, f32[3,16,512]{2,1,0:T(8,128)S(1)}, u32[]{:S(2)}, u32[]{:S(2)}) collective-permute-start(f32[3,16,512]{2,1,0:T(8,128)S(1)} %get-tuple-element.20.edge), channel_id=1, source_target_pairs={{16,48},{32,0},{48,80},{64,32},{80,112},{96,64},{17,49},{33,1},{49... | collective-permute-start | bytes 294920 | tf_op jit(solution)/shard_map/ppermute | solution.py:304
  13.0 0.0 collective-permute-done.3.rest_2_.beyond
  13.0 5.1 %collective-permute-done.2.rest_1_.edge_far = f32[3,16,512]{2,1,0:T(8,128)S(1)} collective-permute-done((f32[3,16,512]{2,1,0:T(8,128)S(1)}, f32[3,16,512]{2,1,0:T(8,128)S(1)}, u32[]{:S(2)}, u32[]{:S(2)}) %collective-permute-start.2) | collective-permute-done | bytes 98336 | tf_op jit(solution)/shard_map/ppermute | solution.py:304
  18.2 0.0 collective-permute-done.1.rest_0_.edge_near
  18.2 1.9 %collective-permute-done.value = f32[16,16,512]{2,1,0:T(8,128)S(1)} collective-permute-done((f32[16,16,512]{2,1,0:T(8,128)S(1)}, f32[16,16,512]{2,1,0:T(8,128)S(1)}, u32[]{:S(2)}, u32[]{:S(2)}) %collective-permute-start) | collective-permute-done | bytes 524320 | tf_op jit(solution)/shard_map/ppermute | solution.py:304
  20.1 3.4 %collective-permute-start.4 = (f32[16,16,512]{2,1,0:T(8,128)S(1)}, f32[16,16,512]{2,1,0:T(8,128)S(1)}, u32[]{:S(2)}, u32[]{:S(2)}) collective-permute-start(f32[16,16,512]{2,1,0:T(8,128)S(1)} %shard_map.29.near), channel_id=1, source_target_pairs={{0,32},{32,64},{48,16},{64,96},{80,48},{112,80},{1,33},{33,65},{49... | collective-permute-start | bytes 1572872 | tf_op jit(solution)/shard_map/ppermute | solution.py:304
  23.5 1.4 %shard_map.31 = (f32[16,32,512]{2,1,0:T(8,128)S(1)}, f32[14,32,512]{2,1,0:T(8,128)S(1)}, f32[14,32,512]{2,1,0:T(8,128)S(1)}) custom-call(f32[16,16,512]{2,1,0:T(8,128)S(1)} %get-tuple-element.19.cells, f32[16,16,512]{2,1,0:T(8,128)S(1)} %shard_map.29.near, f32[3,16,512]{2,1,0:T(8,128)S(1)} %collective-permute-done.2.rest_1_.edge_far, ...), custom_call_target="tpu_custom_call" | custom-call | flops 10000000 | bytes 30000 | tf_op jit(solution)/shard_map/pallas_call | solution.py:329
  24.8 3.7 %collective-permute-start.7 = (f32[14,32,512]{2,1,0:T(8,128)S(1)}, f32[14,32,512]{2,1,0:T(8,128)S(1)}, u32[]{:S(2)}, u32[]{:S(2)}) collective-permute-start(f32[14,32,512]{2,1,0:T(8,128)S(1)} %get-tuple-element.26), channel_id=1, source_target_pairs={{1,2},{2,1},{3,4},{4,3},{5,6},{6,5},{7,8},{8,7},{9,10},{10,9},{11,... | collective-permute-start | bytes 2752520 | tf_op jit(solution)/shard_map/ppermute | solution.py:304
  28.5 0.1 collective-permute-start.8
  28.6 6.1 %collective-permute-done.4.far = f32[16,16,512]{2,1,0:T(8,128)S(1)} collective-permute-done((f32[16,16,512]{2,1,0:T(8,128)S(1)}, f32[16,16,512]{2,1,0:T(8,128)S(1)}, u32[]{:S(2)}, u32[]{:S(2)}) %collective-permute-start.4) | collective-permute-done | bytes 524320 | tf_op jit(solution)/shard_map/ppermute | solution.py:304
  34.7 0.8 %shard_map.30 = (f32[16,16,512]{2,1,0:T(8,128)S(1)}, f32[14,16,512]{2,1,0:T(8,128)S(1)}, f32[14,16,512]{2,1,0:T(8,128)S(1)}) custom-call(f32[16,16,512]{2,1,0:T(8,128)S(1)} %collective-permute-done.4.far, f32[3,16,512]{2,1,0:T(8,128)S(1)} %get-tuple-element.20.edge, f32[3,16,512]{2,1,0:T(8,128)S(1)} %collective-permute-done.3.rest_2_.beyond), custom_call_target="tpu_custom_call" | custom-call | flops 30000001024 | bytes 90000000 | tf_op jit(solution)/shard_map/pallas_call | solution.py:338
  35.6 3.4 %collective-permute-start.5 = (f32[14,16,512]{2,1,0:T(8,128)S(1)}, f32[14,16,512]{2,1,0:T(8,128)S(1)}, u32[]{:S(2)}, u32[]{:S(2)}) collective-permute-start(f32[14,16,512]{2,1,0:T(8,128)S(1)} %get-tuple-element.23), channel_id=1, source_target_pairs={{1,2},{2,1},{3,4},{4,3},{5,6},{6,5},{7,8},{8,7},{9,10},{10,9},{11,... | collective-permute-start | bytes 1376264 | tf_op jit(solution)/shard_map/ppermute | solution.py:304
  38.9 0.3 collective-permute-start.6
  39.2 0.0 collective-permute-done.8.core
  39.2 0.9 %shard_map.32 = (f32[4,4,640,128]{3,2,1,0:T(8,128)S(1)}, f32[4,8,16,512]{3,2,1,0:T(8,128)S(1)}) custom-call(f32[16,32,512]{2,1,0:T(8,128)S(1)} %get-tuple-element.25.own, f32[14,32,512]{2,1,0:T(8,128)S(1)} %collective-permute-done.8.core, f32[16,16,512]{2,1,0:T(8,128)S(1)} %get-tuple-element.22.after.own), custom_call_target="tpu_custom_call" | custom-call | flops 2000000000 | bytes 6000000 | tf_op jit(solution)/shard_map/pallas_call | solution.py:347
  40.2 1.5 %collective-permute-done.7.link = f32[14,32,512]{2,1,0:T(8,128)S(1)} collective-permute-done((f32[14,32,512]{2,1,0:T(8,128)S(1)}, f32[14,32,512]{2,1,0:T(8,128)S(1)}, u32[]{:S(2)}, u32[]{:S(2)}) %collective-permute-start.7) | collective-permute-done | bytes 917536 | tf_op jit(solution)/shard_map/ppermute | solution.py:304
  41.6 1.9 %shard_map.33 = (f32[4,16,16,512]{3,2,1,0:T(8,128)S(1)}, f32[4,4,2,16,8,128]{5,4,3,2,1,0:T(8,128)S(1)}, bf16[512,512]{1,0:T(8,128)(2,1)S(1)}) custom-call(f32[16,32,512]{2,1,0:T(8,128)S(1)} %get-tuple-element.25.own, f32[14,32,512]{2,1,0:T(8,128)S(1)} %collective-permute-done.7.link, f32[4,4,640,128]{3,2,1,0:T(8,128)S(1)} %get-tuple-element.28.before, ...), custom_call_target="tpu_custom_call" | custom-call | flops 3000000000 | bytes 9000000 | tf_op jit(solution)/shard_map/pallas_call | solution.py:353
  43.6 0.0 collective-permute-done.6.core
  43.6 0.0 copy-start.2
  43.6 0.5 shard_map.34.before
  44.1 3.4 %collective-permute-done.5.link = f32[14,16,512]{2,1,0:T(8,128)S(1)} collective-permute-done((f32[14,16,512]{2,1,0:T(8,128)S(1)}, f32[14,16,512]{2,1,0:T(8,128)S(1)}, u32[]{:S(2)}, u32[]{:S(2)}) %collective-permute-start.5) | collective-permute-done | bytes 458784 | tf_op jit(solution)/shard_map/ppermute | solution.py:304
  47.5 0.0 copy-done.2
  47.5 3.4 %shard_map.35 = f32[4,16,16,512]{3,2,1,0:T(8,128)} custom-call(f32[16,16,512]{2,1,0:T(8,128)S(1)} %get-tuple-element.22.after.own, f32[14,16,512]{2,1,0:T(8,128)S(1)} %collective-permute-done.5.link, f32[4,4,384,128]{3,2,1,0:T(8,128)S(1)} %shard_map.34.before, f32[4,4,2,16,8,128]{5,4,3,2,1,0:T(8,128)S(1)} %get-tuple-element.30.after.part, ...), custom_call_target="tpu_custom_call" | custom-call | flops 4000000000 | bytes 12000000 | tf_op jit(solution)/shard_map/pallas_call | solution.py:372
  (1 shorter events, 0.0 us)
Async XLA Ops:
  0.0 1.0 %copy-start = (f32[16,16,512]{2,1,0:T(8,128)S(1)}, f32[16,16,512]{2,1,0:T(8,128)}, u32[]{:S(2)}) copy-start(f32[16,16,512]{2,1,0:T(8,128)} %data.1) | copy-start | bytes 1572868
  1.0 0.8 %copy-start.1 = (s32[16,512]{1,0:T(8,128)S(1)}, s32[16,512]{1,0:T(8,128)}, u32[]{:S(2)}) copy-start(s32[16,512]{1,0:T(8,128)} %blanked.3) | copy-start | bytes 98308
  2.7 17.4 %collective-permute-start = (f32[16,16,512]{2,1,0:T(8,128)S(1)}, f32[16,16,512]{2,1,0:T(8,128)S(1)}, u32[]{:S(2)}, u32[]{:S(2)}) collective-permute-start(f32[16,16,512]{2,1,0:T(8,128)S(1)} %get-tuple-element.19.cells), channel_id=1, source_target_pairs={{0,16},{16,0},{32,48},{48,32},{64,80},{80,64},{96,112},{112,96},{1... | collective-permute-start | bytes 1572872 | tf_op jit(solution)/shard_map/ppermute | solution.py:304
  5.8 7.3 %collective-permute-start.3 = (f32[3,16,512]{2,1,0:T(8,128)S(1)}, f32[3,16,512]{2,1,0:T(8,128)S(1)}, u32[]{:S(2)}, u32[]{:S(2)}) collective-permute-start(f32[3,16,512]{2,1,0:T(8,128)S(1)} %get-tuple-element.21), channel_id=1, source_target_pairs={{0,32},{32,64},{48,16},{64,96},{80,48},{112,80},{1,33},{33,65},{49... | collective-permute-start | bytes 294920 | tf_op jit(solution)/shard_map/ppermute | solution.py:304
  9.2 9.0 %collective-permute-start.2 = (f32[3,16,512]{2,1,0:T(8,128)S(1)}, f32[3,16,512]{2,1,0:T(8,128)S(1)}, u32[]{:S(2)}, u32[]{:S(2)}) collective-permute-start(f32[3,16,512]{2,1,0:T(8,128)S(1)} %get-tuple-element.20.edge), channel_id=1, source_target_pairs={{16,32},{32,16},{48,64},{64,48},{80,96},{96,80},{17,33},{33,17},{4... | collective-permute-start | bytes 294920 | tf_op jit(solution)/shard_map/ppermute | solution.py:304
  11.1 7.1 %collective-permute-start.1 = (f32[3,16,512]{2,1,0:T(8,128)S(1)}, f32[3,16,512]{2,1,0:T(8,128)S(1)}, u32[]{:S(2)}, u32[]{:S(2)}) collective-permute-start(f32[3,16,512]{2,1,0:T(8,128)S(1)} %get-tuple-element.20.edge), channel_id=1, source_target_pairs={{16,48},{32,0},{48,80},{64,32},{80,112},{96,64},{17,49},{33,1},{49... | collective-permute-start | bytes 294920 | tf_op jit(solution)/shard_map/ppermute | solution.py:304
  20.1 14.7 %collective-permute-start.4 = (f32[16,16,512]{2,1,0:T(8,128)S(1)}, f32[16,16,512]{2,1,0:T(8,128)S(1)}, u32[]{:S(2)}, u32[]{:S(2)}) collective-permute-start(f32[16,16,512]{2,1,0:T(8,128)S(1)} %shard_map.29.near), channel_id=1, source_target_pairs={{0,32},{32,64},{48,16},{64,96},{80,48},{112,80},{1,33},{33,65},{49... | collective-permute-start | bytes 1572872 | tf_op jit(solution)/shard_map/ppermute | solution.py:304
  24.8 16.8 %collective-permute-start.7 = (f32[14,32,512]{2,1,0:T(8,128)S(1)}, f32[14,32,512]{2,1,0:T(8,128)S(1)}, u32[]{:S(2)}, u32[]{:S(2)}) collective-permute-start(f32[14,32,512]{2,1,0:T(8,128)S(1)} %get-tuple-element.26), channel_id=1, source_target_pairs={{1,2},{2,1},{3,4},{4,3},{5,6},{6,5},{7,8},{8,7},{9,10},{10,9},{11,... | collective-permute-start | bytes 2752520 | tf_op jit(solution)/shard_map/ppermute | solution.py:304
  28.5 10.7 %collective-permute-start.8 = (f32[14,32,512]{2,1,0:T(8,128)S(1)}, f32[14,32,512]{2,1,0:T(8,128)S(1)}, u32[]{:S(2)}, u32[]{:S(2)}) collective-permute-start(f32[14,32,512]{2,1,0:T(8,128)S(1)} %get-tuple-element.27), channel_id=1, source_target_pairs={{0,1},{1,0},{2,3},{3,2},{4,5},{5,4},{6,7},{7,6},{8,9},{9,8},{10,11... | collective-permute-start | bytes 2752520 | tf_op jit(solution)/shard_map/ppermute | solution.py:304
  35.6 11.9 %collective-permute-start.5 = (f32[14,16,512]{2,1,0:T(8,128)S(1)}, f32[14,16,512]{2,1,0:T(8,128)S(1)}, u32[]{:S(2)}, u32[]{:S(2)}) collective-permute-start(f32[14,16,512]{2,1,0:T(8,128)S(1)} %get-tuple-element.23), channel_id=1, source_target_pairs={{1,2},{2,1},{3,4},{4,3},{5,6},{6,5},{7,8},{8,7},{9,10},{10,9},{11,... | collective-permute-start | bytes 1376264 | tf_op jit(solution)/shard_map/ppermute | solution.py:304
  38.9 4.6 %collective-permute-start.6 = (f32[14,16,512]{2,1,0:T(8,128)S(1)}, f32[14,16,512]{2,1,0:T(8,128)S(1)}, u32[]{:S(2)}, u32[]{:S(2)}) collective-permute-start(f32[14,16,512]{2,1,0:T(8,128)S(1)} %get-tuple-element.24), channel_id=1, source_target_pairs={{0,1},{1,0},{2,3},{3,2},{4,5},{5,4},{6,7},{7,6},{8,9},{9,8},{10,11... | collective-permute-start | bytes 1376264 | tf_op jit(solution)/shard_map/ppermute | solution.py:304
  43.6 3.9 %copy-start.2 = (s32[16,512]{1,0:T(8,128)S(1)}, s32[16,512]{1,0:T(8,128)}, u32[]{:S(2)}) copy-start(s32[16,512]{1,0:T(8,128)} %blanked.3) | copy-start | bytes 98308

commit v6 on v5

--- a/solution.py
+++ b/solution.py
@@ -43,7 +43,7 @@
     return lax.axis_index(axis) % 2
 
 
-def clean_cols_kernel(data, blanked, cells, edge, edge2):
+def clean_cols_kernel(data, blanked, cells, second, edge, edge2):
     taps = kernel_taps()
     chans, rows, cols = data.shape
     even = odd_of("pix") == 0
@@ -57,6 +57,7 @@
             right = jnp.where(lane < cols - t, pltpu.roll(x, cols - t, 1), 0.0)
             acc = acc + taps[3 + t] * (left + right)
         cells[c] = acc
+        second[c] = acc[:, cols - second.shape[2] :]
     for r in range(3):
         top = cells[:, r, :]
         bottom = cells[:, rows - 3 + r, :]
@@ -100,12 +101,13 @@
     send_halos(full, link, core)
 
 
-def far_rows_kernel(far, edge, beyond, full, link, core, field):
-    chans, rows, cols = far.shape
+def far_rows_kernel(far1, far2, edge, beyond, full, link, core, field):
+    chans, rows, half = far1.shape
     at, count = lax.axis_index("pix"), lax.axis_size("pix")
     even = odd_of("pix") == 0
     present = jnp.logical_and(at > 0, at < count - 1).astype(jnp.float32)
-    field[:, 8:24, :] = far[...]
+    field[:, 8:24, :half] = far1[...]
+    field[:, 8:24, half:] = far2[...]
     for r in range(3):
         field[:, 5 + r, :] = jnp.where(even, beyond[r], edge[r])
         field[:, 24 + r, :] = jnp.where(even, edge[r], beyond[r])
@@ -310,21 +312,24 @@
 
     toward = [(i, i + 2 if i % 2 == 0 else i - 2) for i in range(pix)]
     back = [(i, i - 2 if i % 2 == 0 else i + 2) for i in range(pix)]
-    cells, edge, edge2 = call(
-        clean_cols_kernel, [f32(chans, rows, cols), f32(3, chans, cols), f32(3, chans, cols)]
+    half = cols // 2
+    cells, right, edge, edge2 = call(
+        clean_cols_kernel,
+        [f32(chans, rows, cols), f32(chans, rows, half), f32(3, chans, cols), f32(3, chans, cols)],
     )(data_cube, blanked)
     near = swap(cells, "pix", 0)
+    far_right = swap(move(right, "pix", back), "pix", 0)
     edge_near = move(edge, "pix", back)
     edge_far = swap(edge, "pix", 1)
     beyond = move(edge2, "pix", toward)
-    near = call(
-        lambda value, *rest: None,
-        f32(*near.shape),
-        in_specs=[ANY] * 4,
-        out_specs=ANY,
-        input_output_aliases={0: 0},
-    )(near, edge_near, edge_far, beyond)
-    far = move(near, "pix", toward)
+
+    def left_half(value, *rest):
+        rest[-1][...] = value[:, :, : rest[-1].shape[2]]
+
+    near_left = call(left_half, f32(chans, rows, half), in_specs=[VMEM] + [ANY] * 3)(
+        near, edge_near, edge_far, beyond
+    )
+    far_left = move(near_left, "pix", toward)
 
     pair, pair_link, pair_core = call(
         pair_rows_kernel,
@@ -340,7 +345,7 @@
         [f32(chans, 16, cols), f32(HALO, 16, cols), f32(HALO, 16, cols)],
         [pltpu.VMEM((chans, 32, cols), jnp.float32)],
         micros=30.0,
-    )(far, edge, beyond)
+    )(far_left, far_right, edge, beyond)
     outer_link = swap(outer_link, "chan", 1)
     outer_core = swap(outer_core, "chan", 0)
 

time: 51.3 us -> 52 us (1.014)
  starting transfers between devices: 21.1 us -> 29.4 us
  waiting for transfers between devices: 18 us -> 10.4 us
    ppermute x9 -> x11, starting transfers between devices: 21.1 us -> 29.4 us  [move(): lax.ppermute(value, axis, [(a, b) for a, b in pairs if 0 <= b < count])]
    ppermute x9 -> x11, waiting for transfers between devices: 18 us -> 10.4 us  [move(): lax.ppermute(value, axis, [(a, b) for a, b in pairs if 0 <= b < count])]
    unnamed x6 -> x4, local copies, waits for them, and re-layouts: 1.8 us -> 1.8 us
  transfers between devices with their start and end apart: 9 -> 11, of which waited for: 5 -> 4; matrix products, arithmetic and copies ran while one was open for 0% -> 0% of each run, Pallas kernels for 11% -> 11%
where the time goes in v6:
time: 52 us; the launch traced here: 51.6 us
  starting transfers between devices  29.4 us (57%)
  waiting for transfers between devices  10.4 us (20%)
  Pallas kernels  9.87 us (19%)
  local copies, waits for them, and re-layouts  1.8 us (3%)
    ppermute x11, starting transfers between devices, move(): lax.ppermute(value, axis, [(a, b) for a, b in pairs if 0 <= b < count])  29.4 us
    ppermute x11, waiting for transfers between devices, move(): lax.ppermute(value, axis, [(a, b) for a, b in pairs if 0 <= b < count])  10.4 us
    pallas_call x1, Pallas kernels, per_device(): call(snr_kernel, f32(4, chans, rows, cols), [pltpu.VMEM((4, tiles, chans...  3.43 us
    pallas_call x1, Pallas kernels, per_device(): call(pair_noise_kernel, [f32(4, chans, rows, cols), f32(4, tiles, 2, rows...  1.94 us
    unnamed x4, local copies, waits for them, and re-layouts  1.8 us
    pallas_call x1, Pallas kernels, per_device(): call(pair_rows_kernel, [f32(chans, 32, cols), f32(HALO, 32, cols), f32(HA...  1.35 us
  transfers between devices with their start and end apart: 11, of which 4 were waited for; matrix products, arithmetic and copies ran while one was open for 0% of the time, Pallas kernels for 11%

profile of v6, /device:TPU:34, one launch (start us, length us, event | category | flops | bytes accessed | tf_op | source)
XLA Modules:
  0.0 51.6 jit_solution(2481168672037910587)
XLA Ops:
  0.0 0.0 copy-start
  0.0 1.0 %copy-done = f32[16,16,512]{2,1,0:T(8,128)S(1)} copy-done((f32[16,16,512]{2,1,0:T(8,128)S(1)}, f32[16,16,512]{2,1,0:T(8,128)}, u32[]{:S(2)}) %copy-start) | copy-done | bytes 524312
  1.0 0.0 copy-start.1
  1.0 0.8 %copy-done.1 = s32[16,512]{1,0:T(8,128)S(1)} copy-done((s32[16,512]{1,0:T(8,128)S(1)}, s32[16,512]{1,0:T(8,128)}, u32[]{:S(2)}) %copy-start.1) | copy-done | bytes 32792
  1.8 0.9 %shard_map.28 = (f32[16,16,512]{2,1,0:T(8,128)S(1)}, f32[16,16,256]{2,1,0:T(8,128)S(1)}, f32[3,16,512]{2,1,0:T(8,128)S(1)}, f32[3,16,512]{2,1,0:T(8,128)S(1)}) custom-call(f32[16,16,512]{2,1,0:T(8,128)S(1)} %copy-done, s32[16,512]{1,0:T(8,128)S(1)} %copy-done.1), custom_call_target="tpu_custom_call" | custom-call | flops 1000000000 | bytes 3000000 | tf_op jit(solution)/shard_map/pallas_call | solution.py:316
  2.7 3.1 %collective-permute-start = (f32[16,16,512]{2,1,0:T(8,128)S(1)}, f32[16,16,512]{2,1,0:T(8,128)S(1)}, u32[]{:S(2)}, u32[]{:S(2)}) collective-permute-start(f32[16,16,512]{2,1,0:T(8,128)S(1)} %get-tuple-element.20.cells), channel_id=1, source_target_pairs={{0,16},{16,0},{32,48},{48,32},{64,80},{80,64},{96,112},{112,96},{1... | collective-permute-start | bytes 1572872 | tf_op jit(solution)/shard_map/ppermute | solution.py:306
  5.8 2.4 %collective-permute-start.5 = (f32[16,16,256]{2,1,0:T(8,128)S(1)}, f32[16,16,256]{2,1,0:T(8,128)S(1)}, u32[]{:S(2)}, u32[]{:S(2)}) collective-permute-start(f32[16,16,256]{2,1,0:T(8,128)S(1)} %get-tuple-element.23), channel_id=1, source_target_pairs={{16,48},{32,0},{48,80},{64,32},{80,112},{96,64},{17,49},{33,1},{49... | collective-permute-start | bytes 786440 | tf_op jit(solution)/shard_map/ppermute | solution.py:306
  8.2 3.4 %collective-permute-start.3 = (f32[3,16,512]{2,1,0:T(8,128)S(1)}, f32[3,16,512]{2,1,0:T(8,128)S(1)}, u32[]{:S(2)}, u32[]{:S(2)}) collective-permute-start(f32[3,16,512]{2,1,0:T(8,128)S(1)} %get-tuple-element.22), channel_id=1, source_target_pairs={{0,32},{32,64},{48,16},{64,96},{80,48},{112,80},{1,33},{33,65},{49... | collective-permute-start | bytes 294920 | tf_op jit(solution)/shard_map/ppermute | solution.py:306
  11.6 1.9 %collective-permute-start.2 = (f32[3,16,512]{2,1,0:T(8,128)S(1)}, f32[3,16,512]{2,1,0:T(8,128)S(1)}, u32[]{:S(2)}, u32[]{:S(2)}) collective-permute-start(f32[3,16,512]{2,1,0:T(8,128)S(1)} %get-tuple-element.21.edge), channel_id=1, source_target_pairs={{16,32},{32,16},{48,64},{64,48},{80,96},{96,80},{17,33},{33,17},{4... | collective-permute-start | bytes 294920 | tf_op jit(solution)/shard_map/ppermute | solution.py:306
  13.5 1.9 %collective-permute-start.1 = (f32[3,16,512]{2,1,0:T(8,128)S(1)}, f32[3,16,512]{2,1,0:T(8,128)S(1)}, u32[]{:S(2)}, u32[]{:S(2)}) collective-permute-start(f32[3,16,512]{2,1,0:T(8,128)S(1)} %get-tuple-element.21.edge), channel_id=1, source_target_pairs={{16,48},{32,0},{48,80},{64,32},{80,112},{96,64},{17,49},{33,1},{49... | collective-permute-start | bytes 294920 | tf_op jit(solution)/shard_map/ppermute | solution.py:306
  15.5 0.2 collective-permute-done.5
  15.7 4.3 %collective-permute-start.6 = (f32[16,16,256]{2,1,0:T(8,128)S(1)}, f32[16,16,256]{2,1,0:T(8,128)S(1)}, u32[]{:S(2)}, u32[]{:S(2)}) collective-permute-start(f32[16,16,256]{2,1,0:T(8,128)S(1)} %collective-permute-done.5), channel_id=1, source_target_pairs={{0,16},{16,0},{32,48},{48,32},{64,80},{80,64},{96,112},{112,96},{1... | collective-permute-start | bytes 786440 | tf_op jit(solution)/shard_map/ppermute | solution.py:306
  20.0 0.0 collective-permute-done.3.rest_2_.beyond
  20.0 0.6 %collective-permute-done.2.rest_1_.edge_far = f32[3,16,512]{2,1,0:T(8,128)S(1)} collective-permute-done((f32[3,16,512]{2,1,0:T(8,128)S(1)}, f32[3,16,512]{2,1,0:T(8,128)S(1)}, u32[]{:S(2)}, u32[]{:S(2)}) %collective-permute-start.2) | collective-permute-done | bytes 98336 | tf_op jit(solution)/shard_map/ppermute | solution.py:306
  20.6 0.0 collective-permute-done.1.rest_0_.edge_near
  20.6 0.0 collective-permute-done.value.near
  20.7 4.4 %collective-permute-start.4 = (f32[16,16,256]{2,1,0:T(8,128)S(1)}, f32[16,16,256]{2,1,0:T(8,128)S(1)}, u32[]{:S(2)}, u32[]{:S(2)}) collective-permute-start(f32[16,16,256]{2,1,0:T(8,128)S(1)} %shard_map.29), channel_id=1, source_target_pairs={{0,32},{32,64},{48,16},{64,96},{80,48},{112,80},{1,33},{33,65},{49... | collective-permute-start | bytes 786440 | tf_op jit(solution)/shard_map/ppermute | solution.py:306
  25.1 1.4 %shard_map.31 = (f32[16,32,512]{2,1,0:T(8,128)S(1)}, f32[14,32,512]{2,1,0:T(8,128)S(1)}, f32[14,32,512]{2,1,0:T(8,128)S(1)}) custom-call(f32[16,16,512]{2,1,0:T(8,128)S(1)} %get-tuple-element.20.cells, f32[16,16,512]{2,1,0:T(8,128)S(1)} %collective-permute-done.value.near, f32[3,16,512]{2,1,0:T(8,128)S(1)} %collective-permute-done.2.rest_1_.edge_far, ...), custom_call_target="tpu_custom_call" | custom-call | flops 10000000 | bytes 30000 | tf_op jit(solution)/shard_map/pallas_call | solution.py:334
  26.5 1.9 %collective-permute-start.9 = (f32[14,32,512]{2,1,0:T(8,128)S(1)}, f32[14,32,512]{2,1,0:T(8,128)S(1)}, u32[]{:S(2)}, u32[]{:S(2)}) collective-permute-start(f32[14,32,512]{2,1,0:T(8,128)S(1)} %get-tuple-element.28), channel_id=1, source_target_pairs={{1,2},{2,1},{3,4},{4,3},{5,6},{6,5},{7,8},{8,7},{9,10},{10,9},{11,... | collective-permute-start | bytes 2752520 | tf_op jit(solution)/shard_map/ppermute | solution.py:306
  28.4 1.8 %collective-permute-start.10 = (f32[14,32,512]{2,1,0:T(8,128)S(1)}, f32[14,32,512]{2,1,0:T(8,128)S(1)}, u32[]{:S(2)}, u32[]{:S(2)}) collective-permute-start(f32[14,32,512]{2,1,0:T(8,128)S(1)} %get-tuple-element.29), channel_id=1, source_target_pairs={{0,1},{1,0},{2,3},{3,2},{4,5},{5,4},{6,7},{7,6},{8,9},{9,8},{10,11... | collective-permute-start | bytes 2752520 | tf_op jit(solution)/shard_map/ppermute | solution.py:306
  30.1 0.0 collective-permute-done.6.far2
  30.1 0.0 collective-permute-done.4.far1
  30.1 0.8 %shard_map.30 = (f32[16,16,512]{2,1,0:T(8,128)S(1)}, f32[14,16,512]{2,1,0:T(8,128)S(1)}, f32[14,16,512]{2,1,0:T(8,128)S(1)}) custom-call(f32[16,16,256]{2,1,0:T(8,128)S(1)} %collective-permute-done.4.far1, f32[16,16,256]{2,1,0:T(8,128)S(1)} %collective-permute-done.6.far2, f32[3,16,512]{2,1,0:T(8,128)S(1)} %get-tuple-element.21.edge, ...), custom_call_target="tpu_custom_call" | custom-call | flops 30000001024 | bytes 90000000 | tf_op jit(solution)/shard_map/pallas_call | solution.py:343
  31.0 4.1 %collective-permute-start.7 = (f32[14,16,512]{2,1,0:T(8,128)S(1)}, f32[14,16,512]{2,1,0:T(8,128)S(1)}, u32[]{:S(2)}, u32[]{:S(2)}) collective-permute-start(f32[14,16,512]{2,1,0:T(8,128)S(1)} %get-tuple-element.25), channel_id=1, source_target_pairs={{1,2},{2,1},{3,4},{4,3},{5,6},{6,5},{7,8},{8,7},{9,10},{10,9},{11,... | collective-permute-start | bytes 1376264 | tf_op jit(solution)/shard_map/ppermute | solution.py:306
  35.1 0.1 collective-permute-start.8
  35.2 0.0 collective-permute-done.10.core
  35.2 0.9 %shard_map.32 = (f32[4,4,640,128]{3,2,1,0:T(8,128)S(1)}, f32[4,8,16,512]{3,2,1,0:T(8,128)S(1)}) custom-call(f32[16,32,512]{2,1,0:T(8,128)S(1)} %get-tuple-element.27.own, f32[14,32,512]{2,1,0:T(8,128)S(1)} %collective-permute-done.10.core, f32[16,16,512]{2,1,0:T(8,128)S(1)} %get-tuple-element.24.after.own), custom_call_target="tpu_custom_call" | custom-call | flops 2000000000 | bytes 6000000 | tf_op jit(solution)/shard_map/pallas_call | solution.py:352
  36.1 7.2 %collective-permute-done.9.link = f32[14,32,512]{2,1,0:T(8,128)S(1)} collective-permute-done((f32[14,32,512]{2,1,0:T(8,128)S(1)}, f32[14,32,512]{2,1,0:T(8,128)S(1)}, u32[]{:S(2)}, u32[]{:S(2)}) %collective-permute-start.9) | collective-permute-done | bytes 917536 | tf_op jit(solution)/shard_map/ppermute | solution.py:306
  43.3 1.9 %shard_map.33 = (f32[4,16,16,512]{3,2,1,0:T(8,128)S(1)}, f32[4,4,2,16,8,128]{5,4,3,2,1,0:T(8,128)S(1)}, bf16[512,512]{1,0:T(8,128)(2,1)S(1)}) custom-call(f32[16,32,512]{2,1,0:T(8,128)S(1)} %get-tuple-element.27.own, f32[14,32,512]{2,1,0:T(8,128)S(1)} %collective-permute-done.9.link, f32[4,4,640,128]{3,2,1,0:T(8,128)S(1)} %get-tuple-element.30.before, ...), custom_call_target="tpu_custom_call" | custom-call | flops 3000000000 | bytes 9000000 | tf_op jit(solution)/shard_map/pallas_call | solution.py:358
  45.2 0.0 collective-permute-done.8.core
  45.2 0.5 shard_map.34.before
  45.7 2.5 %collective-permute-done.7.link = f32[14,16,512]{2,1,0:T(8,128)S(1)} collective-permute-done((f32[14,16,512]{2,1,0:T(8,128)S(1)}, f32[14,16,512]{2,1,0:T(8,128)S(1)}, u32[]{:S(2)}, u32[]{:S(2)}) %collective-permute-start.7) | collective-permute-done | bytes 458784 | tf_op jit(solution)/shard_map/ppermute | solution.py:306
  48.2 3.4 %shard_map.35 = f32[4,16,16,512]{3,2,1,0:T(8,128)} custom-call(f32[16,16,512]{2,1,0:T(8,128)S(1)} %get-tuple-element.24.after.own, f32[14,16,512]{2,1,0:T(8,128)S(1)} %collective-permute-done.7.link, f32[4,4,384,128]{3,2,1,0:T(8,128)S(1)} %shard_map.34.before, f32[4,4,2,16,8,128]{5,4,3,2,1,0:T(8,128)S(1)} %get-tuple-element.32.after.part, ...), custom_call_target="tpu_custom_call" | custom-call | flops 4000000000 | bytes 12000000 | tf_op jit(solution)/shard_map/pallas_call | solution.py:377
  (1 shorter events, 0.0 us)
Async XLA Ops:
  0.0 1.0 %copy-start = (f32[16,16,512]{2,1,0:T(8,128)S(1)}, f32[16,16,512]{2,1,0:T(8,128)}, u32[]{:S(2)}) copy-start(f32[16,16,512]{2,1,0:T(8,128)} %data.1) | copy-start | bytes 1572868
  1.0 0.8 %copy-start.1 = (s32[16,512]{1,0:T(8,128)S(1)}, s32[16,512]{1,0:T(8,128)}, u32[]{:S(2)}) copy-start(s32[16,512]{1,0:T(8,128)} %blanked.3) | copy-start | bytes 98308
  2.7 17.9 %collective-permute-start = (f32[16,16,512]{2,1,0:T(8,128)S(1)}, f32[16,16,512]{2,1,0:T(8,128)S(1)}, u32[]{:S(2)}, u32[]{:S(2)}) collective-permute-start(f32[16,16,512]{2,1,0:T(8,128)S(1)} %get-tuple-element.20.cells), channel_id=1, source_target_pairs={{0,16},{16,0},{32,48},{48,32},{64,80},{80,64},{96,112},{112,96},{1... | collective-permute-start | bytes 1572872 | tf_op jit(solution)/shard_map/ppermute | solution.py:306
  5.8 9.9 %collective-permute-start.5 = (f32[16,16,256]{2,1,0:T(8,128)S(1)}, f32[16,16,256]{2,1,0:T(8,128)S(1)}, u32[]{:S(2)}, u32[]{:S(2)}) collective-permute-start(f32[16,16,256]{2,1,0:T(8,128)S(1)} %get-tuple-element.23), channel_id=1, source_target_pairs={{16,48},{32,0},{48,80},{64,32},{80,112},{96,64},{17,49},{33,1},{49... | collective-permute-start | bytes 786440 | tf_op jit(solution)/shard_map/ppermute | solution.py:306
  8.2 11.8 %collective-permute-start.3 = (f32[3,16,512]{2,1,0:T(8,128)S(1)}, f32[3,16,512]{2,1,0:T(8,128)S(1)}, u32[]{:S(2)}, u32[]{:S(2)}) collective-permute-start(f32[3,16,512]{2,1,0:T(8,128)S(1)} %get-tuple-element.22), channel_id=1, source_target_pairs={{0,32},{32,64},{48,16},{64,96},{80,48},{112,80},{1,33},{33,65},{49... | collective-permute-start | bytes 294920 | tf_op jit(solution)/shard_map/ppermute | solution.py:306
  11.6 9.0 %collective-permute-start.2 = (f32[3,16,512]{2,1,0:T(8,128)S(1)}, f32[3,16,512]{2,1,0:T(8,128)S(1)}, u32[]{:S(2)}, u32[]{:S(2)}) collective-permute-start(f32[3,16,512]{2,1,0:T(8,128)S(1)} %get-tuple-element.21.edge), channel_id=1, source_target_pairs={{16,32},{32,16},{48,64},{64,48},{80,96},{96,80},{17,33},{33,17},{4... | collective-permute-start | bytes 294920 | tf_op jit(solution)/shard_map/ppermute | solution.py:306
  13.5 7.1 %collective-permute-start.1 = (f32[3,16,512]{2,1,0:T(8,128)S(1)}, f32[3,16,512]{2,1,0:T(8,128)S(1)}, u32[]{:S(2)}, u32[]{:S(2)}) collective-permute-start(f32[3,16,512]{2,1,0:T(8,128)S(1)} %get-tuple-element.21.edge), channel_id=1, source_target_pairs={{16,48},{32,0},{48,80},{64,32},{80,112},{96,64},{17,49},{33,1},{49... | collective-permute-start | bytes 294920 | tf_op jit(solution)/shard_map/ppermute | solution.py:306
  15.7 14.5 %collective-permute-start.6 = (f32[16,16,256]{2,1,0:T(8,128)S(1)}, f32[16,16,256]{2,1,0:T(8,128)S(1)}, u32[]{:S(2)}, u32[]{:S(2)}) collective-permute-start(f32[16,16,256]{2,1,0:T(8,128)S(1)} %collective-permute-done.5), channel_id=1, source_target_pairs={{0,16},{16,0},{32,48},{48,32},{64,80},{80,64},{96,112},{112,96},{1... | collective-permute-start | bytes 786440 | tf_op jit(solution)/shard_map/ppermute | solution.py:306
  20.7 9.5 %collective-permute-start.4 = (f32[16,16,256]{2,1,0:T(8,128)S(1)}, f32[16,16,256]{2,1,0:T(8,128)S(1)}, u32[]{:S(2)}, u32[]{:S(2)}) collective-permute-start(f32[16,16,256]{2,1,0:T(8,128)S(1)} %shard_map.29), channel_id=1, source_target_pairs={{0,32},{32,64},{48,16},{64,96},{80,48},{112,80},{1,33},{33,65},{49... | collective-permute-start | bytes 786440 | tf_op jit(solution)/shard_map/ppermute | solution.py:306
  26.5 16.8 %collective-permute-start.9 = (f32[14,32,512]{2,1,0:T(8,128)S(1)}, f32[14,32,512]{2,1,0:T(8,128)S(1)}, u32[]{:S(2)}, u32[]{:S(2)}) collective-permute-start(f32[14,32,512]{2,1,0:T(8,128)S(1)} %get-tuple-element.28), channel_id=1, source_target_pairs={{1,2},{2,1},{3,4},{4,3},{5,6},{6,5},{7,8},{8,7},{9,10},{10,9},{11,... | collective-permute-start | bytes 2752520 | tf_op jit(solution)/shard_map/ppermute | solution.py:306
  28.4 6.8 %collective-permute-start.10 = (f32[14,32,512]{2,1,0:T(8,128)S(1)}, f32[14,32,512]{2,1,0:T(8,128)S(1)}, u32[]{:S(2)}, u32[]{:S(2)}) collective-permute-start(f32[14,32,512]{2,1,0:T(8,128)S(1)} %get-tuple-element.29), channel_id=1, source_target_pairs={{0,1},{1,0},{2,3},{3,2},{4,5},{5,4},{6,7},{7,6},{8,9},{9,8},{10,11... | collective-permute-start | bytes 2752520 | tf_op jit(solution)/shard_map/ppermute | solution.py:306
  31.0 17.2 %collective-permute-start.7 = (f32[14,16,512]{2,1,0:T(8,128)S(1)}, f32[14,16,512]{2,1,0:T(8,128)S(1)}, u32[]{:S(2)}, u32[]{:S(2)}) collective-permute-start(f32[14,16,512]{2,1,0:T(8,128)S(1)} %get-tuple-element.25), channel_id=1, source_target_pairs={{1,2},{2,1},{3,4},{4,3},{5,6},{6,5},{7,8},{8,7},{9,10},{10,9},{11,... | collective-permute-start | bytes 1376264 | tf_op jit(solution)/shard_map/ppermute | solution.py:306
  35.1 10.1 %collective-permute-start.8 = (f32[14,16,512]{2,1,0:T(8,128)S(1)}, f32[14,16,512]{2,1,0:T(8,128)S(1)}, u32[]{:S(2)}, u32[]{:S(2)}) collective-permute-start(f32[14,16,512]{2,1,0:T(8,128)S(1)} %get-tuple-element.26), channel_id=1, source_target_pairs={{0,1},{1,0},{2,3},{3,2},{4,5},{5,4},{6,7},{7,6},{8,9},{9,8},{10,11... | collective-permute-start | bytes 1376264 | tf_op jit(solution)/shard_map/ppermute | solution.py:306

commit v7 on v5

--- a/solution.py
+++ b/solution.py
@@ -74,11 +74,25 @@
     return acc
 
 
-def send_halos(full, link, core):
+def store_channel(c, value, full, link, core):
     chans = full.shape[0]
+    skip = chans - HALO
     odd = odd_of("chan")
-    link[...] = full[pl.ds((chans - HALO) * odd, HALO)]
-    core[...] = full[pl.ds((chans - HALO) * (1 - odd), HALO)]
+    full[c] = value
+    if skip <= c < HALO:
+        link[c - skip * odd] = value
+        core[c - skip * (1 - odd)] = value
+        return
+    at = c if c < skip else c - skip
+    first, second = (link, core) if c < skip else (core, link)
+
+    @pl.when(odd == 0)
+    def _():
+        first[at] = value
+
+    @pl.when(odd == 1)
+    def _():
+        second[at] = value
 
 
 def pair_rows_kernel(cells, near, edge_far, edge_near, full, link, core, field):
@@ -91,13 +105,8 @@
         field[:, 5 + r, :] = jnp.where(even, edge_far[r], edge_near[r])
         field[:, 40 + r, :] = jnp.where(even, edge_near[r], edge_far[r])
 
-    def channel(c, carry):
-        for part in range(2):
-            full[c, pl.ds(rows * part, rows), :] = smooth_rows(field, c, 8 + rows * part, rows)
-        return carry
-
-    lax.fori_loop(0, chans, channel, 0)
-    send_halos(full, link, core)
+    for c in range(chans):
+        store_channel(c, smooth_rows(field, c, 8, 2 * rows), full, link, core)
 
 
 def far_rows_kernel(far, edge, beyond, full, link, core, field):
@@ -110,12 +119,8 @@
         field[:, 5 + r, :] = jnp.where(even, beyond[r], edge[r])
         field[:, 24 + r, :] = jnp.where(even, edge[r], beyond[r])
 
-    def channel(c, carry):
-        full[c] = smooth_rows(field, c, 8, rows) * present
-        return carry
-
-    lax.fori_loop(0, chans, channel, 0)
-    send_halos(full, link, core)
+    for c in range(chans):
+        store_channel(c, smooth_rows(field, c, 8, rows) * present, full, link, core)
 
 
 def channel_pass(own, halo, down, row, tile, energy, before, boxes, kept_at):
@@ -266,32 +271,34 @@
 
     stride = energy.shape[2] // chans
 
-    def row_windows(w, even):
-        for half in range(2):
-            for tile in range(cols // LANES):
-                run = None
-                for d in range(rows):
-                    if d > 0:
-                        i = 16 - d if even else d - 1
-                        e = energy[w, tile, pl.ds(half * 8 * stride + i, 8, stride=stride), :]
-                        run = e if run is None else run + e
-                    row = 15 - d if even else d
-                    value = part[w, tile, half, row]
-                    at = pl.ds(half * 8 * stride + row, 8, stride=stride)
-                    sums[w, tile, at, :] = value if run is None else value + run
-
-    for_parity(odd, row_windows)
     kept = (1 - blanked[...]).astype(jnp.float32)
-    both = jnp.concatenate([band[...], band[...]], axis=0)
-    copies = []
-    for w, width in enumerate(WIDTHS):
-        total = jnp.dot(two_terms(sums, w), both, preferred_element_type=jnp.float32)
-        scale = lax.rsqrt(total * (1.0 / (VOLUME * width * width)) + 1e-5) * (1.0 / width)
-        ready[w] = boxes[w] * scale.reshape(chans, rows, cols) * kept[None]
-        copies.append(pltpu.make_async_copy(ready.at[w], out.at[w], sems.at[w]))
-        copies[-1].start()
-    for copy in copies:
-        copy.wait()
+
+    def finish(even):
+        both = jnp.concatenate([band[...], band[...]], axis=0)
+        copies = []
+        for w, width in enumerate(WIDTHS):
+            for half in range(2):
+                for tile in range(cols // LANES):
+                    run = None
+                    for d in range(rows):
+                        if d > 0:
+                            i = 16 - d if even else d - 1
+                            e = energy[w, tile, pl.ds(half * 8 * stride + i, 8, stride=stride), :]
+                            run = e if run is None else run + e
+                        row = 15 - d if even else d
+                        value = part[w, tile, half, row]
+                        at = pl.ds(half * 8 * stride + row, 8, stride=stride)
+                        sums[w, tile, at, :] = value if run is None else value + run
+            total = jnp.dot(two_terms(sums, w), both, preferred_element_type=jnp.float32)
+            scale = lax.rsqrt(total * (1.0 / (VOLUME * width * width)) + 1e-5) * (1.0 / width)
+            ready[w] = boxes[w] * scale.reshape(chans, rows, cols) * kept[None]
+            copies.append(pltpu.make_async_copy(ready.at[w], out.at[w], sems.at[w]))
+            copies[-1].start()
+        for copy in copies:
+            copy.wait()
+
+    pl.when(odd == 0)(lambda: finish(True))
+    pl.when(odd == 1)(lambda: finish(False))
 
 
 def per_device(data_cube, blanked):

time: 51.3 us -> 50.9 us (level)
  Pallas kernels: 9.82 us -> 9.11 us
  transfers between devices with their start and end apart: 9 -> 9, of which waited for: 5 -> 5; matrix products, arithmetic and copies ran while one was open for 0% -> 0% of each run, Pallas kernels for 11% -> 10%
where the time goes in v7:
time: 50.9 us; the launch traced here: 50.5 us
  starting transfers between devices  21.1 us (41%)
  waiting for transfers between devices  18.3 us (36%)
  Pallas kernels  9.11 us (18%)
  local copies, waits for them, and re-layouts  1.8 us (4%)
    ppermute x9, starting transfers between devices, move(): lax.ppermute(value, axis, [(a, b) for a, b in pairs if 0 <= b < count])  21.1 us
    ppermute x9, waiting for transfers between devices, move(): lax.ppermute(value, axis, [(a, b) for a, b in pairs if 0 <= b < count])  18.3 us
    pallas_call x1, Pallas kernels, per_device(): call(snr_kernel, f32(4, chans, rows, cols), [pltpu.VMEM((4, tiles, chans...  3.22 us
    pallas_call x1, Pallas kernels, per_device(): call(pair_noise_kernel, [f32(4, chans, rows, cols), f32(4, tiles, 2, rows...  1.94 us
    unnamed x6, local copies, waits for them, and re-layouts  1.8 us
    pallas_call x1, Pallas kernels, per_device(): call(pair_rows_kernel, [f32(chans, 32, cols), f32(HALO, 32, cols), f32(HA...  1.03 us
  transfers between devices with their start and end apart: 9, of which 5 were waited for; matrix products, arithmetic and copies ran while one was open for 0% of the time, Pallas kernels for 10%

profile of v7, /device:TPU:34, one launch (start us, length us, event | category | flops | bytes accessed | tf_op | source)
XLA Modules:
  0.0 50.5 jit_solution(3870395384523331340)
XLA Ops:
  0.0 0.0 copy-start
  0.0 1.0 %copy-done = f32[16,16,512]{2,1,0:T(8,128)S(1)} copy-done((f32[16,16,512]{2,1,0:T(8,128)S(1)}, f32[16,16,512]{2,1,0:T(8,128)}, u32[]{:S(2)}) %copy-start) | copy-done | bytes 524312
  1.0 0.0 copy-start.1
  1.0 0.8 %copy-done.1 = s32[16,512]{1,0:T(8,128)S(1)} copy-done((s32[16,512]{1,0:T(8,128)S(1)}, s32[16,512]{1,0:T(8,128)}, u32[]{:S(2)}) %copy-start.1) | copy-done | bytes 32792
  1.8 0.9 %shard_map.28 = (f32[16,16,512]{2,1,0:T(8,128)S(1)}, f32[3,16,512]{2,1,0:T(8,128)S(1)}, f32[3,16,512]{2,1,0:T(8,128)S(1)}) custom-call(f32[16,16,512]{2,1,0:T(8,128)S(1)} %copy-done, s32[16,512]{1,0:T(8,128)S(1)} %copy-done.1), custom_call_target="tpu_custom_call" | custom-call | flops 1000000000 | bytes 3000000 | tf_op jit(solution)/shard_map/pallas_call | solution.py:320
  2.7 3.1 %collective-permute-start = (f32[16,16,512]{2,1,0:T(8,128)S(1)}, f32[16,16,512]{2,1,0:T(8,128)S(1)}, u32[]{:S(2)}, u32[]{:S(2)}) collective-permute-start(f32[16,16,512]{2,1,0:T(8,128)S(1)} %get-tuple-element.19.cells), channel_id=1, source_target_pairs={{0,16},{16,0},{32,48},{48,32},{64,80},{80,64},{96,112},{112,96},{1... | collective-permute-start | bytes 1572872 | tf_op jit(solution)/shard_map/ppermute | solution.py:311
  5.8 3.4 %collective-permute-start.3 = (f32[3,16,512]{2,1,0:T(8,128)S(1)}, f32[3,16,512]{2,1,0:T(8,128)S(1)}, u32[]{:S(2)}, u32[]{:S(2)}) collective-permute-start(f32[3,16,512]{2,1,0:T(8,128)S(1)} %get-tuple-element.21), channel_id=1, source_target_pairs={{0,32},{32,64},{48,16},{64,96},{80,48},{112,80},{1,33},{33,65},{49... | collective-permute-start | bytes 294920 | tf_op jit(solution)/shard_map/ppermute | solution.py:311
  9.2 1.9 %collective-permute-start.2 = (f32[3,16,512]{2,1,0:T(8,128)S(1)}, f32[3,16,512]{2,1,0:T(8,128)S(1)}, u32[]{:S(2)}, u32[]{:S(2)}) collective-permute-start(f32[3,16,512]{2,1,0:T(8,128)S(1)} %get-tuple-element.20.edge), channel_id=1, source_target_pairs={{16,32},{32,16},{48,64},{64,48},{80,96},{96,80},{17,33},{33,17},{4... | collective-permute-start | bytes 294920 | tf_op jit(solution)/shard_map/ppermute | solution.py:311
  11.1 1.9 %collective-permute-start.1 = (f32[3,16,512]{2,1,0:T(8,128)S(1)}, f32[3,16,512]{2,1,0:T(8,128)S(1)}, u32[]{:S(2)}, u32[]{:S(2)}) collective-permute-start(f32[3,16,512]{2,1,0:T(8,128)S(1)} %get-tuple-element.20.edge), channel_id=1, source_target_pairs={{16,48},{32,0},{48,80},{64,32},{80,112},{96,64},{17,49},{33,1},{49... | collective-permute-start | bytes 294920 | tf_op jit(solution)/shard_map/ppermute | solution.py:311
  13.0 0.0 collective-permute-done.3.rest_2_.beyond
  13.0 5.1 %collective-permute-done.2.rest_1_.edge_far = f32[3,16,512]{2,1,0:T(8,128)S(1)} collective-permute-done((f32[3,16,512]{2,1,0:T(8,128)S(1)}, f32[3,16,512]{2,1,0:T(8,128)S(1)}, u32[]{:S(2)}, u32[]{:S(2)}) %collective-permute-start.2) | collective-permute-done | bytes 98336 | tf_op jit(solution)/shard_map/ppermute | solution.py:311
  18.2 0.0 collective-permute-done.1.rest_0_.edge_near
  18.2 1.9 %collective-permute-done.value = f32[16,16,512]{2,1,0:T(8,128)S(1)} collective-permute-done((f32[16,16,512]{2,1,0:T(8,128)S(1)}, f32[16,16,512]{2,1,0:T(8,128)S(1)}, u32[]{:S(2)}, u32[]{:S(2)}) %collective-permute-start) | collective-permute-done | bytes 524320 | tf_op jit(solution)/shard_map/ppermute | solution.py:311
  20.1 3.4 %collective-permute-start.4 = (f32[16,16,512]{2,1,0:T(8,128)S(1)}, f32[16,16,512]{2,1,0:T(8,128)S(1)}, u32[]{:S(2)}, u32[]{:S(2)}) collective-permute-start(f32[16,16,512]{2,1,0:T(8,128)S(1)} %shard_map.29.near), channel_id=1, source_target_pairs={{0,32},{32,64},{48,16},{64,96},{80,48},{112,80},{1,33},{33,65},{49... | collective-permute-start | bytes 1572872 | tf_op jit(solution)/shard_map/ppermute | solution.py:311
  23.5 1.0 %shard_map.31 = (f32[16,32,512]{2,1,0:T(8,128)S(1)}, f32[14,32,512]{2,1,0:T(8,128)S(1)}, f32[14,32,512]{2,1,0:T(8,128)S(1)}) custom-call(f32[16,16,512]{2,1,0:T(8,128)S(1)} %get-tuple-element.19.cells, f32[16,16,512]{2,1,0:T(8,128)S(1)} %shard_map.29.near, f32[3,16,512]{2,1,0:T(8,128)S(1)} %collective-permute-done.2.rest_1_.edge_far, ...), custom_call_target="tpu_custom_call" | custom-call | flops 10000000 | bytes 30000 | tf_op jit(solution)/shard_map/pallas_call | solution.py:336
  24.5 3.7 %collective-permute-start.7 = (f32[14,32,512]{2,1,0:T(8,128)S(1)}, f32[14,32,512]{2,1,0:T(8,128)S(1)}, u32[]{:S(2)}, u32[]{:S(2)}) collective-permute-start(f32[14,32,512]{2,1,0:T(8,128)S(1)} %get-tuple-element.26), channel_id=1, source_target_pairs={{1,2},{2,1},{3,4},{4,3},{5,6},{6,5},{7,8},{8,7},{9,10},{10,9},{11,... | collective-permute-start | bytes 2752520 | tf_op jit(solution)/shard_map/ppermute | solution.py:311
  28.2 0.1 collective-permute-start.8
  28.3 6.4 %collective-permute-done.4.far = f32[16,16,512]{2,1,0:T(8,128)S(1)} collective-permute-done((f32[16,16,512]{2,1,0:T(8,128)S(1)}, f32[16,16,512]{2,1,0:T(8,128)S(1)}, u32[]{:S(2)}, u32[]{:S(2)}) %collective-permute-start.4) | collective-permute-done | bytes 524320 | tf_op jit(solution)/shard_map/ppermute | solution.py:311
  34.7 0.6 %shard_map.30 = (f32[16,16,512]{2,1,0:T(8,128)S(1)}, f32[14,16,512]{2,1,0:T(8,128)S(1)}, f32[14,16,512]{2,1,0:T(8,128)S(1)}) custom-call(f32[16,16,512]{2,1,0:T(8,128)S(1)} %collective-permute-done.4.far, f32[3,16,512]{2,1,0:T(8,128)S(1)} %get-tuple-element.20.edge, f32[3,16,512]{2,1,0:T(8,128)S(1)} %collective-permute-done.3.rest_2_.beyond), custom_call_target="tpu_custom_call" | custom-call | flops 30000001024 | bytes 90000000 | tf_op jit(solution)/shard_map/pallas_call | solution.py:345
  35.4 3.4 %collective-permute-start.5 = (f32[14,16,512]{2,1,0:T(8,128)S(1)}, f32[14,16,512]{2,1,0:T(8,128)S(1)}, u32[]{:S(2)}, u32[]{:S(2)}) collective-permute-start(f32[14,16,512]{2,1,0:T(8,128)S(1)} %get-tuple-element.23), channel_id=1, source_target_pairs={{1,2},{2,1},{3,4},{4,3},{5,6},{6,5},{7,8},{8,7},{9,10},{10,9},{11,... | collective-permute-start | bytes 1376264 | tf_op jit(solution)/shard_map/ppermute | solution.py:311
  38.8 0.3 collective-permute-start.6
  39.1 0.0 collective-permute-done.8.core
  39.1 0.9 %shard_map.32 = (f32[4,4,640,128]{3,2,1,0:T(8,128)S(1)}, f32[4,8,16,512]{3,2,1,0:T(8,128)S(1)}) custom-call(f32[16,32,512]{2,1,0:T(8,128)S(1)} %get-tuple-element.25.own, f32[14,32,512]{2,1,0:T(8,128)S(1)} %collective-permute-done.8.core, f32[16,16,512]{2,1,0:T(8,128)S(1)} %get-tuple-element.22.after.own), custom_call_target="tpu_custom_call" | custom-call | flops 2000000000 | bytes 6000000 | tf_op jit(solution)/shard_map/pallas_call | solution.py:354
  40.0 1.3 %collective-permute-done.7.link = f32[14,32,512]{2,1,0:T(8,128)S(1)} collective-permute-done((f32[14,32,512]{2,1,0:T(8,128)S(1)}, f32[14,32,512]{2,1,0:T(8,128)S(1)}, u32[]{:S(2)}, u32[]{:S(2)}) %collective-permute-start.7) | collective-permute-done | bytes 917536 | tf_op jit(solution)/shard_map/ppermute | solution.py:311
  41.3 1.9 %shard_map.33 = (f32[4,16,16,512]{3,2,1,0:T(8,128)S(1)}, f32[4,4,2,16,8,128]{5,4,3,2,1,0:T(8,128)S(1)}, bf16[512,512]{1,0:T(8,128)(2,1)S(1)}) custom-call(f32[16,32,512]{2,1,0:T(8,128)S(1)} %get-tuple-element.25.own, f32[14,32,512]{2,1,0:T(8,128)S(1)} %collective-permute-done.7.link, f32[4,4,640,128]{3,2,1,0:T(8,128)S(1)} %get-tuple-element.28.before, ...), custom_call_target="tpu_custom_call" | custom-call | flops 3000000000 | bytes 9000000 | tf_op jit(solution)/shard_map/pallas_call | solution.py:360
  43.3 0.0 collective-permute-done.6.core
  43.3 0.0 copy-start.2
  43.3 0.5 shard_map.34.before
  43.8 3.5 %collective-permute-done.5.link = f32[14,16,512]{2,1,0:T(8,128)S(1)} collective-permute-done((f32[14,16,512]{2,1,0:T(8,128)S(1)}, f32[14,16,512]{2,1,0:T(8,128)S(1)}, u32[]{:S(2)}, u32[]{:S(2)}) %collective-permute-start.5) | collective-permute-done | bytes 458784 | tf_op jit(solution)/shard_map/ppermute | solution.py:311
  47.3 0.0 copy-done.2
  47.3 3.2 %shard_map.35 = f32[4,16,16,512]{3,2,1,0:T(8,128)} custom-call(f32[16,16,512]{2,1,0:T(8,128)S(1)} %get-tuple-element.22.after.own, f32[14,16,512]{2,1,0:T(8,128)S(1)} %collective-permute-done.5.link, f32[4,4,384,128]{3,2,1,0:T(8,128)S(1)} %shard_map.34.before, f32[4,4,2,16,8,128]{5,4,3,2,1,0:T(8,128)S(1)} %get-tuple-element.30.after.part, ...), custom_call_target="tpu_custom_call" | custom-call | flops 4000000000 | bytes 12000000 | tf_op jit(solution)/shard_map/pallas_call | solution.py:379
  (1 shorter events, 0.0 us)
Async XLA Ops:
  0.0 1.0 %copy-start = (f32[16,16,512]{2,1,0:T(8,128)S(1)}, f32[16,16,512]{2,1,0:T(8,128)}, u32[]{:S(2)}) copy-start(f32[16,16,512]{2,1,0:T(8,128)} %data.1) | copy-start | bytes 1572868
  1.0 0.8 %copy-start.1 = (s32[16,512]{1,0:T(8,128)S(1)}, s32[16,512]{1,0:T(8,128)}, u32[]{:S(2)}) copy-start(s32[16,512]{1,0:T(8,128)} %blanked.3) | copy-start | bytes 98308
  2.7 17.4 %collective-permute-start = (f32[16,16,512]{2,1,0:T(8,128)S(1)}, f32[16,16,512]{2,1,0:T(8,128)S(1)}, u32[]{:S(2)}, u32[]{:S(2)}) collective-permute-start(f32[16,16,512]{2,1,0:T(8,128)S(1)} %get-tuple-element.19.cells), channel_id=1, source_target_pairs={{0,16},{16,0},{32,48},{48,32},{64,80},{80,64},{96,112},{112,96},{1... | collective-permute-start | bytes 1572872 | tf_op jit(solution)/shard_map/ppermute | solution.py:311
  5.8 7.3 %collective-permute-start.3 = (f32[3,16,512]{2,1,0:T(8,128)S(1)}, f32[3,16,512]{2,1,0:T(8,128)S(1)}, u32[]{:S(2)}, u32[]{:S(2)}) collective-permute-start(f32[3,16,512]{2,1,0:T(8,128)S(1)} %get-tuple-element.21), channel_id=1, source_target_pairs={{0,32},{32,64},{48,16},{64,96},{80,48},{112,80},{1,33},{33,65},{49... | collective-permute-start | bytes 294920 | tf_op jit(solution)/shard_map/ppermute | solution.py:311
  9.2 9.0 %collective-permute-start.2 = (f32[3,16,512]{2,1,0:T(8,128)S(1)}, f32[3,16,512]{2,1,0:T(8,128)S(1)}, u32[]{:S(2)}, u32[]{:S(2)}) collective-permute-start(f32[3,16,512]{2,1,0:T(8,128)S(1)} %get-tuple-element.20.edge), channel_id=1, source_target_pairs={{16,32},{32,16},{48,64},{64,48},{80,96},{96,80},{17,33},{33,17},{4... | collective-permute-start | bytes 294920 | tf_op jit(solution)/shard_map/ppermute | solution.py:311
  11.1 7.1 %collective-permute-start.1 = (f32[3,16,512]{2,1,0:T(8,128)S(1)}, f32[3,16,512]{2,1,0:T(8,128)S(1)}, u32[]{:S(2)}, u32[]{:S(2)}) collective-permute-start(f32[3,16,512]{2,1,0:T(8,128)S(1)} %get-tuple-element.20.edge), channel_id=1, source_target_pairs={{16,48},{32,0},{48,80},{64,32},{80,112},{96,64},{17,49},{33,1},{49... | collective-permute-start | bytes 294920 | tf_op jit(solution)/shard_map/ppermute | solution.py:311
  20.1 14.7 %collective-permute-start.4 = (f32[16,16,512]{2,1,0:T(8,128)S(1)}, f32[16,16,512]{2,1,0:T(8,128)S(1)}, u32[]{:S(2)}, u32[]{:S(2)}) collective-permute-start(f32[16,16,512]{2,1,0:T(8,128)S(1)} %shard_map.29.near), channel_id=1, source_target_pairs={{0,32},{32,64},{48,16},{64,96},{80,48},{112,80},{1,33},{33,65},{49... | collective-permute-start | bytes 1572872 | tf_op jit(solution)/shard_map/ppermute | solution.py:311
  24.5 16.8 %collective-permute-start.7 = (f32[14,32,512]{2,1,0:T(8,128)S(1)}, f32[14,32,512]{2,1,0:T(8,128)S(1)}, u32[]{:S(2)}, u32[]{:S(2)}) collective-permute-start(f32[14,32,512]{2,1,0:T(8,128)S(1)} %get-tuple-element.26), channel_id=1, source_target_pairs={{1,2},{2,1},{3,4},{4,3},{5,6},{6,5},{7,8},{8,7},{9,10},{10,9},{11,... | collective-permute-start | bytes 2752520 | tf_op jit(solution)/shard_map/ppermute | solution.py:311
  28.2 10.9 %collective-permute-start.8 = (f32[14,32,512]{2,1,0:T(8,128)S(1)}, f32[14,32,512]{2,1,0:T(8,128)S(1)}, u32[]{:S(2)}, u32[]{:S(2)}) collective-permute-start(f32[14,32,512]{2,1,0:T(8,128)S(1)} %get-tuple-element.27), channel_id=1, source_target_pairs={{0,1},{1,0},{2,3},{3,2},{4,5},{5,4},{6,7},{7,6},{8,9},{9,8},{10,11... | collective-permute-start | bytes 2752520 | tf_op jit(solution)/shard_map/ppermute | solution.py:311
  35.4 11.9 %collective-permute-start.5 = (f32[14,16,512]{2,1,0:T(8,128)S(1)}, f32[14,16,512]{2,1,0:T(8,128)S(1)}, u32[]{:S(2)}, u32[]{:S(2)}) collective-permute-start(f32[14,16,512]{2,1,0:T(8,128)S(1)} %get-tuple-element.23), channel_id=1, source_target_pairs={{1,2},{2,1},{3,4},{4,3},{5,6},{6,5},{7,8},{8,7},{9,10},{10,9},{11,... | collective-permute-start | bytes 1376264 | tf_op jit(solution)/shard_map/ppermute | solution.py:311
  38.8 4.5 %collective-permute-start.6 = (f32[14,16,512]{2,1,0:T(8,128)S(1)}, f32[14,16,512]{2,1,0:T(8,128)S(1)}, u32[]{:S(2)}, u32[]{:S(2)}) collective-permute-start(f32[14,16,512]{2,1,0:T(8,128)S(1)} %get-tuple-element.24), channel_id=1, source_target_pairs={{0,1},{1,0},{2,3},{3,2},{4,5},{5,4},{6,7},{7,6},{8,9},{9,8},{10,11... | collective-permute-start | bytes 1376264 | tf_op jit(solution)/shard_map/ppermute | solution.py:311
  43.3 4.0 %copy-start.2 = (s32[16,512]{1,0:T(8,128)S(1)}, s32[16,512]{1,0:T(8,128)}, u32[]{:S(2)}) copy-start(s32[16,512]{1,0:T(8,128)} %blanked.3) | copy-start | bytes 98308

commit v8 on v7

--- a/solution.py
+++ b/solution.py
@@ -43,7 +43,7 @@
     return lax.axis_index(axis) % 2
 
 
-def clean_cols_kernel(data, blanked, cells, edge, edge2):
+def clean_cols_kernel(data, blanked, cells, second, edge, edge2):
     taps = kernel_taps()
     chans, rows, cols = data.shape
     even = odd_of("pix") == 0
@@ -57,6 +57,7 @@
             right = jnp.where(lane < cols - t, pltpu.roll(x, cols - t, 1), 0.0)
             acc = acc + taps[3 + t] * (left + right)
         cells[c] = acc
+        second[c] = acc[:, cols - second.shape[2] :]
     for r in range(3):
         top = cells[:, r, :]
         bottom = cells[:, rows - 3 + r, :]
@@ -109,12 +110,13 @@
         store_channel(c, smooth_rows(field, c, 8, 2 * rows), full, link, core)
 
 
-def far_rows_kernel(far, edge, beyond, full, link, core, field):
-    chans, rows, cols = far.shape
+def far_rows_kernel(far1, far2, edge, beyond, full, link, core, field):
+    chans, rows, half = far1.shape
     at, count = lax.axis_index("pix"), lax.axis_size("pix")
     even = odd_of("pix") == 0
     present = jnp.logical_and(at > 0, at < count - 1).astype(jnp.float32)
-    field[:, 8:24, :] = far[...]
+    field[:, 8:24, :half] = far1[...]
+    field[:, 8:24, half:] = far2[...]
     for r in range(3):
         field[:, 5 + r, :] = jnp.where(even, beyond[r], edge[r])
         field[:, 24 + r, :] = jnp.where(even, edge[r], beyond[r])
@@ -317,21 +319,24 @@
 
     toward = [(i, i + 2 if i % 2 == 0 else i - 2) for i in range(pix)]
     back = [(i, i - 2 if i % 2 == 0 else i + 2) for i in range(pix)]
-    cells, edge, edge2 = call(
-        clean_cols_kernel, [f32(chans, rows, cols), f32(3, chans, cols), f32(3, chans, cols)]
+    half = cols // 2
+    cells, right, edge, edge2 = call(
+        clean_cols_kernel,
+        [f32(chans, rows, cols), f32(chans, rows, half), f32(3, chans, cols), f32(3, chans, cols)],
     )(data_cube, blanked)
     near = swap(cells, "pix", 0)
+    far_right = swap(move(right, "pix", back), "pix", 0)
     edge_near = move(edge, "pix", back)
     edge_far = swap(edge, "pix", 1)
     beyond = move(edge2, "pix", toward)
-    near = call(
-        lambda value, *rest: None,
-        f32(*near.shape),
-        in_specs=[ANY] * 4,
-        out_specs=ANY,
-        input_output_aliases={0: 0},
-    )(near, edge_near, edge_far, beyond)
-    far = move(near, "pix", toward)
+
+    def left_half(value, *rest):
+        rest[-1][...] = value[:, :, : rest[-1].shape[2]]
+
+    near_left = call(left_half, f32(chans, rows, half), in_specs=[VMEM] + [ANY] * 3)(
+        near, edge_near, edge_far, beyond
+    )
+    far_left = move(near_left, "pix", toward)
 
     pair, pair_link, pair_core = call(
         pair_rows_kernel,
@@ -347,7 +352,7 @@
         [f32(chans, 16, cols), f32(HALO, 16, cols), f32(HALO, 16, cols)],
         [pltpu.VMEM((chans, 32, cols), jnp.float32)],
         micros=30.0,
-    )(far, edge, beyond)
+    )(far_left, far_right, edge, beyond)
     outer_link = swap(outer_link, "chan", 1)
     outer_core = swap(outer_core, "chan", 0)
 

time: 50.9 us -> 51.5 us (1.012)
  starting transfers between devices: 21.1 us -> 29.4 us
  waiting for transfers between devices: 18.3 us -> 10.6 us
    ppermute x9 -> x11, starting transfers between devices: 21.1 us -> 29.4 us  [move(): lax.ppermute(value, axis, [(a, b) for a, b in pairs if 0 <= b < count])]
    ppermute x9 -> x11, waiting for transfers between devices: 18.3 us -> 10.6 us  [move(): lax.ppermute(value, axis, [(a, b) for a, b in pairs if 0 <= b < count])]
    unnamed x6 -> x4, local copies, waits for them, and re-layouts: 1.8 us -> 1.8 us
  transfers between devices with their start and end apart: 9 -> 11, of which waited for: 5 -> 4; matrix products, arithmetic and copies ran while one was open for 0% -> 0% of each run, Pallas kernels for 10% -> 10%
where the time goes in v8:
time: 51.5 us; the launch traced here: 51.1 us
  starting transfers between devices  29.4 us (57%)
  waiting for transfers between devices  10.6 us (21%)
  Pallas kernels  9.18 us (18%)
  local copies, waits for them, and re-layouts  1.8 us (3%)
    ppermute x11, starting transfers between devices, move(): lax.ppermute(value, axis, [(a, b) for a, b in pairs if 0 <= b < count])  29.4 us
    ppermute x11, waiting for transfers between devices, move(): lax.ppermute(value, axis, [(a, b) for a, b in pairs if 0 <= b < count])  10.6 us
    pallas_call x1, Pallas kernels, per_device(): call(snr_kernel, f32(4, chans, rows, cols), [pltpu.VMEM((4, tiles, chans...  3.25 us
    pallas_call x1, Pallas kernels, per_device(): call(pair_noise_kernel, [f32(4, chans, rows, cols), f32(4, tiles, 2, rows...  1.94 us
    unnamed x4, local copies, waits for them, and re-layouts  1.8 us
  transfers between devices with their start and end apart: 11, of which 4 were waited for; matrix products, arithmetic and copies ran while one was open for 0% of the time, Pallas kernels for 10%

profile of v8, /device:TPU:34, one launch (start us, length us, event | category | flops | bytes accessed | tf_op | source)
XLA Modules:
  0.0 51.1 jit_solution(3622003233787564124)
XLA Ops:
  0.0 0.0 copy-start
  0.0 1.0 %copy-done = f32[16,16,512]{2,1,0:T(8,128)S(1)} copy-done((f32[16,16,512]{2,1,0:T(8,128)S(1)}, f32[16,16,512]{2,1,0:T(8,128)}, u32[]{:S(2)}) %copy-start) | copy-done | bytes 524312
  1.0 0.0 copy-start.1
  1.0 0.8 %copy-done.1 = s32[16,512]{1,0:T(8,128)S(1)} copy-done((s32[16,512]{1,0:T(8,128)S(1)}, s32[16,512]{1,0:T(8,128)}, u32[]{:S(2)}) %copy-start.1) | copy-done | bytes 32792
  1.8 0.9 %shard_map.28 = (f32[16,16,512]{2,1,0:T(8,128)S(1)}, f32[16,16,256]{2,1,0:T(8,128)S(1)}, f32[3,16,512]{2,1,0:T(8,128)S(1)}, f32[3,16,512]{2,1,0:T(8,128)S(1)}) custom-call(f32[16,16,512]{2,1,0:T(8,128)S(1)} %copy-done, s32[16,512]{1,0:T(8,128)S(1)} %copy-done.1), custom_call_target="tpu_custom_call" | custom-call | flops 1000000000 | bytes 3000000 | tf_op jit(solution)/shard_map/pallas_call | solution.py:323
  2.7 3.1 %collective-permute-start = (f32[16,16,512]{2,1,0:T(8,128)S(1)}, f32[16,16,512]{2,1,0:T(8,128)S(1)}, u32[]{:S(2)}, u32[]{:S(2)}) collective-permute-start(f32[16,16,512]{2,1,0:T(8,128)S(1)} %get-tuple-element.20.cells), channel_id=1, source_target_pairs={{0,16},{16,0},{32,48},{48,32},{64,80},{80,64},{96,112},{112,96},{1... | collective-permute-start | bytes 1572872 | tf_op jit(solution)/shard_map/ppermute | solution.py:313
  5.8 2.4 %collective-permute-start.5 = (f32[16,16,256]{2,1,0:T(8,128)S(1)}, f32[16,16,256]{2,1,0:T(8,128)S(1)}, u32[]{:S(2)}, u32[]{:S(2)}) collective-permute-start(f32[16,16,256]{2,1,0:T(8,128)S(1)} %get-tuple-element.23), channel_id=1, source_target_pairs={{16,48},{32,0},{48,80},{64,32},{80,112},{96,64},{17,49},{33,1},{49... | collective-permute-start | bytes 786440 | tf_op jit(solution)/shard_map/ppermute | solution.py:313
  8.2 3.4 %collective-permute-start.3 = (f32[3,16,512]{2,1,0:T(8,128)S(1)}, f32[3,16,512]{2,1,0:T(8,128)S(1)}, u32[]{:S(2)}, u32[]{:S(2)}) collective-permute-start(f32[3,16,512]{2,1,0:T(8,128)S(1)} %get-tuple-element.22), channel_id=1, source_target_pairs={{0,32},{32,64},{48,16},{64,96},{80,48},{112,80},{1,33},{33,65},{49... | collective-permute-start | bytes 294920 | tf_op jit(solution)/shard_map/ppermute | solution.py:313
  11.6 1.9 %collective-permute-start.2 = (f32[3,16,512]{2,1,0:T(8,128)S(1)}, f32[3,16,512]{2,1,0:T(8,128)S(1)}, u32[]{:S(2)}, u32[]{:S(2)}) collective-permute-start(f32[3,16,512]{2,1,0:T(8,128)S(1)} %get-tuple-element.21.edge), channel_id=1, source_target_pairs={{16,32},{32,16},{48,64},{64,48},{80,96},{96,80},{17,33},{33,17},{4... | collective-permute-start | bytes 294920 | tf_op jit(solution)/shard_map/ppermute | solution.py:313
  13.5 1.9 %collective-permute-start.1 = (f32[3,16,512]{2,1,0:T(8,128)S(1)}, f32[3,16,512]{2,1,0:T(8,128)S(1)}, u32[]{:S(2)}, u32[]{:S(2)}) collective-permute-start(f32[3,16,512]{2,1,0:T(8,128)S(1)} %get-tuple-element.21.edge), channel_id=1, source_target_pairs={{16,48},{32,0},{48,80},{64,32},{80,112},{96,64},{17,49},{33,1},{49... | collective-permute-start | bytes 294920 | tf_op jit(solution)/shard_map/ppermute | solution.py:313
  15.5 0.2 collective-permute-done.5
  15.7 4.3 %collective-permute-start.6 = (f32[16,16,256]{2,1,0:T(8,128)S(1)}, f32[16,16,256]{2,1,0:T(8,128)S(1)}, u32[]{:S(2)}, u32[]{:S(2)}) collective-permute-start(f32[16,16,256]{2,1,0:T(8,128)S(1)} %collective-permute-done.5), channel_id=1, source_target_pairs={{0,16},{16,0},{32,48},{48,32},{64,80},{80,64},{96,112},{112,96},{1... | collective-permute-start | bytes 786440 | tf_op jit(solution)/shard_map/ppermute | solution.py:313
  20.0 0.0 collective-permute-done.3.rest_2_.beyond
  20.0 0.6 %collective-permute-done.2.rest_1_.edge_far = f32[3,16,512]{2,1,0:T(8,128)S(1)} collective-permute-done((f32[3,16,512]{2,1,0:T(8,128)S(1)}, f32[3,16,512]{2,1,0:T(8,128)S(1)}, u32[]{:S(2)}, u32[]{:S(2)}) %collective-permute-start.2) | collective-permute-done | bytes 98336 | tf_op jit(solution)/shard_map/ppermute | solution.py:313
  20.6 0.0 collective-permute-done.1.rest_0_.edge_near
  20.6 0.0 collective-permute-done.value.near
  20.7 4.4 %collective-permute-start.4 = (f32[16,16,256]{2,1,0:T(8,128)S(1)}, f32[16,16,256]{2,1,0:T(8,128)S(1)}, u32[]{:S(2)}, u32[]{:S(2)}) collective-permute-start(f32[16,16,256]{2,1,0:T(8,128)S(1)} %shard_map.29), channel_id=1, source_target_pairs={{0,32},{32,64},{48,16},{64,96},{80,48},{112,80},{1,33},{33,65},{49... | collective-permute-start | bytes 786440 | tf_op jit(solution)/shard_map/ppermute | solution.py:313
  25.1 1.0 %shard_map.31 = (f32[16,32,512]{2,1,0:T(8,128)S(1)}, f32[14,32,512]{2,1,0:T(8,128)S(1)}, f32[14,32,512]{2,1,0:T(8,128)S(1)}) custom-call(f32[16,16,512]{2,1,0:T(8,128)S(1)} %get-tuple-element.20.cells, f32[16,16,512]{2,1,0:T(8,128)S(1)} %collective-permute-done.value.near, f32[3,16,512]{2,1,0:T(8,128)S(1)} %collective-permute-done.2.rest_1_.edge_far, ...), custom_call_target="tpu_custom_call" | custom-call | flops 10000000 | bytes 30000 | tf_op jit(solution)/shard_map/pallas_call | solution.py:341
  26.1 1.9 %collective-permute-start.9 = (f32[14,32,512]{2,1,0:T(8,128)S(1)}, f32[14,32,512]{2,1,0:T(8,128)S(1)}, u32[]{:S(2)}, u32[]{:S(2)}) collective-permute-start(f32[14,32,512]{2,1,0:T(8,128)S(1)} %get-tuple-element.28), channel_id=1, source_target_pairs={{1,2},{2,1},{3,4},{4,3},{5,6},{6,5},{7,8},{8,7},{9,10},{10,9},{11,... | collective-permute-start | bytes 2752520 | tf_op jit(solution)/shard_map/ppermute | solution.py:313
  28.1 1.8 %collective-permute-start.10 = (f32[14,32,512]{2,1,0:T(8,128)S(1)}, f32[14,32,512]{2,1,0:T(8,128)S(1)}, u32[]{:S(2)}, u32[]{:S(2)}) collective-permute-start(f32[14,32,512]{2,1,0:T(8,128)S(1)} %get-tuple-element.29), channel_id=1, source_target_pairs={{0,1},{1,0},{2,3},{3,2},{4,5},{5,4},{6,7},{7,6},{8,9},{9,8},{10,11... | collective-permute-start | bytes 2752520 | tf_op jit(solution)/shard_map/ppermute | solution.py:313
  29.8 0.0 collective-permute-done.6.far2
  29.8 0.0 collective-permute-done.4.far1
  29.8 0.6 %shard_map.30 = (f32[16,16,512]{2,1,0:T(8,128)S(1)}, f32[14,16,512]{2,1,0:T(8,128)S(1)}, f32[14,16,512]{2,1,0:T(8,128)S(1)}) custom-call(f32[16,16,256]{2,1,0:T(8,128)S(1)} %collective-permute-done.4.far1, f32[16,16,256]{2,1,0:T(8,128)S(1)} %collective-permute-done.6.far2, f32[3,16,512]{2,1,0:T(8,128)S(1)} %get-tuple-element.21.edge, ...), custom_call_target="tpu_custom_call" | custom-call | flops 30000001024 | bytes 90000000 | tf_op jit(solution)/shard_map/pallas_call | solution.py:350
  30.5 4.1 %collective-permute-start.7 = (f32[14,16,512]{2,1,0:T(8,128)S(1)}, f32[14,16,512]{2,1,0:T(8,128)S(1)}, u32[]{:S(2)}, u32[]{:S(2)}) collective-permute-start(f32[14,16,512]{2,1,0:T(8,128)S(1)} %get-tuple-element.25), channel_id=1, source_target_pairs={{1,2},{2,1},{3,4},{4,3},{5,6},{6,5},{7,8},{8,7},{9,10},{10,9},{11,... | collective-permute-start | bytes 1376264 | tf_op jit(solution)/shard_map/ppermute | solution.py:313
  34.6 0.1 collective-permute-start.8
  34.7 0.0 collective-permute-done.10.core
  34.7 0.9 %shard_map.32 = (f32[4,4,640,128]{3,2,1,0:T(8,128)S(1)}, f32[4,8,16,512]{3,2,1,0:T(8,128)S(1)}) custom-call(f32[16,32,512]{2,1,0:T(8,128)S(1)} %get-tuple-element.27.own, f32[14,32,512]{2,1,0:T(8,128)S(1)} %collective-permute-done.10.core, f32[16,16,512]{2,1,0:T(8,128)S(1)} %get-tuple-element.24.after.own), custom_call_target="tpu_custom_call" | custom-call | flops 2000000000 | bytes 6000000 | tf_op jit(solution)/shard_map/pallas_call | solution.py:359
  35.6 7.3 %collective-permute-done.9.link = f32[14,32,512]{2,1,0:T(8,128)S(1)} collective-permute-done((f32[14,32,512]{2,1,0:T(8,128)S(1)}, f32[14,32,512]{2,1,0:T(8,128)S(1)}, u32[]{:S(2)}, u32[]{:S(2)}) %collective-permute-start.9) | collective-permute-done | bytes 917536 | tf_op jit(solution)/shard_map/ppermute | solution.py:313
  42.9 1.9 %shard_map.33 = (f32[4,16,16,512]{3,2,1,0:T(8,128)S(1)}, f32[4,4,2,16,8,128]{5,4,3,2,1,0:T(8,128)S(1)}, bf16[512,512]{1,0:T(8,128)(2,1)S(1)}) custom-call(f32[16,32,512]{2,1,0:T(8,128)S(1)} %get-tuple-element.27.own, f32[14,32,512]{2,1,0:T(8,128)S(1)} %collective-permute-done.9.link, f32[4,4,640,128]{3,2,1,0:T(8,128)S(1)} %get-tuple-element.30.before, ...), custom_call_target="tpu_custom_call" | custom-call | flops 3000000000 | bytes 9000000 | tf_op jit(solution)/shard_map/pallas_call | solution.py:365
  44.9 0.0 collective-permute-done.8.core
  44.9 0.5 shard_map.34.before
  45.4 2.5 %collective-permute-done.7.link = f32[14,16,512]{2,1,0:T(8,128)S(1)} collective-permute-done((f32[14,16,512]{2,1,0:T(8,128)S(1)}, f32[14,16,512]{2,1,0:T(8,128)S(1)}, u32[]{:S(2)}, u32[]{:S(2)}) %collective-permute-start.7) | collective-permute-done | bytes 458784 | tf_op jit(solution)/shard_map/ppermute | solution.py:313
  47.9 3.2 %shard_map.35 = f32[4,16,16,512]{3,2,1,0:T(8,128)} custom-call(f32[16,16,512]{2,1,0:T(8,128)S(1)} %get-tuple-element.24.after.own, f32[14,16,512]{2,1,0:T(8,128)S(1)} %collective-permute-done.7.link, f32[4,4,384,128]{3,2,1,0:T(8,128)S(1)} %shard_map.34.before, f32[4,4,2,16,8,128]{5,4,3,2,1,0:T(8,128)S(1)} %get-tuple-element.32.after.part, ...), custom_call_target="tpu_custom_call" | custom-call | flops 4000000000 | bytes 12000000 | tf_op jit(solution)/shard_map/pallas_call | solution.py:384
  (1 shorter events, 0.0 us)
Async XLA Ops:
  0.0 1.0 %copy-start = (f32[16,16,512]{2,1,0:T(8,128)S(1)}, f32[16,16,512]{2,1,0:T(8,128)}, u32[]{:S(2)}) copy-start(f32[16,16,512]{2,1,0:T(8,128)} %data.1) | copy-start | bytes 1572868
  1.0 0.8 %copy-start.1 = (s32[16,512]{1,0:T(8,128)S(1)}, s32[16,512]{1,0:T(8,128)}, u32[]{:S(2)}) copy-start(s32[16,512]{1,0:T(8,128)} %blanked.3) | copy-start | bytes 98308
  2.7 17.9 %collective-permute-start = (f32[16,16,512]{2,1,0:T(8,128)S(1)}, f32[16,16,512]{2,1,0:T(8,128)S(1)}, u32[]{:S(2)}, u32[]{:S(2)}) collective-permute-start(f32[16,16,512]{2,1,0:T(8,128)S(1)} %get-tuple-element.20.cells), channel_id=1, source_target_pairs={{0,16},{16,0},{32,48},{48,32},{64,80},{80,64},{96,112},{112,96},{1... | collective-permute-start | bytes 1572872 | tf_op jit(solution)/shard_map/ppermute | solution.py:313
  5.8 9.9 %collective-permute-start.5 = (f32[16,16,256]{2,1,0:T(8,128)S(1)}, f32[16,16,256]{2,1,0:T(8,128)S(1)}, u32[]{:S(2)}, u32[]{:S(2)}) collective-permute-start(f32[16,16,256]{2,1,0:T(8,128)S(1)} %get-tuple-element.23), channel_id=1, source_target_pairs={{16,48},{32,0},{48,80},{64,32},{80,112},{96,64},{17,49},{33,1},{49... | collective-permute-start | bytes 786440 | tf_op jit(solution)/shard_map/ppermute | solution.py:313
  8.2 11.8 %collective-permute-start.3 = (f32[3,16,512]{2,1,0:T(8,128)S(1)}, f32[3,16,512]{2,1,0:T(8,128)S(1)}, u32[]{:S(2)}, u32[]{:S(2)}) collective-permute-start(f32[3,16,512]{2,1,0:T(8,128)S(1)} %get-tuple-element.22), channel_id=1, source_target_pairs={{0,32},{32,64},{48,16},{64,96},{80,48},{112,80},{1,33},{33,65},{49... | collective-permute-start | bytes 294920 | tf_op jit(solution)/shard_map/ppermute | solution.py:313
  11.6 9.0 %collective-permute-start.2 = (f32[3,16,512]{2,1,0:T(8,128)S(1)}, f32[3,16,512]{2,1,0:T(8,128)S(1)}, u32[]{:S(2)}, u32[]{:S(2)}) collective-permute-start(f32[3,16,512]{2,1,0:T(8,128)S(1)} %get-tuple-element.21.edge), channel_id=1, source_target_pairs={{16,32},{32,16},{48,64},{64,48},{80,96},{96,80},{17,33},{33,17},{4... | collective-permute-start | bytes 294920 | tf_op jit(solution)/shard_map/ppermute | solution.py:313
  13.5 7.1 %collective-permute-start.1 = (f32[3,16,512]{2,1,0:T(8,128)S(1)}, f32[3,16,512]{2,1,0:T(8,128)S(1)}, u32[]{:S(2)}, u32[]{:S(2)}) collective-permute-start(f32[3,16,512]{2,1,0:T(8,128)S(1)} %get-tuple-element.21.edge), channel_id=1, source_target_pairs={{16,48},{32,0},{48,80},{64,32},{80,112},{96,64},{17,49},{33,1},{49... | collective-permute-start | bytes 294920 | tf_op jit(solution)/shard_map/ppermute | solution.py:313
  15.7 14.1 %collective-permute-start.6 = (f32[16,16,256]{2,1,0:T(8,128)S(1)}, f32[16,16,256]{2,1,0:T(8,128)S(1)}, u32[]{:S(2)}, u32[]{:S(2)}) collective-permute-start(f32[16,16,256]{2,1,0:T(8,128)S(1)} %collective-permute-done.5), channel_id=1, source_target_pairs={{0,16},{16,0},{32,48},{48,32},{64,80},{80,64},{96,112},{112,96},{1... | collective-permute-start | bytes 786440 | tf_op jit(solution)/shard_map/ppermute | solution.py:313
  20.7 9.2 %collective-permute-start.4 = (f32[16,16,256]{2,1,0:T(8,128)S(1)}, f32[16,16,256]{2,1,0:T(8,128)S(1)}, u32[]{:S(2)}, u32[]{:S(2)}) collective-permute-start(f32[16,16,256]{2,1,0:T(8,128)S(1)} %shard_map.29), channel_id=1, source_target_pairs={{0,32},{32,64},{48,16},{64,96},{80,48},{112,80},{1,33},{33,65},{49... | collective-permute-start | bytes 786440 | tf_op jit(solution)/shard_map/ppermute | solution.py:313
  26.1 16.8 %collective-permute-start.9 = (f32[14,32,512]{2,1,0:T(8,128)S(1)}, f32[14,32,512]{2,1,0:T(8,128)S(1)}, u32[]{:S(2)}, u32[]{:S(2)}) collective-permute-start(f32[14,32,512]{2,1,0:T(8,128)S(1)} %get-tuple-element.28), channel_id=1, source_target_pairs={{1,2},{2,1},{3,4},{4,3},{5,6},{6,5},{7,8},{8,7},{9,10},{10,9},{11,... | collective-permute-start | bytes 2752520 | tf_op jit(solution)/shard_map/ppermute | solution.py:313
  28.1 6.6 %collective-permute-start.10 = (f32[14,32,512]{2,1,0:T(8,128)S(1)}, f32[14,32,512]{2,1,0:T(8,128)S(1)}, u32[]{:S(2)}, u32[]{:S(2)}) collective-permute-start(f32[14,32,512]{2,1,0:T(8,128)S(1)} %get-tuple-element.29), channel_id=1, source_target_pairs={{0,1},{1,0},{2,3},{3,2},{4,5},{5,4},{6,7},{7,6},{8,9},{9,8},{10,11... | collective-permute-start | bytes 2752520 | tf_op jit(solution)/shard_map/ppermute | solution.py:313
  30.5 17.4 %collective-permute-start.7 = (f32[14,16,512]{2,1,0:T(8,128)S(1)}, f32[14,16,512]{2,1,0:T(8,128)S(1)}, u32[]{:S(2)}, u32[]{:S(2)}) collective-permute-start(f32[14,16,512]{2,1,0:T(8,128)S(1)} %get-tuple-element.25), channel_id=1, source_target_pairs={{1,2},{2,1},{3,4},{4,3},{5,6},{6,5},{7,8},{8,7},{9,10},{10,9},{11,... | collective-permute-start | bytes 1376264 | tf_op jit(solution)/shard_map/ppermute | solution.py:313
  34.6 10.3 %collective-permute-start.8 = (f32[14,16,512]{2,1,0:T(8,128)S(1)}, f32[14,16,512]{2,1,0:T(8,128)S(1)}, u32[]{:S(2)}, u32[]{:S(2)}) collective-permute-start(f32[14,16,512]{2,1,0:T(8,128)S(1)} %get-tuple-element.26), channel_id=1, source_target_pairs={{0,1},{1,0},{2,3},{3,2},{4,5},{5,4},{6,7},{7,6},{8,9},{9,8},{10,11... | collective-permute-start | bytes 1376264 | tf_op jit(solution)/shard_map/ppermute | solution.py:313

commit v9 on v7

--- a/solution.py
+++ b/solution.py
@@ -208,11 +208,12 @@
 
 def two_terms(sums, w):
     tiles, height = sums.shape[1:3]
-    value = jnp.concatenate([sums[w, tile] for tile in range(tiles)], axis=1)
-    value = value.reshape(16, height // 16, tiles * LANES)[:, :16].reshape(256, tiles * LANES)
-    first = value.astype(jnp.bfloat16)
-    second = (value - first.astype(jnp.float32)).astype(jnp.bfloat16)
-    return jnp.concatenate([first, second], axis=1)
+    firsts, seconds = [], []
+    for tile in range(tiles):
+        value = sums[w, tile].reshape(16, height // 16, LANES)[:, :16].reshape(256, LANES)
+        firsts.append(value.astype(jnp.bfloat16))
+        seconds.append((value - firsts[-1].astype(jnp.float32)).astype(jnp.bfloat16))
+    return firsts, seconds
 
 
 def for_parity(odd, body):
@@ -227,15 +228,20 @@
     pl.when(odd == 1)(lambda: loop(False))
 
 
-def pair_noise_kernel(own, link, before, core_boxes, after, boxes, sums, band, link_boxes, energy):
+def pair_noise_kernel(
+    own, link, before, core_boxes, blanked, after, boxes, sums, band, link_boxes, energy
+):
     chans, tall, cols = own.shape
     rows = tall // 2
     odd = odd_of("pix")
     strips(own, link, False, energy, before, link_boxes)
     low = pl.ds(8 * odd_of("chan"), 8)
     high = pl.ds(8 - 8 * odd_of("chan"), 8)
-    boxes[:, low] = link_boxes[...]
-    boxes[:, high] = core_boxes[...]
+    kept = (1 - blanked[...]).astype(jnp.float32)
+    for w, width in enumerate(WIDTHS):
+        factor = (kept * (1.0 / width))[None]
+        boxes[w, low] = link_boxes[w] * factor
+        boxes[w, high] = core_boxes[w] * factor
 
     stride = energy.shape[2] // chans
 
@@ -256,14 +262,14 @@
                     sums[w, tile, half, d if even else 15 - d] = run
 
     for_parity(odd, row_windows)
-    apart = lax.broadcasted_iota(jnp.int32, (cols, cols), 0) - lax.broadcasted_iota(
-        jnp.int32, (cols, cols), 1
-    )
-    band[...] = (jnp.abs(apart) <= 15).astype(jnp.float32).astype(jnp.bfloat16)
+    for h in range(2):
+        i = lax.broadcasted_iota(jnp.int32, band.shape[1:], 0) + h * LANES
+        j = lax.broadcasted_iota(jnp.int32, band.shape[1:], 1) + h * 2 * LANES
+        band[h] = (jnp.abs(i - j) <= 15).astype(jnp.float32).astype(jnp.bfloat16)
 
 
 def snr_kernel(
-    own, link, before, part, band, boxes, blanked, out, energy, sums, ready, sems
+    own, link, before, part, band, boxes, out, energy, sums, ready, sems
 ):
     chans, rows, cols = own.shape
     odd = odd_of("pix")
@@ -271,10 +277,7 @@
 
     stride = energy.shape[2] // chans
 
-    kept = (1 - blanked[...]).astype(jnp.float32)
-
     def finish(even):
-        both = jnp.concatenate([band[...], band[...]], axis=0)
         copies = []
         for w, width in enumerate(WIDTHS):
             for half in range(2):
@@ -289,9 +292,14 @@
                         value = part[w, tile, half, row]
                         at = pl.ds(half * 8 * stride + row, 8, stride=stride)
                         sums[w, tile, at, :] = value if run is None else value + run
-            total = jnp.dot(two_terms(sums, w), both, preferred_element_type=jnp.float32)
-            scale = lax.rsqrt(total * (1.0 / (VOLUME * width * width)) + 1e-5) * (1.0 / width)
-            ready[w] = boxes[w] * scale.reshape(chans, rows, cols) * kept[None]
+            firsts, seconds = two_terms(sums, w)
+            for h in range(2):
+                both = jnp.concatenate(firsts[h : h + 3] + seconds[h : h + 3], axis=1)
+                ones = jnp.concatenate([band[h], band[h]], axis=0)
+                total = jnp.dot(both, ones, preferred_element_type=jnp.float32)
+                scale = lax.rsqrt(total * (1.0 / (VOLUME * width * width)) + 1e-5)
+                lanes = slice(h * 2 * LANES, (h + 1) * 2 * LANES)
+                ready[w, :, :, lanes] = boxes[w, :, :, lanes] * scale.reshape(chans, rows, -1)
             copies.append(pltpu.make_async_copy(ready.at[w], out.at[w], sems.at[w]))
             copies[-1].start()
         for copy in copies:
@@ -362,15 +370,15 @@
         [
             f32(4, chans, rows, cols),
             f32(4, tiles, 2, rows, chans // 2, LANES),
-            jax.ShapeDtypeStruct((cols, cols), jnp.bfloat16),
+            jax.ShapeDtypeStruct((2, 3 * LANES, 2 * LANES), jnp.bfloat16),
         ],
         [
             pltpu.VMEM((4, chans // 2, rows, cols), jnp.float32),
             pltpu.VMEM((4, tiles, chans * 40, LANES), jnp.float32),
         ],
         micros=3.0,
-        in_specs=[VMEM, VMEM, VMEM, VMEM, ANY],
-    )(pair, pair_link, pair_energy, core_boxes, outer)
+        in_specs=[VMEM] * 5 + [ANY],
+    )(pair, pair_link, pair_energy, core_boxes, blanked, outer)
     far_energy = call(
         far_core_kernel,
         f32(4, tiles, chans * 24, LANES),
@@ -387,7 +395,7 @@
         ],
         micros=4.0,
         out_specs=ANY,
-    )(outer, outer_link, far_energy, part, band, boxes, blanked)
+    )(outer, outer_link, far_energy, part, band, boxes)
 
 
 def solution(mesh):

time: 50.9 us -> 50.4 us (level)
  no operation moved by 1% of the time
where the time goes in v9:
time: 50.4 us; the launch traced here: 50.1 us
  starting transfers between devices  21.1 us (42%)
  waiting for transfers between devices  18.3 us (36%)
  Pallas kernels  8.7 us (17%)
  local copies, waits for them, and re-layouts  1.8 us (4%)
    ppermute x9, starting transfers between devices, move(): lax.ppermute(value, axis, [(a, b) for a, b in pairs if 0 <= b < count])  21.1 us
    ppermute x9, waiting for transfers between devices, move(): lax.ppermute(value, axis, [(a, b) for a, b in pairs if 0 <= b < count])  18.3 us
    pallas_call x1, Pallas kernels, per_device(): call(snr_kernel, f32(4, chans, rows, cols), [pltpu.VMEM((4, tiles, chans...  2.79 us
    pallas_call x1, Pallas kernels, per_device(): call(pair_noise_kernel, [f32(4, chans, rows, cols), f32(4, tiles, 2, rows...  1.96 us
    unnamed x6, local copies, waits for them, and re-layouts  1.8 us
    pallas_call x1, Pallas kernels, per_device(): call(pair_rows_kernel, [f32(chans, 32, cols), f32(HALO, 32, cols), f32(HA...  1.03 us
  transfers between devices with their start and end apart: 9, of which 5 were waited for; matrix products, arithmetic and copies ran while one was open for 0% of the time, Pallas kernels for 10%

profile of v9, /device:TPU:34, one launch (start us, length us, event | category | flops | bytes accessed | tf_op | source)
XLA Modules:
  0.0 50.1 jit_solution(1204567465298169)
XLA Ops:
  0.0 0.0 copy-start
  0.0 1.0 %copy-done = f32[16,16,512]{2,1,0:T(8,128)S(1)} copy-done((f32[16,16,512]{2,1,0:T(8,128)S(1)}, f32[16,16,512]{2,1,0:T(8,128)}, u32[]{:S(2)}) %copy-start) | copy-done | bytes 524312
  1.0 0.0 copy-start.1
  1.0 0.8 %copy-done.1 = s32[16,512]{1,0:T(8,128)S(1)} copy-done((s32[16,512]{1,0:T(8,128)S(1)}, s32[16,512]{1,0:T(8,128)}, u32[]{:S(2)}) %copy-start.1) | copy-done | bytes 32792
  1.8 0.9 %shard_map.28 = (f32[16,16,512]{2,1,0:T(8,128)S(1)}, f32[3,16,512]{2,1,0:T(8,128)S(1)}, f32[3,16,512]{2,1,0:T(8,128)S(1)}) custom-call(f32[16,16,512]{2,1,0:T(8,128)S(1)} %copy-done, s32[16,512]{1,0:T(8,128)S(1)} %copy-done.1), custom_call_target="tpu_custom_call" | custom-call | flops 1000000000 | bytes 3000000 | tf_op jit(solution)/shard_map/pallas_call | solution.py:328
  2.7 3.1 %collective-permute-start = (f32[16,16,512]{2,1,0:T(8,128)S(1)}, f32[16,16,512]{2,1,0:T(8,128)S(1)}, u32[]{:S(2)}, u32[]{:S(2)}) collective-permute-start(f32[16,16,512]{2,1,0:T(8,128)S(1)} %get-tuple-element.19.cells), channel_id=1, source_target_pairs={{0,16},{16,0},{32,48},{48,32},{64,80},{80,64},{96,112},{112,96},{1... | collective-permute-start | bytes 1572872 | tf_op jit(solution)/shard_map/ppermute | solution.py:319
  5.8 3.4 %collective-permute-start.3 = (f32[3,16,512]{2,1,0:T(8,128)S(1)}, f32[3,16,512]{2,1,0:T(8,128)S(1)}, u32[]{:S(2)}, u32[]{:S(2)}) collective-permute-start(f32[3,16,512]{2,1,0:T(8,128)S(1)} %get-tuple-element.21), channel_id=1, source_target_pairs={{0,32},{32,64},{48,16},{64,96},{80,48},{112,80},{1,33},{33,65},{49... | collective-permute-start | bytes 294920 | tf_op jit(solution)/shard_map/ppermute | solution.py:319
  9.2 1.9 %collective-permute-start.2 = (f32[3,16,512]{2,1,0:T(8,128)S(1)}, f32[3,16,512]{2,1,0:T(8,128)S(1)}, u32[]{:S(2)}, u32[]{:S(2)}) collective-permute-start(f32[3,16,512]{2,1,0:T(8,128)S(1)} %get-tuple-element.20.edge), channel_id=1, source_target_pairs={{16,32},{32,16},{48,64},{64,48},{80,96},{96,80},{17,33},{33,17},{4... | collective-permute-start | bytes 294920 | tf_op jit(solution)/shard_map/ppermute | solution.py:319
  11.1 1.9 %collective-permute-start.1 = (f32[3,16,512]{2,1,0:T(8,128)S(1)}, f32[3,16,512]{2,1,0:T(8,128)S(1)}, u32[]{:S(2)}, u32[]{:S(2)}) collective-permute-start(f32[3,16,512]{2,1,0:T(8,128)S(1)} %get-tuple-element.20.edge), channel_id=1, source_target_pairs={{16,48},{32,0},{48,80},{64,32},{80,112},{96,64},{17,49},{33,1},{49... | collective-permute-start | bytes 294920 | tf_op jit(solution)/shard_map/ppermute | solution.py:319
  13.0 0.0 collective-permute-done.3.rest_2_.beyond
  13.0 5.1 %collective-permute-done.2.rest_1_.edge_far = f32[3,16,512]{2,1,0:T(8,128)S(1)} collective-permute-done((f32[3,16,512]{2,1,0:T(8,128)S(1)}, f32[3,16,512]{2,1,0:T(8,128)S(1)}, u32[]{:S(2)}, u32[]{:S(2)}) %collective-permute-start.2) | collective-permute-done | bytes 98336 | tf_op jit(solution)/shard_map/ppermute | solution.py:319
  18.2 0.0 collective-permute-done.1.rest_0_.edge_near
  18.2 1.9 %collective-permute-done.value = f32[16,16,512]{2,1,0:T(8,128)S(1)} collective-permute-done((f32[16,16,512]{2,1,0:T(8,128)S(1)}, f32[16,16,512]{2,1,0:T(8,128)S(1)}, u32[]{:S(2)}, u32[]{:S(2)}) %collective-permute-start) | collective-permute-done | bytes 524320 | tf_op jit(solution)/shard_map/ppermute | solution.py:319
  20.1 3.4 %collective-permute-start.4 = (f32[16,16,512]{2,1,0:T(8,128)S(1)}, f32[16,16,512]{2,1,0:T(8,128)S(1)}, u32[]{:S(2)}, u32[]{:S(2)}) collective-permute-start(f32[16,16,512]{2,1,0:T(8,128)S(1)} %shard_map.29.near), channel_id=1, source_target_pairs={{0,32},{32,64},{48,16},{64,96},{80,48},{112,80},{1,33},{33,65},{49... | collective-permute-start | bytes 1572872 | tf_op jit(solution)/shard_map/ppermute | solution.py:319
  23.5 1.0 %shard_map.31 = (f32[16,32,512]{2,1,0:T(8,128)S(1)}, f32[14,32,512]{2,1,0:T(8,128)S(1)}, f32[14,32,512]{2,1,0:T(8,128)S(1)}) custom-call(f32[16,16,512]{2,1,0:T(8,128)S(1)} %get-tuple-element.19.cells, f32[16,16,512]{2,1,0:T(8,128)S(1)} %shard_map.29.near, f32[3,16,512]{2,1,0:T(8,128)S(1)} %collective-permute-done.2.rest_1_.edge_far, ...), custom_call_target="tpu_custom_call" | custom-call | flops 10000000 | bytes 30000 | tf_op jit(solution)/shard_map/pallas_call | solution.py:344
  24.5 3.7 %collective-permute-start.7 = (f32[14,32,512]{2,1,0:T(8,128)S(1)}, f32[14,32,512]{2,1,0:T(8,128)S(1)}, u32[]{:S(2)}, u32[]{:S(2)}) collective-permute-start(f32[14,32,512]{2,1,0:T(8,128)S(1)} %get-tuple-element.26), channel_id=1, source_target_pairs={{1,2},{2,1},{3,4},{4,3},{5,6},{6,5},{7,8},{8,7},{9,10},{10,9},{11,... | collective-permute-start | bytes 2752520 | tf_op jit(solution)/shard_map/ppermute | solution.py:319
  28.2 0.1 collective-permute-start.8
  28.3 6.4 %collective-permute-done.4.far = f32[16,16,512]{2,1,0:T(8,128)S(1)} collective-permute-done((f32[16,16,512]{2,1,0:T(8,128)S(1)}, f32[16,16,512]{2,1,0:T(8,128)S(1)}, u32[]{:S(2)}, u32[]{:S(2)}) %collective-permute-start.4) | collective-permute-done | bytes 524320 | tf_op jit(solution)/shard_map/ppermute | solution.py:319
  34.7 0.6 %shard_map.30 = (f32[16,16,512]{2,1,0:T(8,128)S(1)}, f32[14,16,512]{2,1,0:T(8,128)S(1)}, f32[14,16,512]{2,1,0:T(8,128)S(1)}) custom-call(f32[16,16,512]{2,1,0:T(8,128)S(1)} %collective-permute-done.4.far, f32[3,16,512]{2,1,0:T(8,128)S(1)} %get-tuple-element.20.edge, f32[3,16,512]{2,1,0:T(8,128)S(1)} %collective-permute-done.3.rest_2_.beyond), custom_call_target="tpu_custom_call" | custom-call | flops 30000001024 | bytes 90000000 | tf_op jit(solution)/shard_map/pallas_call | solution.py:353
  35.4 3.4 %collective-permute-start.5 = (f32[14,16,512]{2,1,0:T(8,128)S(1)}, f32[14,16,512]{2,1,0:T(8,128)S(1)}, u32[]{:S(2)}, u32[]{:S(2)}) collective-permute-start(f32[14,16,512]{2,1,0:T(8,128)S(1)} %get-tuple-element.23), channel_id=1, source_target_pairs={{1,2},{2,1},{3,4},{4,3},{5,6},{6,5},{7,8},{8,7},{9,10},{10,9},{11,... | collective-permute-start | bytes 1376264 | tf_op jit(solution)/shard_map/ppermute | solution.py:319
  38.8 0.3 collective-permute-start.6
  39.1 0.0 collective-permute-done.8.core
  39.1 0.0 copy-start.2
  39.1 0.9 %shard_map.32 = (f32[4,4,640,128]{3,2,1,0:T(8,128)S(1)}, f32[4,8,16,512]{3,2,1,0:T(8,128)S(1)}) custom-call(f32[16,32,512]{2,1,0:T(8,128)S(1)} %get-tuple-element.25.own, f32[14,32,512]{2,1,0:T(8,128)S(1)} %collective-permute-done.8.core, f32[16,16,512]{2,1,0:T(8,128)S(1)} %get-tuple-element.22.after.own), custom_call_target="tpu_custom_call" | custom-call | flops 2000000000 | bytes 6000000 | tf_op jit(solution)/shard_map/pallas_call | solution.py:362
  40.0 1.3 %collective-permute-done.7.link = f32[14,32,512]{2,1,0:T(8,128)S(1)} collective-permute-done((f32[14,32,512]{2,1,0:T(8,128)S(1)}, f32[14,32,512]{2,1,0:T(8,128)S(1)}, u32[]{:S(2)}, u32[]{:S(2)}) %collective-permute-start.7) | collective-permute-done | bytes 917536 | tf_op jit(solution)/shard_map/ppermute | solution.py:319
  41.3 0.0 copy-done.2
  41.3 2.0 %shard_map.33 = (f32[4,16,16,512]{3,2,1,0:T(8,128)S(1)}, f32[4,4,2,16,8,128]{5,4,3,2,1,0:T(8,128)S(1)}, bf16[2,384,256]{2,1,0:T(8,128)(2,1)S(1)}) custom-call(f32[16,32,512]{2,1,0:T(8,128)S(1)} %get-tuple-element.25.own, f32[14,32,512]{2,1,0:T(8,128)S(1)} %collective-permute-done.7.link, f32[4,4,640,128]{3,2,1,0:T(8,128)S(1)} %get-tuple-element.28.before, ...), custom_call_target="tpu_custom_call" | custom-call | flops 3000000000 | bytes 9000000 | tf_op jit(solution)/shard_map/pallas_call | solution.py:368
  43.3 0.0 collective-permute-done.6.core
  43.3 0.5 shard_map.34.before
  43.8 3.5 %collective-permute-done.5.link = f32[14,16,512]{2,1,0:T(8,128)S(1)} collective-permute-done((f32[14,16,512]{2,1,0:T(8,128)S(1)}, f32[14,16,512]{2,1,0:T(8,128)S(1)}, u32[]{:S(2)}, u32[]{:S(2)}) %collective-permute-start.5) | collective-permute-done | bytes 458784 | tf_op jit(solution)/shard_map/ppermute | solution.py:319
  47.3 2.8 %shard_map.35 = f32[4,16,16,512]{3,2,1,0:T(8,128)} custom-call(f32[16,16,512]{2,1,0:T(8,128)S(1)} %get-tuple-element.22.after.own, f32[14,16,512]{2,1,0:T(8,128)S(1)} %collective-permute-done.5.link, f32[4,4,384,128]{3,2,1,0:T(8,128)S(1)} %shard_map.34.before, f32[4,4,2,16,8,128]{5,4,3,2,1,0:T(8,128)S(1)} %get-tuple-element.30.after.part, ...), custom_call_target="tpu_custom_call" | custom-call | flops 4000000000 | bytes 12000000 | tf_op jit(solution)/shard_map/pallas_call | solution.py:387
  (1 shorter events, 0.0 us)
Async XLA Ops:
  0.0 1.0 %copy-start = (f32[16,16,512]{2,1,0:T(8,128)S(1)}, f32[16,16,512]{2,1,0:T(8,128)}, u32[]{:S(2)}) copy-start(f32[16,16,512]{2,1,0:T(8,128)} %data.1) | copy-start | bytes 1572868
  1.0 0.8 %copy-start.1 = (s32[16,512]{1,0:T(8,128)S(1)}, s32[16,512]{1,0:T(8,128)}, u32[]{:S(2)}) copy-start(s32[16,512]{1,0:T(8,128)} %blanked.3) | copy-start | bytes 98308
  2.7 17.4 %collective-permute-start = (f32[16,16,512]{2,1,0:T(8,128)S(1)}, f32[16,16,512]{2,1,0:T(8,128)S(1)}, u32[]{:S(2)}, u32[]{:S(2)}) collective-permute-start(f32[16,16,512]{2,1,0:T(8,128)S(1)} %get-tuple-element.19.cells), channel_id=1, source_target_pairs={{0,16},{16,0},{32,48},{48,32},{64,80},{80,64},{96,112},{112,96},{1... | collective-permute-start | bytes 1572872 | tf_op jit(solution)/shard_map/ppermute | solution.py:319
  5.8 7.3 %collective-permute-start.3 = (f32[3,16,512]{2,1,0:T(8,128)S(1)}, f32[3,16,512]{2,1,0:T(8,128)S(1)}, u32[]{:S(2)}, u32[]{:S(2)}) collective-permute-start(f32[3,16,512]{2,1,0:T(8,128)S(1)} %get-tuple-element.21), channel_id=1, source_target_pairs={{0,32},{32,64},{48,16},{64,96},{80,48},{112,80},{1,33},{33,65},{49... | collective-permute-start | bytes 294920 | tf_op jit(solution)/shard_map/ppermute | solution.py:319
  9.2 9.0 %collective-permute-start.2 = (f32[3,16,512]{2,1,0:T(8,128)S(1)}, f32[3,16,512]{2,1,0:T(8,128)S(1)}, u32[]{:S(2)}, u32[]{:S(2)}) collective-permute-start(f32[3,16,512]{2,1,0:T(8,128)S(1)} %get-tuple-element.20.edge), channel_id=1, source_target_pairs={{16,32},{32,16},{48,64},{64,48},{80,96},{96,80},{17,33},{33,17},{4... | collective-permute-start | bytes 294920 | tf_op jit(solution)/shard_map/ppermute | solution.py:319
  11.1 7.1 %collective-permute-start.1 = (f32[3,16,512]{2,1,0:T(8,128)S(1)}, f32[3,16,512]{2,1,0:T(8,128)S(1)}, u32[]{:S(2)}, u32[]{:S(2)}) collective-permute-start(f32[3,16,512]{2,1,0:T(8,128)S(1)} %get-tuple-element.20.edge), channel_id=1, source_target_pairs={{16,48},{32,0},{48,80},{64,32},{80,112},{96,64},{17,49},{33,1},{49... | collective-permute-start | bytes 294920 | tf_op jit(solution)/shard_map/ppermute | solution.py:319
  20.1 14.7 %collective-permute-start.4 = (f32[16,16,512]{2,1,0:T(8,128)S(1)}, f32[16,16,512]{2,1,0:T(8,128)S(1)}, u32[]{:S(2)}, u32[]{:S(2)}) collective-permute-start(f32[16,16,512]{2,1,0:T(8,128)S(1)} %shard_map.29.near), channel_id=1, source_target_pairs={{0,32},{32,64},{48,16},{64,96},{80,48},{112,80},{1,33},{33,65},{49... | collective-permute-start | bytes 1572872 | tf_op jit(solution)/shard_map/ppermute | solution.py:319
  24.5 16.8 %collective-permute-start.7 = (f32[14,32,512]{2,1,0:T(8,128)S(1)}, f32[14,32,512]{2,1,0:T(8,128)S(1)}, u32[]{:S(2)}, u32[]{:S(2)}) collective-permute-start(f32[14,32,512]{2,1,0:T(8,128)S(1)} %get-tuple-element.26), channel_id=1, source_target_pairs={{1,2},{2,1},{3,4},{4,3},{5,6},{6,5},{7,8},{8,7},{9,10},{10,9},{11,... | collective-permute-start | bytes 2752520 | tf_op jit(solution)/shard_map/ppermute | solution.py:319
  28.2 10.9 %collective-permute-start.8 = (f32[14,32,512]{2,1,0:T(8,128)S(1)}, f32[14,32,512]{2,1,0:T(8,128)S(1)}, u32[]{:S(2)}, u32[]{:S(2)}) collective-permute-start(f32[14,32,512]{2,1,0:T(8,128)S(1)} %get-tuple-element.27), channel_id=1, source_target_pairs={{0,1},{1,0},{2,3},{3,2},{4,5},{5,4},{6,7},{7,6},{8,9},{9,8},{10,11... | collective-permute-start | bytes 2752520 | tf_op jit(solution)/shard_map/ppermute | solution.py:319
  35.4 11.9 %collective-permute-start.5 = (f32[14,16,512]{2,1,0:T(8,128)S(1)}, f32[14,16,512]{2,1,0:T(8,128)S(1)}, u32[]{:S(2)}, u32[]{:S(2)}) collective-permute-start(f32[14,16,512]{2,1,0:T(8,128)S(1)} %get-tuple-element.23), channel_id=1, source_target_pairs={{1,2},{2,1},{3,4},{4,3},{5,6},{6,5},{7,8},{8,7},{9,10},{10,9},{11,... | collective-permute-start | bytes 1376264 | tf_op jit(solution)/shard_map/ppermute | solution.py:319
  38.8 4.5 %collective-permute-start.6 = (f32[14,16,512]{2,1,0:T(8,128)S(1)}, f32[14,16,512]{2,1,0:T(8,128)S(1)}, u32[]{:S(2)}, u32[]{:S(2)}) collective-permute-start(f32[14,16,512]{2,1,0:T(8,128)S(1)} %get-tuple-element.24), channel_id=1, source_target_pairs={{0,1},{1,0},{2,3},{3,2},{4,5},{5,4},{6,7},{7,6},{8,9},{9,8},{10,11... | collective-permute-start | bytes 1376264 | tf_op jit(solution)/shard_map/ppermute | solution.py:319
  39.1 2.3 %copy-start.2 = (s32[16,512]{1,0:T(8,128)S(1)}, s32[16,512]{1,0:T(8,128)}, u32[]{:S(2)}) copy-start(s32[16,512]{1,0:T(8,128)} %blanked.3) | copy-start | bytes 98308

commit v10 on v9

--- a/solution.py
+++ b/solution.py
@@ -109,7 +109,7 @@
         store_channel(c, smooth_rows(field, c, 8, 2 * rows), full, link, core)
 
 
-def far_rows_kernel(far, edge, beyond, full, link, core, field):
+def far_rows_kernel(far, edge, beyond, full1, link1, core1, full2, link2, core2, field):
     chans, rows, cols = far.shape
     at, count = lax.axis_index("pix"), lax.axis_size("pix")
     even = odd_of("pix") == 0
@@ -120,7 +120,9 @@
         field[:, 24 + r, :] = jnp.where(even, edge[r], beyond[r])
 
     for c in range(chans):
-        store_channel(c, smooth_rows(field, c, 8, rows) * present, full, link, core)
+        value = smooth_rows(field, c, 8, rows) * present
+        store_channel(c, value[:, : cols // 2], full1, link1, core1)
+        store_channel(c, value[:, cols // 2 :], full2, link2, core2)
 
 
 def channel_pass(own, halo, down, row, tile, energy, before, boxes, kept_at):
@@ -268,31 +270,41 @@
         band[h] = (jnp.abs(i - j) <= 15).astype(jnp.float32).astype(jnp.bfloat16)
 
 
+def far_windows(w, even, first, part, sums, energy):
+    stride = energy.shape[2] // 16
+    for half in range(2):
+        for tile in range(sums.shape[1]):
+            run = None
+            for d in range(16):
+                if d > 0:
+                    i = 16 - d if even else d - 1
+                    e = energy[w, tile, pl.ds(half * 8 * stride + i, 8, stride=stride), :]
+                    run = e if run is None else run + e
+                row = 15 - d if even else d
+                value = part[w, first + tile, half, row]
+                at = pl.ds(half * 8 * stride + row, 8, stride=stride)
+                sums[w, tile, at, :] = value if run is None else value + run
+
+
+def far_first_kernel(own, link, before, part, sums, energy):
+    strips(own, link, False, energy, before, None)
+    for_parity(odd_of("pix"), lambda w, even: far_windows(w, even, 0, part, sums, energy))
+
+
 def snr_kernel(
-    own, link, before, part, band, boxes, out, energy, sums, ready, sems
+    own, link, before, part, first, band, boxes, out, energy, sums, ready, sems
 ):
-    chans, rows, cols = own.shape
+    chans, rows = boxes.shape[1:3]
     odd = odd_of("pix")
     strips(own, link, False, energy, before, None)
-
-    stride = energy.shape[2] // chans
 
     def finish(even):
         copies = []
         for w, width in enumerate(WIDTHS):
-            for half in range(2):
-                for tile in range(cols // LANES):
-                    run = None
-                    for d in range(rows):
-                        if d > 0:
-                            i = 16 - d if even else d - 1
-                            e = energy[w, tile, pl.ds(half * 8 * stride + i, 8, stride=stride), :]
-                            run = e if run is None else run + e
-                        row = 15 - d if even else d
-                        value = part[w, tile, half, row]
-                        at = pl.ds(half * 8 * stride + row, 8, stride=stride)
-                        sums[w, tile, at, :] = value if run is None else value + run
-            firsts, seconds = two_terms(sums, w)
+            far_windows(w, even, 2, part, sums, energy)
+            firsts, seconds = two_terms(first, w)
+            more = two_terms(sums, w)
+            firsts, seconds = firsts + more[0], seconds + more[1]
             for h in range(2):
                 both = jnp.concatenate(firsts[h : h + 3] + seconds[h : h + 3], axis=1)
                 ones = jnp.concatenate([band[h], band[h]], axis=0)
@@ -350,14 +362,15 @@
     pair_link = swap(pair_link, "chan", 1)
     pair_core = swap(pair_core, "chan", 0)
 
-    outer, outer_link, outer_core = call(
+    half = cols // 2
+    outer, link1, core1, outer2, link2, core2 = call(
         far_rows_kernel,
-        [f32(chans, 16, cols), f32(HALO, 16, cols), f32(HALO, 16, cols)],
+        [f32(chans, 16, half), f32(HALO, 16, half), f32(HALO, 16, half)] * 2,
         [pltpu.VMEM((chans, 32, cols), jnp.float32)],
         micros=30.0,
     )(far, edge, beyond)
-    outer_link = swap(outer_link, "chan", 1)
-    outer_core = swap(outer_core, "chan", 0)
+    link1, core1 = swap(link1, "chan", 1), swap(core1, "chan", 0)
+    link2, core2 = swap(link2, "chan", 1), swap(core2, "chan", 0)
 
     pair_energy, core_boxes = call(
         pair_core_kernel,
@@ -379,23 +392,24 @@
         micros=3.0,
         in_specs=[VMEM] * 5 + [ANY],
     )(pair, pair_link, pair_energy, core_boxes, blanked, outer)
-    far_energy = call(
-        far_core_kernel,
-        f32(4, tiles, chans * 24, LANES),
-        in_specs=[VMEM, VMEM, ANY],
-    )(outer, outer_core, part)
+    sums = f32(4, tiles // 2, chans * 24, LANES)
+    scratch = pltpu.VMEM(sums.shape, jnp.float32)
+    ordered = dict(in_specs=[VMEM, VMEM, ANY])
+    energy1 = call(far_core_kernel, sums, **ordered)(outer, core1, part)
+    energy2 = call(far_core_kernel, sums, **ordered)(outer2, core2, part)
+    first = call(far_first_kernel, sums, [scratch])(outer, link1, energy1, part)
     return call(
         snr_kernel,
         f32(4, chans, rows, cols),
         [
-            pltpu.VMEM((4, tiles, chans * 24, LANES), jnp.float32),
-            pltpu.VMEM((4, tiles, chans * 24, LANES), jnp.float32),
+            scratch,
+            scratch,
             pltpu.VMEM((4, chans, rows, cols), jnp.float32),
             pltpu.SemaphoreType.DMA((4,)),
         ],
         micros=4.0,
         out_specs=ANY,
-    )(outer, outer_link, far_energy, part, band, boxes)
+    )(outer2, link2, energy2, part, first, band, boxes)
 
 
 def solution(mesh):

time: 50.4 us -> 52.2 us (1.036)
  starting transfers between devices: 21.1 us -> 25.3 us
  waiting for transfers between devices: 18.3 us -> 15.5 us
    ppermute x9 -> x11, starting transfers between devices: 21.1 us -> 25.3 us  [move(): lax.ppermute(value, axis, [(a, b) for a, b in pairs if 0 <= b < count])]
    ppermute x9 -> x11, waiting for transfers between devices: 18.3 us -> 15.5 us  [move(): lax.ppermute(value, axis, [(a, b) for a, b in pairs if 0 <= b < count])]
    pallas_call x3 -> x5, Pallas kernels: 3.9 us -> 3.95 us  [the longest x1 2.24 us: per_device(): call(snr_kernel, f32(4, chans, rows, cols), [scratch, scratch, pltpu.VMEM...]
    unnamed x6 -> x4, local copies, waits for them, and re-layouts: 1.8 us -> 1.8 us
  transfers between devices with their start and end apart: 9 -> 11, of which waited for: 5 -> 4; matrix products, arithmetic and copies ran while one was open for 0% -> 0% of each run, Pallas kernels for 10% -> 11%
where the time goes in v10:
time: 52.2 us; the launch traced here: 51.6 us
  starting transfers between devices  25.3 us (48%)
  waiting for transfers between devices  15.5 us (30%)
  Pallas kernels  8.81 us (17%)
  local copies, waits for them, and re-layouts  1.8 us (3%)
    ppermute x11, starting transfers between devices, move(): lax.ppermute(value, axis, [(a, b) for a, b in pairs if 0 <= b < count])  25.3 us
    ppermute x11, waiting for transfers between devices, move(): lax.ppermute(value, axis, [(a, b) for a, b in pairs if 0 <= b < count])  15.5 us
    pallas_call x1, Pallas kernels, per_device(): call(snr_kernel, f32(4, chans, rows, cols), [scratch, scratch, pltpu.VMEM...  2.24 us
    pallas_call x1, Pallas kernels, per_device(): call(pair_noise_kernel, [f32(4, chans, rows, cols), f32(4, tiles, 2, rows...  1.99 us
    unnamed x4, local copies, waits for them, and re-layouts  1.8 us
  transfers between devices with their start and end apart: 11, of which 4 were waited for; matrix products, arithmetic and copies ran while one was open for 0% of the time, Pallas kernels for 11%

profile of v10, /device:TPU:34, one launch (start us, length us, event | category | flops | bytes accessed | tf_op | source)
XLA Modules:
  0.0 51.6 jit_solution(7013231786872784073)
XLA Ops:
  0.0 0.0 copy-start
  0.0 1.0 %copy-done = f32[16,16,512]{2,1,0:T(8,128)S(1)} copy-done((f32[16,16,512]{2,1,0:T(8,128)S(1)}, f32[16,16,512]{2,1,0:T(8,128)}, u32[]{:S(2)}) %copy-start) | copy-done | bytes 524312
  1.0 0.0 copy-start.1
  1.0 0.8 %copy-done.1 = s32[16,512]{1,0:T(8,128)S(1)} copy-done((s32[16,512]{1,0:T(8,128)S(1)}, s32[16,512]{1,0:T(8,128)}, u32[]{:S(2)}) %copy-start.1) | copy-done | bytes 32792
  1.8 0.9 %shard_map.28 = (f32[16,16,512]{2,1,0:T(8,128)S(1)}, f32[3,16,512]{2,1,0:T(8,128)S(1)}, f32[3,16,512]{2,1,0:T(8,128)S(1)}) custom-call(f32[16,16,512]{2,1,0:T(8,128)S(1)} %copy-done, s32[16,512]{1,0:T(8,128)S(1)} %copy-done.1), custom_call_target="tpu_custom_call" | custom-call | flops 1000000000 | bytes 3000000 | tf_op jit(solution)/shard_map/pallas_call | solution.py:340
  2.7 3.1 %collective-permute-start = (f32[16,16,512]{2,1,0:T(8,128)S(1)}, f32[16,16,512]{2,1,0:T(8,128)S(1)}, u32[]{:S(2)}, u32[]{:S(2)}) collective-permute-start(f32[16,16,512]{2,1,0:T(8,128)S(1)} %get-tuple-element.22.cells), channel_id=1, source_target_pairs={{0,16},{16,0},{32,48},{48,32},{64,80},{80,64},{96,112},{112,96},{1... | collective-permute-start | bytes 1572872 | tf_op jit(solution)/shard_map/ppermute | solution.py:331
  5.8 3.4 %collective-permute-start.3 = (f32[3,16,512]{2,1,0:T(8,128)S(1)}, f32[3,16,512]{2,1,0:T(8,128)S(1)}, u32[]{:S(2)}, u32[]{:S(2)}) collective-permute-start(f32[3,16,512]{2,1,0:T(8,128)S(1)} %get-tuple-element.24), channel_id=1, source_target_pairs={{0,32},{32,64},{48,16},{64,96},{80,48},{112,80},{1,33},{33,65},{49... | collective-permute-start | bytes 294920 | tf_op jit(solution)/shard_map/ppermute | solution.py:331
  9.2 1.9 %collective-permute-start.2 = (f32[3,16,512]{2,1,0:T(8,128)S(1)}, f32[3,16,512]{2,1,0:T(8,128)S(1)}, u32[]{:S(2)}, u32[]{:S(2)}) collective-permute-start(f32[3,16,512]{2,1,0:T(8,128)S(1)} %get-tuple-element.23.edge), channel_id=1, source_target_pairs={{16,32},{32,16},{48,64},{64,48},{80,96},{96,80},{17,33},{33,17},{4... | collective-permute-start | bytes 294920 | tf_op jit(solution)/shard_map/ppermute | solution.py:331
  11.1 1.9 %collective-permute-start.1 = (f32[3,16,512]{2,1,0:T(8,128)S(1)}, f32[3,16,512]{2,1,0:T(8,128)S(1)}, u32[]{:S(2)}, u32[]{:S(2)}) collective-permute-start(f32[3,16,512]{2,1,0:T(8,128)S(1)} %get-tuple-element.23.edge), channel_id=1, source_target_pairs={{16,48},{32,0},{48,80},{64,32},{80,112},{96,64},{17,49},{33,1},{49... | collective-permute-start | bytes 294920 | tf_op jit(solution)/shard_map/ppermute | solution.py:331
  13.0 0.0 collective-permute-done.3.rest_2_.beyond
  13.0 5.1 %collective-permute-done.2.rest_1_.edge_far = f32[3,16,512]{2,1,0:T(8,128)S(1)} collective-permute-done((f32[3,16,512]{2,1,0:T(8,128)S(1)}, f32[3,16,512]{2,1,0:T(8,128)S(1)}, u32[]{:S(2)}, u32[]{:S(2)}) %collective-permute-start.2) | collective-permute-done | bytes 98336 | tf_op jit(solution)/shard_map/ppermute | solution.py:331
  18.2 0.0 collective-permute-done.1.rest_0_.edge_near
  18.2 1.9 %collective-permute-done.value = f32[16,16,512]{2,1,0:T(8,128)S(1)} collective-permute-done((f32[16,16,512]{2,1,0:T(8,128)S(1)}, f32[16,16,512]{2,1,0:T(8,128)S(1)}, u32[]{:S(2)}, u32[]{:S(2)}) %collective-permute-start) | collective-permute-done | bytes 524320 | tf_op jit(solution)/shard_map/ppermute | solution.py:331
  20.1 3.4 %collective-permute-start.4 = (f32[16,16,512]{2,1,0:T(8,128)S(1)}, f32[16,16,512]{2,1,0:T(8,128)S(1)}, u32[]{:S(2)}, u32[]{:S(2)}) collective-permute-start(f32[16,16,512]{2,1,0:T(8,128)S(1)} %shard_map.29.near), channel_id=1, source_target_pairs={{0,32},{32,64},{48,16},{64,96},{80,48},{112,80},{1,33},{33,65},{49... | collective-permute-start | bytes 1572872 | tf_op jit(solution)/shard_map/ppermute | solution.py:331
  23.5 1.0 %shard_map.31 = (f32[16,32,512]{2,1,0:T(8,128)S(1)}, f32[14,32,512]{2,1,0:T(8,128)S(1)}, f32[14,32,512]{2,1,0:T(8,128)S(1)}) custom-call(f32[16,16,512]{2,1,0:T(8,128)S(1)} %get-tuple-element.22.cells, f32[16,16,512]{2,1,0:T(8,128)S(1)} %shard_map.29.near, f32[3,16,512]{2,1,0:T(8,128)S(1)} %collective-permute-done.2.rest_1_.edge_far, ...), custom_call_target="tpu_custom_call" | custom-call | flops 10000000 | bytes 30000 | tf_op jit(solution)/shard_map/pallas_call | solution.py:356
  24.5 3.7 %collective-permute-start.7 = (f32[14,32,512]{2,1,0:T(8,128)S(1)}, f32[14,32,512]{2,1,0:T(8,128)S(1)}, u32[]{:S(2)}, u32[]{:S(2)}) collective-permute-start(f32[14,32,512]{2,1,0:T(8,128)S(1)} %get-tuple-element.29), channel_id=1, source_target_pairs={{1,2},{2,1},{3,4},{4,3},{5,6},{6,5},{7,8},{8,7},{9,10},{10,9},{11,... | collective-permute-start | bytes 2752520 | tf_op jit(solution)/shard_map/ppermute | solution.py:331
  28.2 0.1 collective-permute-start.8
  28.3 6.4 %collective-permute-done.4.far = f32[16,16,512]{2,1,0:T(8,128)S(1)} collective-permute-done((f32[16,16,512]{2,1,0:T(8,128)S(1)}, f32[16,16,512]{2,1,0:T(8,128)S(1)}, u32[]{:S(2)}, u32[]{:S(2)}) %collective-permute-start.4) | collective-permute-done | bytes 524320 | tf_op jit(solution)/shard_map/ppermute | solution.py:331
  34.7 0.6 %shard_map.30 = (f32[16,16,256]{2,1,0:T(8,128)S(1)}, f32[14,16,256]{2,1,0:T(8,128)S(1)}, f32[14,16,256]{2,1,0:T(8,128)S(1)}, f32[16,16,256]{2,1,0:T(8,128)S(1)},...) custom-call(f32[16,16,512]{2,1,0:T(8,128)S(1)} %collective-permute-done.4.far, ...), custom_call_target="tpu_custom_call" | custom-call | flops 30000001024 | bytes 90000000 | tf_op jit(solution)/shard_map/pallas_call | solution.py:366
  35.4 3.4 %collective-permute-start.5 = (f32[14,16,256]{2,1,0:T(8,128)S(1)}, f32[14,16,256]{2,1,0:T(8,128)S(1)}, u32[]{:S(2)}, u32[]{:S(2)}) collective-permute-start(f32[14,16,256]{2,1,0:T(8,128)S(1)} %get-tuple-element.26), channel_id=1, source_target_pairs={{1,2},{2,1},{3,4},{4,3},{5,6},{6,5},{7,8},{8,7},{9,10},{10,9},{11,... | collective-permute-start | bytes 688136 | tf_op jit(solution)/shard_map/ppermute | solution.py:331
  38.8 0.3 collective-permute-start.6
  39.1 4.1 %collective-permute-start.9 = (f32[14,16,256]{2,1,0:T(8,128)S(1)}, f32[14,16,256]{2,1,0:T(8,128)S(1)}, u32[]{:S(2)}, u32[]{:S(2)}) collective-permute-start(f32[14,16,256]{2,1,0:T(8,128)S(1)} %get-tuple-element.35), channel_id=1, source_target_pairs={{1,2},{2,1},{3,4},{4,3},{5,6},{6,5},{7,8},{8,7},{9,10},{10,9},{11,... | collective-permute-start | bytes 688136 | tf_op jit(solution)/shard_map/ppermute | solution.py:331
  43.2 0.0 collective-permute-done.8.core
  43.2 0.1 collective-permute-start.10
  43.3 0.9 %shard_map.32 = (f32[4,4,640,128]{3,2,1,0:T(8,128)S(1)}, f32[4,8,16,512]{3,2,1,0:T(8,128)S(1)}) custom-call(f32[16,32,512]{2,1,0:T(8,128)S(1)} %get-tuple-element.28.own, f32[14,32,512]{2,1,0:T(8,128)S(1)} %collective-permute-done.8.core, f32[16,16,256]{2,1,0:T(8,128)S(1)} %get-tuple-element.31.after.own), custom_call_target="tpu_custom_call" | custom-call | flops 2000000000 | bytes 6000000 | tf_op jit(solution)/shard_map/pallas_call | solution.py:375
  44.2 0.0 collective-permute-done.7.link
  44.2 2.0 %shard_map.33 = (f32[4,16,16,512]{3,2,1,0:T(8,128)S(1)}, f32[4,4,2,16,8,128]{5,4,3,2,1,0:T(8,128)S(1)}, bf16[2,384,256]{2,1,0:T(8,128)(2,1)S(1)}) custom-call(f32[16,32,512]{2,1,0:T(8,128)S(1)} %get-tuple-element.28.own, f32[14,32,512]{2,1,0:T(8,128)S(1)} %collective-permute-done.7.link, f32[4,4,640,128]{3,2,1,0:T(8,128)S(1)} %get-tuple-element.32.before, ...), custom_call_target="tpu_custom_call" | custom-call | flops 3000000000 | bytes 9000000 | tf_op jit(solution)/shard_map/pallas_call | solution.py:381
  46.2 0.0 collective-permute-done.10.core
  46.2 0.3 shard_map.35.before
  46.5 2.0 %collective-permute-done.9.link = f32[14,16,256]{2,1,0:T(8,128)S(1)} collective-permute-done((f32[14,16,256]{2,1,0:T(8,128)S(1)}, f32[14,16,256]{2,1,0:T(8,128)S(1)}, u32[]{:S(2)}, u32[]{:S(2)}) %collective-permute-start.9) | collective-permute-done | bytes 229408 | tf_op jit(solution)/shard_map/ppermute | solution.py:331
  48.5 0.6 %shard_map.36.first = f32[4,2,384,128]{3,2,1,0:T(8,128)S(1)} custom-call(f32[16,16,256]{2,1,0:T(8,128)S(1)} %get-tuple-element.31.after.own, f32[14,16,256]{2,1,0:T(8,128)S(1)} %collective-permute-done.9.link, f32[4,2,384,128]{3,2,1,0:T(8,128)S(1)} %shard_map.35.before, f32[4,4,2,16,8,128]{5,4,3,2,1,0:T(8,128)S(1)} %get-tuple-element.34.after.part), custom_call_target="tpu_custom_call" | custom-call | flops 1000000000 | bytes 3000000 | tf_op jit(solution)/shard_map/pallas_call | solution.py:400
  49.1 0.0 collective-permute-done.6.core
  49.1 0.3 shard_map.34.before
  49.4 0.0 collective-permute-done.5.link
  49.4 2.2 %shard_map.37 = f32[4,16,16,512]{3,2,1,0:T(8,128)} custom-call(f32[16,16,256]{2,1,0:T(8,128)S(1)} %get-tuple-element.25.own, f32[14,16,256]{2,1,0:T(8,128)S(1)} %collective-permute-done.5.link, f32[4,2,384,128]{3,2,1,0:T(8,128)S(1)} %shard_map.34.before, f32[4,4,2,16,8,128]{5,4,3,2,1,0:T(8,128)S(1)} %get-tuple-element.34.after.part, ...), custom_call_target="tpu_custom_call" | custom-call | flops 4000000000 | bytes 12000000 | tf_op jit(solution)/shard_map/pallas_call | solution.py:401
  (1 shorter events, 0.0 us)
Async XLA Ops:
  0.0 1.0 %copy-start = (f32[16,16,512]{2,1,0:T(8,128)S(1)}, f32[16,16,512]{2,1,0:T(8,128)}, u32[]{:S(2)}) copy-start(f32[16,16,512]{2,1,0:T(8,128)} %data.1) | copy-start | bytes 1572868
  1.0 0.8 %copy-start.1 = (s32[16,512]{1,0:T(8,128)S(1)}, s32[16,512]{1,0:T(8,128)}, u32[]{:S(2)}) copy-start(s32[16,512]{1,0:T(8,128)} %blanked.3) | copy-start | bytes 98308
  2.7 17.4 %collective-permute-start = (f32[16,16,512]{2,1,0:T(8,128)S(1)}, f32[16,16,512]{2,1,0:T(8,128)S(1)}, u32[]{:S(2)}, u32[]{:S(2)}) collective-permute-start(f32[16,16,512]{2,1,0:T(8,128)S(1)} %get-tuple-element.22.cells), channel_id=1, source_target_pairs={{0,16},{16,0},{32,48},{48,32},{64,80},{80,64},{96,112},{112,96},{1... | collective-permute-start | bytes 1572872 | tf_op jit(solution)/shard_map/ppermute | solution.py:331
  5.8 7.3 %collective-permute-start.3 = (f32[3,16,512]{2,1,0:T(8,128)S(1)}, f32[3,16,512]{2,1,0:T(8,128)S(1)}, u32[]{:S(2)}, u32[]{:S(2)}) collective-permute-start(f32[3,16,512]{2,1,0:T(8,128)S(1)} %get-tuple-element.24), channel_id=1, source_target_pairs={{0,32},{32,64},{48,16},{64,96},{80,48},{112,80},{1,33},{33,65},{49... | collective-permute-start | bytes 294920 | tf_op jit(solution)/shard_map/ppermute | solution.py:331
  9.2 9.0 %collective-permute-start.2 = (f32[3,16,512]{2,1,0:T(8,128)S(1)}, f32[3,16,512]{2,1,0:T(8,128)S(1)}, u32[]{:S(2)}, u32[]{:S(2)}) collective-permute-start(f32[3,16,512]{2,1,0:T(8,128)S(1)} %get-tuple-element.23.edge), channel_id=1, source_target_pairs={{16,32},{32,16},{48,64},{64,48},{80,96},{96,80},{17,33},{33,17},{4... | collective-permute-start | bytes 294920 | tf_op jit(solution)/shard_map/ppermute | solution.py:331
  11.1 7.1 %collective-permute-start.1 = (f32[3,16,512]{2,1,0:T(8,128)S(1)}, f32[3,16,512]{2,1,0:T(8,128)S(1)}, u32[]{:S(2)}, u32[]{:S(2)}) collective-permute-start(f32[3,16,512]{2,1,0:T(8,128)S(1)} %get-tuple-element.23.edge), channel_id=1, source_target_pairs={{16,48},{32,0},{48,80},{64,32},{80,112},{96,64},{17,49},{33,1},{49... | collective-permute-start | bytes 294920 | tf_op jit(solution)/shard_map/ppermute | solution.py:331
  20.1 14.7 %collective-permute-start.4 = (f32[16,16,512]{2,1,0:T(8,128)S(1)}, f32[16,16,512]{2,1,0:T(8,128)S(1)}, u32[]{:S(2)}, u32[]{:S(2)}) collective-permute-start(f32[16,16,512]{2,1,0:T(8,128)S(1)} %shard_map.29.near), channel_id=1, source_target_pairs={{0,32},{32,64},{48,16},{64,96},{80,48},{112,80},{1,33},{33,65},{49... | collective-permute-start | bytes 1572872 | tf_op jit(solution)/shard_map/ppermute | solution.py:331
  24.5 19.7 %collective-permute-start.7 = (f32[14,32,512]{2,1,0:T(8,128)S(1)}, f32[14,32,512]{2,1,0:T(8,128)S(1)}, u32[]{:S(2)}, u32[]{:S(2)}) collective-permute-start(f32[14,32,512]{2,1,0:T(8,128)S(1)} %get-tuple-element.29), channel_id=1, source_target_pairs={{1,2},{2,1},{3,4},{4,3},{5,6},{6,5},{7,8},{8,7},{9,10},{10,9},{11,... | collective-permute-start | bytes 2752520 | tf_op jit(solution)/shard_map/ppermute | solution.py:331
  28.2 15.0 %collective-permute-start.8 = (f32[14,32,512]{2,1,0:T(8,128)S(1)}, f32[14,32,512]{2,1,0:T(8,128)S(1)}, u32[]{:S(2)}, u32[]{:S(2)}) collective-permute-start(f32[14,32,512]{2,1,0:T(8,128)S(1)} %get-tuple-element.30), channel_id=1, source_target_pairs={{0,1},{1,0},{2,3},{3,2},{4,5},{5,4},{6,7},{7,6},{8,9},{9,8},{10,11... | collective-permute-start | bytes 2752520 | tf_op jit(solution)/shard_map/ppermute | solution.py:331
  35.4 14.0 %collective-permute-start.5 = (f32[14,16,256]{2,1,0:T(8,128)S(1)}, f32[14,16,256]{2,1,0:T(8,128)S(1)}, u32[]{:S(2)}, u32[]{:S(2)}) collective-permute-start(f32[14,16,256]{2,1,0:T(8,128)S(1)} %get-tuple-element.26), channel_id=1, source_target_pairs={{1,2},{2,1},{3,4},{4,3},{5,6},{6,5},{7,8},{8,7},{9,10},{10,9},{11,... | collective-permute-start | bytes 688136 | tf_op jit(solution)/shard_map/ppermute | solution.py:331
  38.8 10.3 %collective-permute-start.6 = (f32[14,16,256]{2,1,0:T(8,128)S(1)}, f32[14,16,256]{2,1,0:T(8,128)S(1)}, u32[]{:S(2)}, u32[]{:S(2)}) collective-permute-start(f32[14,16,256]{2,1,0:T(8,128)S(1)} %get-tuple-element.27), channel_id=1, source_target_pairs={{0,1},{1,0},{2,3},{3,2},{4,5},{5,4},{6,7},{7,6},{8,9},{9,8},{10,11... | collective-permute-start | bytes 688136 | tf_op jit(solution)/shard_map/ppermute | solution.py:331
  39.1 9.4 %collective-permute-start.9 = (f32[14,16,256]{2,1,0:T(8,128)S(1)}, f32[14,16,256]{2,1,0:T(8,128)S(1)}, u32[]{:S(2)}, u32[]{:S(2)}) collective-permute-start(f32[14,16,256]{2,1,0:T(8,128)S(1)} %get-tuple-element.35), channel_id=1, source_target_pairs={{1,2},{2,1},{3,4},{4,3},{5,6},{6,5},{7,8},{8,7},{9,10},{10,9},{11,... | collective-permute-start | bytes 688136 | tf_op jit(solution)/shard_map/ppermute | solution.py:331
  43.2 3.0 %collective-permute-start.10 = (f32[14,16,256]{2,1,0:T(8,128)S(1)}, f32[14,16,256]{2,1,0:T(8,128)S(1)}, u32[]{:S(2)}, u32[]{:S(2)}) collective-permute-start(f32[14,16,256]{2,1,0:T(8,128)S(1)} %get-tuple-element.36), channel_id=1, source_target_pairs={{0,1},{1,0},{2,3},{3,2},{4,5},{5,4},{6,7},{7,6},{8,9},{9,8},{10,11... | collective-permute-start | bytes 688136 | tf_op jit(solution)/shard_map/ppermute | solution.py:331

commit v11 on v10

--- a/solution.py
+++ b/solution.py
@@ -43,7 +43,7 @@
     return lax.axis_index(axis) % 2
 
 
-def clean_cols_kernel(data, blanked, cells, edge, edge2):
+def clean_cols_kernel(data, blanked, cells, second, edge, edge2):
     taps = kernel_taps()
     chans, rows, cols = data.shape
     even = odd_of("pix") == 0
@@ -57,6 +57,7 @@
             right = jnp.where(lane < cols - t, pltpu.roll(x, cols - t, 1), 0.0)
             acc = acc + taps[3 + t] * (left + right)
         cells[c] = acc
+        second[c] = acc[:, cols - second.shape[2] :]
     for r in range(3):
         top = cells[:, r, :]
         bottom = cells[:, rows - 3 + r, :]
@@ -109,20 +110,23 @@
         store_channel(c, smooth_rows(field, c, 8, 2 * rows), full, link, core)
 
 
-def far_rows_kernel(far, edge, beyond, full1, link1, core1, full2, link2, core2, field):
-    chans, rows, cols = far.shape
+def far_rows_kernel(
+    far1, far2, edge, beyond, full1, link1, core1, full2, link2, core2, field
+):
+    chans, rows, half = far1.shape
     at, count = lax.axis_index("pix"), lax.axis_size("pix")
     even = odd_of("pix") == 0
     present = jnp.logical_and(at > 0, at < count - 1).astype(jnp.float32)
-    field[:, 8:24, :] = far[...]
+    field[:, 8:24, :half] = far1[...]
+    field[:, 8:24, half:] = far2[...]
     for r in range(3):
         field[:, 5 + r, :] = jnp.where(even, beyond[r], edge[r])
         field[:, 24 + r, :] = jnp.where(even, edge[r], beyond[r])
 
     for c in range(chans):
         value = smooth_rows(field, c, 8, rows) * present
-        store_channel(c, value[:, : cols // 2], full1, link1, core1)
-        store_channel(c, value[:, cols // 2 :], full2, link2, core2)
+        store_channel(c, value[:, :half], full1, link1, core1)
+        store_channel(c, value[:, half:], full2, link2, core2)
 
 
 def channel_pass(own, halo, down, row, tile, energy, before, boxes, kept_at):
@@ -337,21 +341,24 @@
 
     toward = [(i, i + 2 if i % 2 == 0 else i - 2) for i in range(pix)]
     back = [(i, i - 2 if i % 2 == 0 else i + 2) for i in range(pix)]
-    cells, edge, edge2 = call(
-        clean_cols_kernel, [f32(chans, rows, cols), f32(3, chans, cols), f32(3, chans, cols)]
+    half = cols // 2
+    cells, right, edge, edge2 = call(
+        clean_cols_kernel,
+        [f32(chans, rows, cols), f32(chans, rows, half), f32(3, chans, cols), f32(3, chans, cols)],
     )(data_cube, blanked)
     near = swap(cells, "pix", 0)
+    far_right = swap(move(right, "pix", back), "pix", 0)
     edge_near = move(edge, "pix", back)
     edge_far = swap(edge, "pix", 1)
     beyond = move(edge2, "pix", toward)
-    near = call(
-        lambda value, *rest: None,
-        f32(*near.shape),
-        in_specs=[ANY] * 4,
-        out_specs=ANY,
-        input_output_aliases={0: 0},
-    )(near, edge_near, edge_far, beyond)
-    far = move(near, "pix", toward)
+
+    def left_half(value, *rest):
+        rest[-1][...] = value[:, :, : rest[-1].shape[2]]
+
+    near_left = call(left_half, f32(chans, rows, half), in_specs=[VMEM] + [ANY] * 3)(
+        near, edge_near, edge_far, beyond
+    )
+    far_left = move(near_left, "pix", toward)
 
     pair, pair_link, pair_core = call(
         pair_rows_kernel,
@@ -362,13 +369,12 @@
     pair_link = swap(pair_link, "chan", 1)
     pair_core = swap(pair_core, "chan", 0)
 
-    half = cols // 2
     outer, link1, core1, outer2, link2, core2 = call(
         far_rows_kernel,
         [f32(chans, 16, half), f32(HALO, 16, half), f32(HALO, 16, half)] * 2,
         [pltpu.VMEM((chans, 32, cols), jnp.float32)],
         micros=30.0,
-    )(far, edge, beyond)
+    )(far_left, far_right, edge, beyond)
     link1, core1 = swap(link1, "chan", 1), swap(core1, "chan", 0)
     link2, core2 = swap(link2, "chan", 1), swap(core2, "chan", 0)
 

time: 52.2 us -> 51.4 us (0.985)
  waiting for transfers between devices: 15.5 us -> 7.12 us
  starting transfers between devices: 25.3 us -> 33 us
    ppermute x11 -> x13, waiting for transfers between devices: 15.5 us -> 7.12 us  [move(): lax.ppermute(value, axis, [(a, b) for a, b in pairs if 0 <= b < count])]
    ppermute x11 -> x13, starting transfers between devices: 25.3 us -> 33 us  [move(): lax.ppermute(value, axis, [(a, b) for a, b in pairs if 0 <= b < count])]
    unnamed x4 -> x6, local copies, waits for them, and re-layouts: 1.8 us -> 1.8 us
  transfers between devices with their start and end apart: 11 -> 13, of which waited for: 4 -> 4; matrix products, arithmetic and copies ran while one was open for 0% -> 0% of each run, Pallas kernels for 11% -> 11%
where the time goes in v11:
time: 51.4 us; the launch traced here: 51 us
  starting transfers between devices  33 us (64%)
  Pallas kernels  8.81 us (17%)
  waiting for transfers between devices  7.12 us (14%)
  local copies, waits for them, and re-layouts  1.8 us (4%)
    ppermute x13, starting transfers between devices, move(): lax.ppermute(value, axis, [(a, b) for a, b in pairs if 0 <= b < count])  33 us
    ppermute x13, waiting for transfers between devices, move(): lax.ppermute(value, axis, [(a, b) for a, b in pairs if 0 <= b < count])  7.12 us
    pallas_call x1, Pallas kernels, per_device(): call(snr_kernel, f32(4, chans, rows, cols), [scratch, scratch, pltpu.VMEM...  2.25 us
    pallas_call x1, Pallas kernels, per_device(): call(pair_noise_kernel, [f32(4, chans, rows, cols), f32(4, tiles, 2, rows...  1.96 us
    unnamed x6, local copies, waits for them, and re-layouts  1.8 us
  transfers between devices with their start and end apart: 13, of which 4 were waited for; matrix products, arithmetic and copies ran while one was open for 0% of the time, Pallas kernels for 11%

profile of v11, /device:TPU:34, one launch (start us, length us, event | category | flops | bytes accessed | tf_op | source)
XLA Modules:
  0.0 51.0 jit_solution(4636896013560341824)
XLA Ops:
  0.0 0.0 copy-start
  0.0 1.0 %copy-done = f32[16,16,512]{2,1,0:T(8,128)S(1)} copy-done((f32[16,16,512]{2,1,0:T(8,128)S(1)}, f32[16,16,512]{2,1,0:T(8,128)}, u32[]{:S(2)}) %copy-start) | copy-done | bytes 524312
  1.0 0.0 copy-start.1
  1.0 0.8 %copy-done.1 = s32[16,512]{1,0:T(8,128)S(1)} copy-done((s32[16,512]{1,0:T(8,128)S(1)}, s32[16,512]{1,0:T(8,128)}, u32[]{:S(2)}) %copy-start.1) | copy-done | bytes 32792
  1.8 0.9 %shard_map.28 = (f32[16,16,512]{2,1,0:T(8,128)S(1)}, f32[16,16,256]{2,1,0:T(8,128)S(1)}, f32[3,16,512]{2,1,0:T(8,128)S(1)}, f32[3,16,512]{2,1,0:T(8,128)S(1)}) custom-call(f32[16,16,512]{2,1,0:T(8,128)S(1)} %copy-done, s32[16,512]{1,0:T(8,128)S(1)} %copy-done.1), custom_call_target="tpu_custom_call" | custom-call | flops 1000000000 | bytes 3000000 | tf_op jit(solution)/shard_map/pallas_call | solution.py:345
  2.7 3.1 %collective-permute-start = (f32[16,16,512]{2,1,0:T(8,128)S(1)}, f32[16,16,512]{2,1,0:T(8,128)S(1)}, u32[]{:S(2)}, u32[]{:S(2)}) collective-permute-start(f32[16,16,512]{2,1,0:T(8,128)S(1)} %get-tuple-element.23.cells), channel_id=1, source_target_pairs={{0,16},{16,0},{32,48},{48,32},{64,80},{80,64},{96,112},{112,96},{1... | collective-permute-start | bytes 1572872 | tf_op jit(solution)/shard_map/ppermute | solution.py:335
  5.8 2.4 %collective-permute-start.5 = (f32[16,16,256]{2,1,0:T(8,128)S(1)}, f32[16,16,256]{2,1,0:T(8,128)S(1)}, u32[]{:S(2)}, u32[]{:S(2)}) collective-permute-start(f32[16,16,256]{2,1,0:T(8,128)S(1)} %get-tuple-element.26), channel_id=1, source_target_pairs={{16,48},{32,0},{48,80},{64,32},{80,112},{96,64},{17,49},{33,1},{49... | collective-permute-start | bytes 786440 | tf_op jit(solution)/shard_map/ppermute | solution.py:335
  8.2 3.4 %collective-permute-start.3 = (f32[3,16,512]{2,1,0:T(8,128)S(1)}, f32[3,16,512]{2,1,0:T(8,128)S(1)}, u32[]{:S(2)}, u32[]{:S(2)}) collective-permute-start(f32[3,16,512]{2,1,0:T(8,128)S(1)} %get-tuple-element.25), channel_id=1, source_target_pairs={{0,32},{32,64},{48,16},{64,96},{80,48},{112,80},{1,33},{33,65},{49... | collective-permute-start | bytes 294920 | tf_op jit(solution)/shard_map/ppermute | solution.py:335
  11.6 1.9 %collective-permute-start.2 = (f32[3,16,512]{2,1,0:T(8,128)S(1)}, f32[3,16,512]{2,1,0:T(8,128)S(1)}, u32[]{:S(2)}, u32[]{:S(2)}) collective-permute-start(f32[3,16,512]{2,1,0:T(8,128)S(1)} %get-tuple-element.24.edge), channel_id=1, source_target_pairs={{16,32},{32,16},{48,64},{64,48},{80,96},{96,80},{17,33},{33,17},{4... | collective-permute-start | bytes 294920 | tf_op jit(solution)/shard_map/ppermute | solution.py:335
  13.5 1.9 %collective-permute-start.1 = (f32[3,16,512]{2,1,0:T(8,128)S(1)}, f32[3,16,512]{2,1,0:T(8,128)S(1)}, u32[]{:S(2)}, u32[]{:S(2)}) collective-permute-start(f32[3,16,512]{2,1,0:T(8,128)S(1)} %get-tuple-element.24.edge), channel_id=1, source_target_pairs={{16,48},{32,0},{48,80},{64,32},{80,112},{96,64},{17,49},{33,1},{49... | collective-permute-start | bytes 294920 | tf_op jit(solution)/shard_map/ppermute | solution.py:335
  15.5 0.2 collective-permute-done.5
  15.7 4.3 %collective-permute-start.6 = (f32[16,16,256]{2,1,0:T(8,128)S(1)}, f32[16,16,256]{2,1,0:T(8,128)S(1)}, u32[]{:S(2)}, u32[]{:S(2)}) collective-permute-start(f32[16,16,256]{2,1,0:T(8,128)S(1)} %collective-permute-done.5), channel_id=1, source_target_pairs={{0,16},{16,0},{32,48},{48,32},{64,80},{80,64},{96,112},{112,96},{1... | collective-permute-start | bytes 786440 | tf_op jit(solution)/shard_map/ppermute | solution.py:335
  20.0 0.0 collective-permute-done.3.rest_2_.beyond
  20.0 0.6 %collective-permute-done.2.rest_1_.edge_far = f32[3,16,512]{2,1,0:T(8,128)S(1)} collective-permute-done((f32[3,16,512]{2,1,0:T(8,128)S(1)}, f32[3,16,512]{2,1,0:T(8,128)S(1)}, u32[]{:S(2)}, u32[]{:S(2)}) %collective-permute-start.2) | collective-permute-done | bytes 98336 | tf_op jit(solution)/shard_map/ppermute | solution.py:335
  20.6 0.0 collective-permute-done.1.rest_0_.edge_near
  20.6 0.0 collective-permute-done.value.near
  20.7 4.4 %collective-permute-start.4 = (f32[16,16,256]{2,1,0:T(8,128)S(1)}, f32[16,16,256]{2,1,0:T(8,128)S(1)}, u32[]{:S(2)}, u32[]{:S(2)}) collective-permute-start(f32[16,16,256]{2,1,0:T(8,128)S(1)} %shard_map.29), channel_id=1, source_target_pairs={{0,32},{32,64},{48,16},{64,96},{80,48},{112,80},{1,33},{33,65},{49... | collective-permute-start | bytes 786440 | tf_op jit(solution)/shard_map/ppermute | solution.py:335
  25.1 1.0 %shard_map.31 = (f32[16,32,512]{2,1,0:T(8,128)S(1)}, f32[14,32,512]{2,1,0:T(8,128)S(1)}, f32[14,32,512]{2,1,0:T(8,128)S(1)}) custom-call(f32[16,16,512]{2,1,0:T(8,128)S(1)} %get-tuple-element.23.cells, f32[16,16,512]{2,1,0:T(8,128)S(1)} %collective-permute-done.value.near, f32[3,16,512]{2,1,0:T(8,128)S(1)} %collective-permute-done.2.rest_1_.edge_far, ...), custom_call_target="tpu_custom_call" | custom-call | flops 10000000 | bytes 30000 | tf_op jit(solution)/shard_map/pallas_call | solution.py:363
  26.1 1.9 %collective-permute-start.9 = (f32[14,32,512]{2,1,0:T(8,128)S(1)}, f32[14,32,512]{2,1,0:T(8,128)S(1)}, u32[]{:S(2)}, u32[]{:S(2)}) collective-permute-start(f32[14,32,512]{2,1,0:T(8,128)S(1)} %get-tuple-element.31), channel_id=1, source_target_pairs={{1,2},{2,1},{3,4},{4,3},{5,6},{6,5},{7,8},{8,7},{9,10},{10,9},{11,... | collective-permute-start | bytes 2752520 | tf_op jit(solution)/shard_map/ppermute | solution.py:335
  28.1 1.8 %collective-permute-start.10 = (f32[14,32,512]{2,1,0:T(8,128)S(1)}, f32[14,32,512]{2,1,0:T(8,128)S(1)}, u32[]{:S(2)}, u32[]{:S(2)}) collective-permute-start(f32[14,32,512]{2,1,0:T(8,128)S(1)} %get-tuple-element.32), channel_id=1, source_target_pairs={{0,1},{1,0},{2,3},{3,2},{4,5},{5,4},{6,7},{7,6},{8,9},{9,8},{10,11... | collective-permute-start | bytes 2752520 | tf_op jit(solution)/shard_map/ppermute | solution.py:335
  29.8 0.0 collective-permute-done.6.far2
  29.8 0.0 collective-permute-done.4.far1
  29.8 0.7 %shard_map.30 = (f32[16,16,256]{2,1,0:T(8,128)S(1)}, f32[14,16,256]{2,1,0:T(8,128)S(1)}, f32[14,16,256]{2,1,0:T(8,128)S(1)}, f32[16,16,256]{2,1,0:T(8,128)S(1)},...) custom-call(f32[16,16,256]{2,1,0:T(8,128)S(1)} %collective-permute-done.4.far1, ...), custom_call_target="tpu_custom_call" | custom-call | flops 30000001024 | bytes 90000000 | tf_op jit(solution)/shard_map/pallas_call | solution.py:372
  30.5 4.1 %collective-permute-start.7 = (f32[14,16,256]{2,1,0:T(8,128)S(1)}, f32[14,16,256]{2,1,0:T(8,128)S(1)}, u32[]{:S(2)}, u32[]{:S(2)}) collective-permute-start(f32[14,16,256]{2,1,0:T(8,128)S(1)} %get-tuple-element.28), channel_id=1, source_target_pairs={{1,2},{2,1},{3,4},{4,3},{5,6},{6,5},{7,8},{8,7},{9,10},{10,9},{11,... | collective-permute-start | bytes 688136 | tf_op jit(solution)/shard_map/ppermute | solution.py:335
  34.6 0.1 collective-permute-start.8
  34.7 3.6 %collective-permute-start.11 = (f32[14,16,256]{2,1,0:T(8,128)S(1)}, f32[14,16,256]{2,1,0:T(8,128)S(1)}, u32[]{:S(2)}, u32[]{:S(2)}) collective-permute-start(f32[14,16,256]{2,1,0:T(8,128)S(1)} %get-tuple-element.37), channel_id=1, source_target_pairs={{1,2},{2,1},{3,4},{4,3},{5,6},{6,5},{7,8},{8,7},{9,10},{10,9},{11,... | collective-permute-start | bytes 688136 | tf_op jit(solution)/shard_map/ppermute | solution.py:335
  38.3 0.0 collective-permute-done.10.core
  38.3 0.1 collective-permute-start.12
  38.4 0.0 copy-start.2
  38.4 0.9 %shard_map.32 = (f32[4,4,640,128]{3,2,1,0:T(8,128)S(1)}, f32[4,8,16,512]{3,2,1,0:T(8,128)S(1)}) custom-call(f32[16,32,512]{2,1,0:T(8,128)S(1)} %get-tuple-element.30.own, f32[14,32,512]{2,1,0:T(8,128)S(1)} %collective-permute-done.10.core, f32[16,16,256]{2,1,0:T(8,128)S(1)} %get-tuple-element.33.after.own), custom_call_target="tpu_custom_call" | custom-call | flops 2000000000 | bytes 6000000 | tf_op jit(solution)/shard_map/pallas_call | solution.py:381
  39.3 3.6 %collective-permute-done.9.link = f32[14,32,512]{2,1,0:T(8,128)S(1)} collective-permute-done((f32[14,32,512]{2,1,0:T(8,128)S(1)}, f32[14,32,512]{2,1,0:T(8,128)S(1)}, u32[]{:S(2)}, u32[]{:S(2)}) %collective-permute-start.9) | collective-permute-done | bytes 917536 | tf_op jit(solution)/shard_map/ppermute | solution.py:335
  42.9 0.0 copy-done.2
  42.9 2.0 %shard_map.33 = (f32[4,16,16,512]{3,2,1,0:T(8,128)S(1)}, f32[4,4,2,16,8,128]{5,4,3,2,1,0:T(8,128)S(1)}, bf16[2,384,256]{2,1,0:T(8,128)(2,1)S(1)}) custom-call(f32[16,32,512]{2,1,0:T(8,128)S(1)} %get-tuple-element.30.own, f32[14,32,512]{2,1,0:T(8,128)S(1)} %collective-permute-done.9.link, f32[4,4,640,128]{3,2,1,0:T(8,128)S(1)} %get-tuple-element.34.before, ...), custom_call_target="tpu_custom_call" | custom-call | flops 3000000000 | bytes 9000000 | tf_op jit(solution)/shard_map/pallas_call | solution.py:387
  44.9 0.0 collective-permute-done.12.core
  44.9 0.3 shard_map.35.before
  45.2 2.7 %collective-permute-done.11.link = f32[14,16,256]{2,1,0:T(8,128)S(1)} collective-permute-done((f32[14,16,256]{2,1,0:T(8,128)S(1)}, f32[14,16,256]{2,1,0:T(8,128)S(1)}, u32[]{:S(2)}, u32[]{:S(2)}) %collective-permute-start.11) | collective-permute-done | bytes 229408 | tf_op jit(solution)/shard_map/ppermute | solution.py:335
  47.9 0.6 %shard_map.36.first = f32[4,2,384,128]{3,2,1,0:T(8,128)S(1)} custom-call(f32[16,16,256]{2,1,0:T(8,128)S(1)} %get-tuple-element.33.after.own, f32[14,16,256]{2,1,0:T(8,128)S(1)} %collective-permute-done.11.link, f32[4,2,384,128]{3,2,1,0:T(8,128)S(1)} %shard_map.35.before, f32[4,4,2,16,8,128]{5,4,3,2,1,0:T(8,128)S(1)} %get-tuple-element.36.after.part), custom_call_target="tpu_custom_call" | custom-call | flops 1000000000 | bytes 3000000 | tf_op jit(solution)/shard_map/pallas_call | solution.py:406
  48.4 0.0 collective-permute-done.8.core
  48.4 0.3 shard_map.34.before
  48.7 0.0 collective-permute-done.7.link
  48.7 2.2 %shard_map.37 = f32[4,16,16,512]{3,2,1,0:T(8,128)} custom-call(f32[16,16,256]{2,1,0:T(8,128)S(1)} %get-tuple-element.27.own, f32[14,16,256]{2,1,0:T(8,128)S(1)} %collective-permute-done.7.link, f32[4,2,384,128]{3,2,1,0:T(8,128)S(1)} %shard_map.34.before, f32[4,4,2,16,8,128]{5,4,3,2,1,0:T(8,128)S(1)} %get-tuple-element.36.after.part, ...), custom_call_target="tpu_custom_call" | custom-call | flops 4000000000 | bytes 12000000 | tf_op jit(solution)/shard_map/pallas_call | solution.py:407
  (1 shorter events, 0.0 us)
Async XLA Ops:
  0.0 1.0 %copy-start = (f32[16,16,512]{2,1,0:T(8,128)S(1)}, f32[16,16,512]{2,1,0:T(8,128)}, u32[]{:S(2)}) copy-start(f32[16,16,512]{2,1,0:T(8,128)} %data.1) | copy-start | bytes 1572868
  1.0 0.8 %copy-start.1 = (s32[16,512]{1,0:T(8,128)S(1)}, s32[16,512]{1,0:T(8,128)}, u32[]{:S(2)}) copy-start(s32[16,512]{1,0:T(8,128)} %blanked.3) | copy-start | bytes 98308
  2.7 17.9 %collective-permute-start = (f32[16,16,512]{2,1,0:T(8,128)S(1)}, f32[16,16,512]{2,1,0:T(8,128)S(1)}, u32[]{:S(2)}, u32[]{:S(2)}) collective-permute-start(f32[16,16,512]{2,1,0:T(8,128)S(1)} %get-tuple-element.23.cells), channel_id=1, source_target_pairs={{0,16},{16,0},{32,48},{48,32},{64,80},{80,64},{96,112},{112,96},{1... | collective-permute-start | bytes 1572872 | tf_op jit(solution)/shard_map/ppermute | solution.py:335
  5.8 9.9 %collective-permute-start.5 = (f32[16,16,256]{2,1,0:T(8,128)S(1)}, f32[16,16,256]{2,1,0:T(8,128)S(1)}, u32[]{:S(2)}, u32[]{:S(2)}) collective-permute-start(f32[16,16,256]{2,1,0:T(8,128)S(1)} %get-tuple-element.26), channel_id=1, source_target_pairs={{16,48},{32,0},{48,80},{64,32},{80,112},{96,64},{17,49},{33,1},{49... | collective-permute-start | bytes 786440 | tf_op jit(solution)/shard_map/ppermute | solution.py:335
  8.2 11.8 %collective-permute-start.3 = (f32[3,16,512]{2,1,0:T(8,128)S(1)}, f32[3,16,512]{2,1,0:T(8,128)S(1)}, u32[]{:S(2)}, u32[]{:S(2)}) collective-permute-start(f32[3,16,512]{2,1,0:T(8,128)S(1)} %get-tuple-element.25), channel_id=1, source_target_pairs={{0,32},{32,64},{48,16},{64,96},{80,48},{112,80},{1,33},{33,65},{49... | collective-permute-start | bytes 294920 | tf_op jit(solution)/shard_map/ppermute | solution.py:335
  11.6 9.0 %collective-permute-start.2 = (f32[3,16,512]{2,1,0:T(8,128)S(1)}, f32[3,16,512]{2,1,0:T(8,128)S(1)}, u32[]{:S(2)}, u32[]{:S(2)}) collective-permute-start(f32[3,16,512]{2,1,0:T(8,128)S(1)} %get-tuple-element.24.edge), channel_id=1, source_target_pairs={{16,32},{32,16},{48,64},{64,48},{80,96},{96,80},{17,33},{33,17},{4... | collective-permute-start | bytes 294920 | tf_op jit(solution)/shard_map/ppermute | solution.py:335
  13.5 7.1 %collective-permute-start.1 = (f32[3,16,512]{2,1,0:T(8,128)S(1)}, f32[3,16,512]{2,1,0:T(8,128)S(1)}, u32[]{:S(2)}, u32[]{:S(2)}) collective-permute-start(f32[3,16,512]{2,1,0:T(8,128)S(1)} %get-tuple-element.24.edge), channel_id=1, source_target_pairs={{16,48},{32,0},{48,80},{64,32},{80,112},{96,64},{17,49},{33,1},{49... | collective-permute-start | bytes 294920 | tf_op jit(solution)/shard_map/ppermute | solution.py:335
  15.7 14.1 %collective-permute-start.6 = (f32[16,16,256]{2,1,0:T(8,128)S(1)}, f32[16,16,256]{2,1,0:T(8,128)S(1)}, u32[]{:S(2)}, u32[]{:S(2)}) collective-permute-start(f32[16,16,256]{2,1,0:T(8,128)S(1)} %collective-permute-done.5), channel_id=1, source_target_pairs={{0,16},{16,0},{32,48},{48,32},{64,80},{80,64},{96,112},{112,96},{1... | collective-permute-start | bytes 786440 | tf_op jit(solution)/shard_map/ppermute | solution.py:335
  20.7 9.2 %collective-permute-start.4 = (f32[16,16,256]{2,1,0:T(8,128)S(1)}, f32[16,16,256]{2,1,0:T(8,128)S(1)}, u32[]{:S(2)}, u32[]{:S(2)}) collective-permute-start(f32[16,16,256]{2,1,0:T(8,128)S(1)} %shard_map.29), channel_id=1, source_target_pairs={{0,32},{32,64},{48,16},{64,96},{80,48},{112,80},{1,33},{33,65},{49... | collective-permute-start | bytes 786440 | tf_op jit(solution)/shard_map/ppermute | solution.py:335
  26.1 16.8 %collective-permute-start.9 = (f32[14,32,512]{2,1,0:T(8,128)S(1)}, f32[14,32,512]{2,1,0:T(8,128)S(1)}, u32[]{:S(2)}, u32[]{:S(2)}) collective-permute-start(f32[14,32,512]{2,1,0:T(8,128)S(1)} %get-tuple-element.31), channel_id=1, source_target_pairs={{1,2},{2,1},{3,4},{4,3},{5,6},{6,5},{7,8},{8,7},{9,10},{10,9},{11,... | collective-permute-start | bytes 2752520 | tf_op jit(solution)/shard_map/ppermute | solution.py:335
  28.1 10.2 %collective-permute-start.10 = (f32[14,32,512]{2,1,0:T(8,128)S(1)}, f32[14,32,512]{2,1,0:T(8,128)S(1)}, u32[]{:S(2)}, u32[]{:S(2)}) collective-permute-start(f32[14,32,512]{2,1,0:T(8,128)S(1)} %get-tuple-element.32), channel_id=1, source_target_pairs={{0,1},{1,0},{2,3},{3,2},{4,5},{5,4},{6,7},{7,6},{8,9},{9,8},{10,11... | collective-permute-start | bytes 2752520 | tf_op jit(solution)/shard_map/ppermute | solution.py:335
  30.5 18.2 %collective-permute-start.7 = (f32[14,16,256]{2,1,0:T(8,128)S(1)}, f32[14,16,256]{2,1,0:T(8,128)S(1)}, u32[]{:S(2)}, u32[]{:S(2)}) collective-permute-start(f32[14,16,256]{2,1,0:T(8,128)S(1)} %get-tuple-element.28), channel_id=1, source_target_pairs={{1,2},{2,1},{3,4},{4,3},{5,6},{6,5},{7,8},{8,7},{9,10},{10,9},{11,... | collective-permute-start | bytes 688136 | tf_op jit(solution)/shard_map/ppermute | solution.py:335
  34.6 13.8 %collective-permute-start.8 = (f32[14,16,256]{2,1,0:T(8,128)S(1)}, f32[14,16,256]{2,1,0:T(8,128)S(1)}, u32[]{:S(2)}, u32[]{:S(2)}) collective-permute-start(f32[14,16,256]{2,1,0:T(8,128)S(1)} %get-tuple-element.29), channel_id=1, source_target_pairs={{0,1},{1,0},{2,3},{3,2},{4,5},{5,4},{6,7},{7,6},{8,9},{9,8},{10,11... | collective-permute-start | bytes 688136 | tf_op jit(solution)/shard_map/ppermute | solution.py:335
  34.7 13.2 %collective-permute-start.11 = (f32[14,16,256]{2,1,0:T(8,128)S(1)}, f32[14,16,256]{2,1,0:T(8,128)S(1)}, u32[]{:S(2)}, u32[]{:S(2)}) collective-permute-start(f32[14,16,256]{2,1,0:T(8,128)S(1)} %get-tuple-element.37), channel_id=1, source_target_pairs={{1,2},{2,1},{3,4},{4,3},{5,6},{6,5},{7,8},{8,7},{9,10},{10,9},{11,... | collective-permute-start | bytes 688136 | tf_op jit(solution)/shard_map/ppermute | solution.py:335
  38.3 6.6 %collective-permute-start.12 = (f32[14,16,256]{2,1,0:T(8,128)S(1)}, f32[14,16,256]{2,1,0:T(8,128)S(1)}, u32[]{:S(2)}, u32[]{:S(2)}) collective-permute-start(f32[14,16,256]{2,1,0:T(8,128)S(1)} %get-tuple-element.38), channel_id=1, source_target_pairs={{0,1},{1,0},{2,3},{3,2},{4,5},{5,4},{6,7},{7,6},{8,9},{9,8},{10,11... | collective-permute-start | bytes 688136 | tf_op jit(solution)/shard_map/ppermute | solution.py:335
  38.4 4.6 %copy-start.2 = (s32[16,512]{1,0:T(8,128)S(1)}, s32[16,512]{1,0:T(8,128)}, u32[]{:S(2)}) copy-start(s32[16,512]{1,0:T(8,128)} %blanked.3) | copy-start | bytes 98308
